TPU v7x, 32 devices: a whole 2x2x4 slice. The times are simulated.
32 devices in a mesh: ao: 4 (over z), vir: 4 (over y, core), occ: 2 (over x).
Axes of the slice: x: 2, y: 2, z: 4, core: 2. Of those that a mesh axis runs over, the one named last changes fastest.
Arguments:
- pair_list: int32 [10, 2], P('occ'), may hold values from 0 to 3, as said below
- half_ints: bfloat16 [2560, 4, 6144], P('ao', 'occ', 'vir'), may hold values from -6 to 6
- vir_coef: bfloat16 [2560, 2048], P('ao'), may hold values from -0.125 to 0.125
- metric: bfloat16 [6144, 6144], P('vir'), may hold values from -2 to 2, as said below
- occ_energy: float32 [4], replicated, may hold values from -2 to -0.3
- vir_energy: float32 [2048], replicated, may hold values from 0.2 to 3
Outputs:
- density: float32 [2048, 4, 6144], P('vir', 'occ', 'ao')
Inputs may be any that keep to these rules, and one draw needn't show every extreme that they name: `pair_list`: each unordered pair of the window's orbitals (an orbital with itself included) appears once, in an order and an orientation (i, j) or (j, i) drawn from the seed. `metric`: symmetric.
All inputs are finite; a program needn't handle non-finite values.
Results may differ from a plain program's by a relative error of at most 0.006.
Values may be sent and summed in bfloat16 or wider, within the bound.
No kernel may reach another device: no remote copies, remote signals or barrier semaphores. Data moves between devices by JAX's collectives and lax.ppermute only.
A program may use at most 192 MiB of HBM per device.

v0:
```python
import jax
import jax.numpy as jnp
from jax import lax
from jax.sharding import PartitionSpec as P


def local(pair_list, half_ints, vir_coef, metric, occ_energy, vir_energy):
    n_atomic = lax.axis_size("ao")
    n_virtual = lax.axis_size("vir")
    mu_rows, occ_rows, aux_rows = half_ints.shape
    n_virt = vir_coef.shape[1]
    width = n_virt // (n_virtual * n_atomic)
    ordered = (
        vir_coef.reshape(mu_rows, n_virtual, n_atomic, width)
        .transpose(0, 2, 1, 3)
        .reshape(mu_rows, n_virt)
    )
    flat_half = half_ints.reshape(mu_rows, occ_rows * aux_rows)
    vir_rows = n_virt // n_atomic
    columns = ordered
    summed = lax.psum_scatter(
        lax.dot_general(
            columns, flat_half, (((0,), (0,)), ((), ())), preferred_element_type=jnp.float32
        ),
        "ao",
        scatter_dimension=0,
        tiled=True,
    )
    transformed = summed.astype(jnp.bfloat16).reshape(vir_rows * occ_rows, aux_rows)
    columns = metric
    fitted = lax.dot_general(
        lax.all_gather(transformed, "vir", axis=1, tiled=True),
        columns,
        (((1,), (1,)), ((), ())),
        preferred_element_type=jnp.float32,
    )
    fitted = fitted.astype(jnp.bfloat16).reshape(vir_rows, occ_rows, aux_rows)
    local_blocks = lax.all_to_all(
        lax.all_to_all(fitted, "vir", split_axis=0, concat_axis=2, tiled=True),
        "ao",
        split_axis=2,
        concat_axis=0,
        tiled=True,
    )
    blocks = lax.all_gather(local_blocks, "occ", axis=1, tiled=True)
    a_rows, n_orbitals, q_cols = blocks.shape
    levels = jnp.arange(n_orbitals, dtype=jnp.int32)
    first = (pair_list[:, 0:1] == levels[None, :]).astype(jnp.float32)
    second = (pair_list[:, 1:2] == levels[None, :]).astype(jnp.float32)
    first_low = first.astype(jnp.bfloat16)
    second_low = second.astype(jnp.bfloat16)
    left = jnp.einsum("po,aok->pak", first_low, blocks, preferred_element_type=jnp.float32).astype(
        jnp.bfloat16
    )
    occ_sum = jnp.dot(first + second, occ_energy, precision=lax.Precision.HIGHEST)
    own_energy = lax.dynamic_slice_in_dim(vir_energy, lax.axis_index("vir") * a_rows, a_rows)

    def select_second(piece):
        return jnp.einsum(
            "po,bok->pbk", second_low, piece, preferred_element_type=jnp.float32
        ).astype(jnp.bfloat16)

    part = jnp.einsum(
        "pak,pbk->pab",
        left,
        select_second(lax.all_gather(blocks, "vir", axis=0, tiled=True)),
        preferred_element_type=jnp.float32,
    )
    coulomb = lax.psum(part.astype(jnp.bfloat16), "ao").astype(jnp.float32)
    denom = own_energy[None, :, None] + vir_energy[None, None, :] - occ_sum[:, None, None]
    amplitude = (-coulomb / denom).astype(jnp.bfloat16)
    density_pairs = jnp.einsum(
        "pab,pbk->pak",
        amplitude,
        select_second(lax.all_gather(blocks, "vir", axis=0, tiled=True)),
        preferred_element_type=jnp.float32,
    )
    orbital_density = jnp.einsum(
        "po,pak->aok", first, density_pairs, precision=lax.Precision.HIGHEST
    )
    return lax.psum_scatter(orbital_density, "occ", scatter_dimension=1, tiled=True)


def solution(mesh):
    return jax.shard_map(
        local,
        mesh=mesh,
        in_specs=(P("occ", None), P("ao", "occ", "vir"), P("ao", None), P("vir", None), P(), P()),
        out_specs=P("vir", "occ", "ao"),
        check_vma=False,
    )
```

profile of v0, /device:TPU:0, one launch (start us, length us, event | category | flops | bytes accessed | tf_op | source)
XLA Modules:
  0.0 1671.3 jit_solution(15622341416261825540)
XLA Ops:
  6.5 0.0 copy-start
  6.5 0.0 reduce-scatter.3.cloned.1.call-start
  6.5 3.1 copy.46
  9.7 0.3 copy.47
  10.0 3.1 copy.60
  13.0 13.2 fusion.29
  26.2 0.0 reduce-scatter.3.cloned.1.call-update
  26.3 0.0 all-gather.4.cloned.1.call-start
  26.3 417.2 %reduce-scatter.3.cloned.1.call-done = f32[512,3072]{1,0:T(8,128)} async-done(((f32[2048,3072]{1,0:T(8,128)}), f32[512,3072]{1,0:T(8,128)}) %reduce-scatter.3.cloned.1.call-update) | async-done | bytes 6291472 | tf_op jit(solution)/shard_map/reduce_scatter | solution.py:21
  443.5 3.2 convert_element_type.36
  446.8 2.6 reshape.51
  449.3 0.0 all-gather.4.cloned.1.call-update
  449.4 0.0 all-gather.6.cloned.1.call-start
  449.4 84.0 %all-gather.4.cloned.1.call-done = bf16[1024,6144]{1,0:T(8,128)(2,1)} async-done(((bf16[1024,1536]{1,0:T(8,128)(2,1)}), bf16[1024,6144]{1,0:T(8,128)(2,1)}) %all-gather.4.cloned.1.call-update) | async-done | bytes 12582928 | tf_op jit(solution)/shard_map/all_gather | solution.py:32
  533.4 27.4 %convolution_convert_fusion.1 = bf16[1024,1536]{1,0:T(8,128)(2,1)} fusion(bf16[1024,6144]{1,0:T(8,128)(2,1)} %all-gather.4.cloned.1.call-done, bf16[1536,6144]{1,0:T(8,128)(2,1)} %param.9), kind=kOutput, calls=%fused_computation.12 | convolution fusion | flops 19328925696 | bytes 34603008 | tf_op jit(solution)/shard_map/dot_general | solution.py:31
  560.9 6.0 reshape.52
  566.9 39.7 %all_to_all.36 = bf16[512,2,1536]{2,1,0:T(2,128)(2,1)S(1)} all-to-all(bf16[512,2,1536]{2,1,0:T(2,128)(2,1)S(1)} %reshape.52), channel_id=1, replica_groups=mesh['ao'=4,'vir'=4,'occ'=2] {'vir'}, dimensions={0} | all-to-all | bytes 6291456 | tf_op jit(solution)/shard_map/all_to_all | solution.py:39
  606.6 0.5 copy.48
  607.0 2.8 copy.49
  609.8 6.8 copy.50
  616.6 74.7 %all_to_all.37 = bf16[128,2,6144]{0,1,2:T(2,128)(2,1)S(1)} all-to-all(bf16[128,2,6144]{0,1,2:T(2,128)(2,1)S(1)} %copy.50), channel_id=1, replica_groups=mesh['ao'=4,'vir'=4,'occ'=2] {'ao'}, dimensions={2} | all-to-all | bytes 6291456 | tf_op jit(solution)/shard_map/all_to_all | solution.py:38
  691.3 0.4 copy.51
  691.7 2.8 copy.52
  694.5 0.0 copy-start.5
  694.5 0.0 all-gather.6.cloned.1.call-update
  694.5 0.0 all-gather.8.cloned.1.call-start
  694.6 79.1 %all-gather.6.cloned.1.call-done = bf16[512,4,1536]{2,0,1:T(8,128)(2,1)} async-done(((bf16[512,2,1536]{2,0,1:T(8,128)(2,1)}), bf16[512,4,1536]{2,0,1:T(8,128)(2,1)}) %all-gather.6.cloned.1.call-update) | async-done | bytes 6291472 | tf_op jit(solution)/shard_map/all_gather | solution.py:45
  773.6 10.3 copy.53
  784.0 0.0 all-gather.8.cloned.1.call-update
  784.0 0.0 all-reduce.2.cloned.1.call-start
  784.0 0.0 copy-done.5
  784.1 0.0 copy-start.3
  784.1 11.8 convolution_convert_fusion
  795.9 143.1 %all-gather.8.cloned.1.call-done = bf16[2048,4,1536]{2,1,0:T(4,128)(2,1)} async-done(((bf16[512,4,1536]{2,1,0:T(4,128)(2,1)}), bf16[2048,4,1536]{2,1,0:T(4,128)(2,1)}) %all-gather.8.cloned.1.call-update) | async-done | bytes 25165840 | tf_op jit(solution)/shard_map/all_gather | solution.py:66
  939.0 29.7 %fusion.18 = bf16[5,2048,1536]{2,0,1:T(8,128)(2,1)} fusion(bf16[2048,4,1536]{2,1,0:T(4,128)(2,1)} %all-gather.8.cloned.1.call-done, s32[5]{0:T(128)S(1)} %get-tuple-element.6), kind=kOutput, calls=%fused_computation.23 | convolution fusion | flops 125829184 | bytes 56623124 | tf_op jit(solution)/shard_map/po,bok->pbk/dot_general | solution.py:59
  968.7 91.9 %fusion.10 = bf16[5,512,2048]{2,1,0:T(8,128)(2,1)} fusion(bf16[5,512,1536]{2,0,1:T(8,128)(2,1)} %convolution_convert_fusion, bf16[5,2048,1536]{2,0,1:T(8,128)(2,1)} %fusion.18), kind=kOutput, calls=%fused_computation.11 | convolution fusion | flops 16111370240 | bytes 49807360 | tf_op jit(solution)/shard_map/pak,pbk->pab/dot_general | solution.py:63
  1060.6 0.0 copy-start.2
  1060.6 0.0 all-reduce.2.cloned.1.call-update
  1060.6 0.0 reduce-scatter.5.cloned.1.call-start
  1060.7 0.6 copy-done.2
  1061.3 0.1 dynamic_slice.3
  1061.3 0.0 copy-done.3
  1061.3 0.0 copy-done
  1061.3 0.1 convolution_bitcast_fusion
  1061.5 2.4 broadcast_add_fusion
  1063.8 355.4 %all-reduce.2.cloned.1.call-done = bf16[5,512,2048]{2,1,0:T(8,128)(2,1)} async-done(((bf16[5,512,2048]{2,1,0:T(8,128)(2,1)}), bf16[5,512,2048]{2,1,0:T(8,128)(2,1)}) %all-reduce.2.cloned.1.call-update) | async-done | bytes 10485776 | tf_op jit(solution)/shard_map/psum | solution.py:69
  1419.2 0.0 copy-start.4
  1419.2 49.7 %fusion.5 = f32[5,512,1536]{2,1,0:T(8,128)} fusion(bf16[5,512,2048]{2,1,0:T(8,128)(2,1)} %all-reduce.2.cloned.1.call-done, f32[5]{0:T(128)S(1)} %convolution_bitcast_fusion, f32[512,2048]{1,0:T(8,128)} %broadcast_add_fusion, bf16[5,2048,1536]{2,0,1:T(8,128)(2,1)} %fusion.18), kind=kOutput, calls=%fused_computation.6 | convolution fusion | flops 16132341760 | bytes 61866004 | tf_op jit(solution)/shard_map/pab,pbk->pak/dot_general | solution.py:72
  1468.9 0.0 copy-done.4
  1468.9 28.1 %fusion.2 = f32[512,4,1536]{2,1,0:T(4,128)} fusion(f32[5,512,1536]{2,1,0:T(8,128)} %fusion.5, s32[5]{0:T(128)S(1)} %copy-done.4), kind=kOutput, calls=%fused_computation.5 | convolution fusion | flops 188743696 | bytes 28311572 | tf_op jit(solution)/shard_map/po,pak->aok/dot_general | solution.py:78
  1497.0 13.1 copy.58
  1510.1 0.0 copy-start.1
  1510.1 0.0 reduce-scatter.5.cloned.1.call-update
  1510.1 143.6 %reduce-scatter.5.cloned.1.call-done = f32[512,2,1536]{2,0,1:T(8,128)} async-done(((f32[512,4,1536]{2,0,1:T(8,128)}), f32[512,2,1536]{2,0,1:T(8,128)}) %reduce-scatter.5.cloned.1.call-update) | async-done | bytes 6291472 | tf_op jit(solution)/shard_map/reduce_scatter | solution.py:81
  1653.7 10.3 copy.59
  1664.1 0.0 copy-done.1
  (1 shorter events, 0.0 us)
Async XLA Ops:
  6.5 1054.8 %copy-start = (f32[4]{0:T(128)S(1)}, f32[4]{0:T(128)}, u32[]{:S(2)}) copy-start(f32[4]{0:T(128)} %param.10) | copy-start | bytes 52
  6.5 437.0 %reduce-scatter.3.cloned.1.call-start = ((), (), s32[]{:S(2)}) async-start(), calls=%async_computation.4 | async-start | bytes 31457280 | tf_op jit(solution)/shard_map/reduce_scatter | solution.py:21
  26.3 507.2 %all-gather.4.cloned.1.call-start = ((), (), s32[]{:S(2)}) async-start(), calls=%async_computation.5 | async-start | bytes 15728640 | tf_op jit(solution)/shard_map/all_gather | solution.py:32
  449.4 324.3 %all-gather.6.cloned.1.call-start = ((), (), s32[]{:S(2)}) async-start(), calls=%async_computation.6 | async-start | bytes 9437184 | tf_op jit(solution)/shard_map/all_gather | solution.py:45
  694.5 89.6 %copy-start.5 = (s32[5,2]{0,1:T(2,128)S(1)}, s32[5,2]{0,1:T(2,128)}, u32[]{:S(2)}) copy-start(s32[5,2]{0,1:T(2,128)} %param.6) | copy-start | bytes 124
  694.5 244.5 %all-gather.8.cloned.1.call-start = ((), (), s32[]{:S(2)}) async-start(), calls=%async_computation.7 | async-start | bytes 31457280 | tf_op jit(solution)/shard_map/all_gather | solution.py:66
  784.0 635.2 %all-reduce.2.cloned.1.call-start = ((), (), s32[]{:S(2)}) async-start(), calls=%async_computation.8 | async-start | bytes 20971520 | tf_op jit(solution)/shard_map/psum | solution.py:69
  784.1 277.3 %copy-start.3 = (s32[5]{0:T(128)}, s32[5]{0:T(128)S(1)}, u32[]{:S(2)}) copy-start(s32[5]{0:T(128)S(1)} %get-tuple-element.5) | copy-start | bytes 64
  1060.6 0.7 copy-start.2
  1060.6 593.1 %reduce-scatter.5.cloned.1.call-start = ((), (), s32[]{:S(2)}) async-start(), calls=%async_computation.9 | async-start | bytes 18874368 | tf_op jit(solution)/shard_map/reduce_scatter | solution.py:81
  1419.2 49.7 %copy-start.4 = (s32[5]{0:T(128)S(1)}, s32[5]{0:T(128)}, u32[]{:S(2)}) copy-start(s32[5]{0:T(128)} %copy-done.3) | copy-start | bytes 64
  1510.1 153.9 %copy-start.1 = (f32[4]{0:T(128)S(1)}, f32[4]{0:T(128)}, u32[]{:S(2)}) copy-start(f32[4]{0:T(128)} %param.10) | copy-start | bytes 52
Sparse Core Ops, SparseCore 0:
  26.4 417.0 reduce-scatter.2
  449.5 83.8 all-gather.3
  694.6 78.9 all-gather.5
  784.1 154.8 all-gather.7
  1060.7 358.4 all-reduce.1
  1510.3 143.4 reduce-scatter.4
where the time goes:
time: 1680 us; the launch traced here: 1670 us
  waiting for transfers between devices  1220 us (73%)
  matrix products  252 us (15%)
  blocking collectives  114 us (7%)
  local copies, waits for them, and re-layouts  62.8 us (4%)
    reduce_scatter x1, waiting for transfers between devices, local(): lax.psum_scatter(lax.dot_general(columns, flat_half, (((0,), (0,)), ((),...  417 us
    psum x1, waiting for transfers between devices, local(): coulomb = lax.psum(part.astype(jnp.bfloat16), 'ao').astype(jnp.float32)  355 us
    reduce_scatter x1, waiting for transfers between devices, local(): lax.psum_scatter(orbital_density, 'occ', scatter_dimension=1, tiled=True)  144 us
    all_gather x1, waiting for transfers between devices, local(): lax.all_gather(blocks, 'vir', axis=0, tiled=True)  143 us
    dot_general x1, matrix products, local(): jnp.einsum('pak,pbk->pab', left, select_second(lax.all_gather(blocks, 'vi...  91.9 us
    all_gather x1, waiting for transfers between devices, local(): lax.all_gather(transformed, 'vir', axis=1, tiled=True)  84 us
    all_gather x1, waiting for transfers between devices, local(): blocks = lax.all_gather(local_blocks, 'occ', axis=1, tiled=True)  79.1 us
    all_to_all x1, blocking collectives, local(): lax.all_to_all(lax.all_to_all(fitted, 'vir', split_axis=0, concat_axis=2,...  74.7 us
  transfers between devices with their start and end apart: 6, of which 6 were waited for; matrix products, arithmetic and copies ran while one was open for 1% of the time, Pallas kernels for 0%

commit v1 on v0

v1 whole, which is shorter than its diff:
```python
import functools

import jax
import jax.numpy as jnp
from jax import lax
from jax.experimental import pallas as pl
from jax.experimental.pallas import tpu as pltpu
from jax.sharding import Mesh, PartitionSpec as P

BF = jnp.bfloat16
F32 = jnp.float32
VMEM = 56 * 1024 * 1024
NT = (((1,), (1,)), ((), ()))


def swap(value, axis):
    return lax.ppermute(value, axis, [(0, 1), (1, 0)])


def tile_of(width):
    return 256 if width % 256 == 0 else width


def cost(flops, nbytes):
    return pl.CostEstimate(flops=int(flops), bytes_accessed=int(nbytes), transcendentals=0)


def call(kernel, prefetch, operands, grid, in_specs, out_specs, out_shape, scratch, estimate, name):
    return pl.pallas_call(
        kernel,
        grid_spec=pltpu.PrefetchScalarGridSpec(
            num_scalar_prefetch=1,
            grid=grid,
            in_specs=in_specs,
            out_specs=out_specs,
            scratch_shapes=scratch,
        ),
        out_shape=out_shape,
        compiler_params=pltpu.CompilerParams(vmem_limit_bytes=VMEM),
        cost_estimate=estimate,
        name=name,
    )(prefetch, *operands)


def fit(pieces, owners, metric, half):
    rows, depth = pieces[0].shape
    block, total = metric.shape
    width = block // 2
    tile = tile_of(width)
    steps = width // tile
    count = len(pieces)

    def kernel(index, *refs):
        held, metric_ref, out = refs[:count], refs[count], refs[count + 1]
        acc = None
        for at in range(count):
            columns = pl.ds(pl.multiple_of(index[1 + at] * depth, 128), depth)
            term = lax.dot_general(
                held[at][...], metric_ref[:, columns], NT, preferred_element_type=F32
            )
            acc = term if acc is None else acc + term
        out[...] = acc.astype(BF)

    return call(
        kernel,
        jnp.concatenate([jnp.reshape(half, (1,)), owners]).astype(jnp.int32),
        (*pieces, metric),
        (steps,),
        [pl.BlockSpec((rows, depth), lambda t, index: (0, 0))] * count
        + [pl.BlockSpec((tile, total), lambda t, index: (index[0] * steps + t, 0))],
        pl.BlockSpec((rows, tile), lambda t, index: (0, t)),
        jax.ShapeDtypeStruct((rows, width), BF),
        [],
        cost(2 * rows * total * width, 2 * (rows * total + width * total + rows * width)),
        "fit",
    )


def coulomb(own, sib, pairs, flips, blocks, a_block, rows, segments):
    orbitals = sorted(own)
    n_virt, width = own[orbitals[0]].shape
    count = blocks.shape[0]
    bw = n_virt // count
    n_orb, n_pairs = len(orbitals), len(pairs)
    half = rows // 2
    n_seg = len(segments)
    mixed = [pair for pair in pairs if pair[0] != pair[1]]

    def kernel(index, *refs):
        left = [refs[at * n_orb : (at + 1) * n_orb] for at in range(2)]
        right = [refs[(2 + at) * n_orb : (3 + at) * n_orb] for at in range(2)]
        outs = refs[4 * n_orb : 4 * n_orb + 2 * n_seg]
        acc = refs[4 * n_orb + 2 * n_seg]
        step = pl.program_id(0)

        def product(first, second):
            total = None
            for side in range(2):
                term = lax.dot_general(
                    left[side][orbitals.index(first)][...],
                    right[side][orbitals.index(second)][...],
                    NT,
                    preferred_element_type=F32,
                )
                total = term if total is None else total + term
            return total.astype(BF)

        for at, (i, j) in enumerate(pairs):
            if i == j:
                acc[at] = product(i, j)
            else:
                flip = index[1 + count + mixed.index((i, j))]

                @pl.when(flip == 0)
                def _(at=at, i=i, j=j):
                    acc[at] = product(i, j)

                @pl.when(flip != 0)
                def _(at=at, i=i, j=j):
                    acc[at] = product(j, i)

        start = 0
        for seg, length in enumerate(segments):

            @pl.when((step >= start) & (step < start + length))
            def _(seg=seg):
                for part in range(2):
                    outs[part * n_seg + seg][0] = acc[:, part * half : (part + 1) * half, :]

            start += length

    starts = [sum(segments[:at]) for at in range(n_seg)]
    out_specs = [
        pl.BlockSpec(
            (1, n_pairs, half, bw),
            lambda t, index, start=start, length=length: (
                jnp.clip(t - start, 0, length - 1),
                0,
                0,
                0,
            ),
        )
        for _ in range(2)
        for start, length in zip(starts, segments)
    ]
    out_shape = [
        jax.ShapeDtypeStruct((length, n_pairs, half, bw), BF)
        for _ in range(2)
        for length in segments
    ]
    arrays = [own[o] for o in orbitals] + [sib[o] for o in orbitals]
    index = jnp.concatenate(
        [jnp.reshape(a_block, (1,)), blocks]
        + [jnp.reshape(flips[pair], (1,)) for pair in mixed]
    ).astype(jnp.int32)
    outs = call(
        kernel,
        index,
        (*arrays, *arrays),
        (count,),
        [pl.BlockSpec((rows, width), lambda t, index: (index[0], 0))] * (2 * n_orb)
        + [pl.BlockSpec((bw, width), lambda t, index: (index[1 + t], 0))] * (2 * n_orb),
        out_specs,
        out_shape,
        [pltpu.VMEM((n_pairs, rows, bw), BF)],
        cost(
            4 * n_pairs * rows * n_virt * width,
            4 * n_orb * n_virt * width + 2 * n_pairs * rows * n_virt,
        ),
        "coulomb",
    )
    return [list(outs[part * n_seg : (part + 1) * n_seg]) for part in range(2)]


def contract(groups, own, sib, flips, blocks, core, n_v):
    n_orb = len(own)
    n_virt, width = own[0].shape
    count = blocks.shape[0]
    bw = n_virt // count
    tile = tile_of(width)
    steps = width // tile
    pairs = [pair for group, _ in groups for pair in group]
    mixed = [pair for pair in pairs if pair[0] != pair[1]]
    pieces = [piece for _, held in groups for piece in held]
    rows = pieces[0].shape[1]
    sub = rows // n_v
    half_orb = n_orb // 2

    def kernel(index, *refs):
        held = refs[: len(pieces)]
        sides = [
            refs[len(pieces) + side * n_orb : len(pieces) + (side + 1) * n_orb]
            for side in range(2)
        ]
        out, amp, acc = refs[len(pieces) + 2 * n_orb :]
        step = pl.program_id(0)

        @pl.when(step == 0)
        def _():
            base = at = 0
            for group, stored in groups:
                for block in range(count):
                    columns = pl.ds(pl.multiple_of(index[1 + block] * bw, 128), bw)
                    for p in range(len(group)):
                        amp[base + p, :, columns] = held[at][p]
                    at += 1
                base += len(group)

        acc[...] = jnp.zeros_like(acc)

        def add(side, p, i, j):
            acc[i] += jnp.dot(amp[p], sides[side][j][...], preferred_element_type=F32)

        for side in range(2):

            @pl.when((step >= side * steps) & (step < (side + 1) * steps))
            def _(side=side):
                for p, (i, j) in enumerate(pairs):
                    if i == j:
                        add(side, p, i, j)
                    else:
                        flip = index[1 + count + mixed.index((i, j))]

                        @pl.when(flip == 0)
                        def _(p=p, i=i, j=j):
                            add(side, p, i, j)

                        @pl.when(flip != 0)
                        def _(p=p, i=i, j=j):
                            add(side, p, j, i)

        for i in range(n_orb):
            for v in range(n_v):
                out[v, i // half_orb, 0, i % half_orb] = acc[i, v * sub : (v + 1) * sub, :].astype(BF)

    index = jnp.concatenate(
        [jnp.reshape(core, (1,)), blocks] + [jnp.reshape(flips[pair], (1,)) for pair in mixed]
    ).astype(jnp.int32)

    def place(t, index):
        second = (t >= steps).astype(jnp.int32)
        return (0, 0, (index[0] + second) % 2, 0, 0, t - second * steps)

    return call(
        kernel,
        index,
        (*pieces, *[own[o] for o in range(n_orb)], *[sib[o] for o in range(n_orb)]),
        (2 * steps,),
        [pl.BlockSpec(piece.shape, lambda t, index: (0, 0, 0)) for piece in pieces]
        + [pl.BlockSpec((n_virt, tile), lambda t, index: (0, jnp.minimum(t, steps - 1)))] * n_orb
        + [pl.BlockSpec((n_virt, tile), lambda t, index: (0, jnp.maximum(t - steps, 0)))] * n_orb,
        pl.BlockSpec((n_v, 2, 1, half_orb, sub, tile), place),
        jax.ShapeDtypeStruct((n_v, 2, 2, half_orb, sub, width), BF),
        [
            pltpu.VMEM((len(pairs), rows, n_virt), BF),
            pltpu.VMEM((n_orb, rows, tile), F32),
        ],
        cost(
            4 * len(pairs) * rows * n_virt * width,
            4 * n_orb * n_virt * width + 2 * len(pairs) * rows * n_virt,
        ),
        "contract",
    )


def local(pair_list, half_ints, vir_coef, metric, occ_energy, vir_energy):
    n_z, n_v = lax.axis_size("z"), lax.axis_size("v")
    z, v, c, x = (lax.axis_index(name) for name in "zvcx")
    mu_rows, occ_rows, aux = half_ints.shape
    n_virt = vir_coef.shape[1]
    n_orb = 2 * occ_rows
    paired = n_v == 2
    a_rows = n_virt // (2 * n_z)
    sub = a_rows // (2 * n_v)

    def order(value, axis=0):
        shape = value.shape
        split = value.reshape(shape[:axis] + (n_v, 2, n_z, 2, sub) + shape[axis + 1 :])
        perm = [axis + 2, axis + 1, axis + 3, axis, axis + 4]
        rest = list(range(axis + 5, split.ndim))
        return split.transpose(list(range(axis)) + perm + rest).reshape(shape)

    listed = jnp.concatenate([pair_list, swap(pair_list, "x")])
    flips = {
        (i, j): jnp.any((listed[:, 0] == j) & (listed[:, 1] == i)).astype(jnp.int32)
        for i in range(n_orb)
        for j in range(i + 1, n_orb)
    }

    if paired:
        owners = jnp.stack([v * 2 + c, v * 2 + 1 - c, (1 - v) * 2 + c, (1 - v) * 2 + 1 - c])
    else:
        owners = jnp.arange(2 * n_v)

    def fitted_pair(at):
        block = half_ints[:, at, :]
        if paired:
            far = swap(block, "v")
            pieces = [block, swap(block, "c"), far, swap(far, "c")]
        else:
            gathered = lax.all_gather(block, ("v", "c"))
            pieces = [gathered[s] for s in range(2 * n_v)]
        moved = swap(fit(pieces, owners, metric, 1 - x), "x")
        return fit(pieces, owners, metric, x), moved

    def gather_z(value):
        return lax.all_gather(value, "z", axis=0, tiled=True)

    quarter = n_virt // 4
    turned = order(vir_coef.T)
    piece = lax.dynamic_slice_in_dim(turned, (x * 2 + c) * quarter, quarter)
    piece = lax.all_gather(piece, "z", axis=1, tiled=True)
    other = swap(piece, "x")
    coef = jnp.zeros((4, quarter, mu_rows * n_z), BF)
    for part, owner in (
        (piece, x * 2 + c),
        (other, (1 - x) * 2 + c),
        (swap(piece, "c"), x * 2 + 1 - c),
        (swap(other, "c"), (1 - x) * 2 + 1 - c),
    ):
        coef = lax.dynamic_update_slice(coef, part[None], (owner, 0, 0))
    coef = coef.reshape(n_virt, mu_rows * n_z)

    own, sib = {}, {}

    def transform(orbital, held):
        own[orbital] = jnp.dot(coef, held, preferred_element_type=F32).astype(BF)
        sib[orbital] = swap(own[orbital], "c")

    energies = order(vir_energy)
    a_block = z * 2 + c
    if paired:
        blocks = jnp.stack(
            [
                h * 4 + ((x ^ r1) * 2 + (v ^ r2) if h == 0 else (x ^ r2) * 2 + (v ^ r1))
                for h in range(2)
                for r1 in range(2)
                for r2 in range(2)
            ]
        )
        segments = [2] * 4
    else:
        blocks = jnp.arange(2 * n_v)
        segments = [2 * n_v]
    bw = n_virt // blocks.shape[0]

    def amplitude(total, pairs, part, block):
        rows = total.shape[1]
        a = lax.dynamic_slice_in_dim(energies, a_block * a_rows + part * rows, rows)
        b = lax.dynamic_slice_in_dim(energies, block * bw, bw)
        occ = jnp.stack([occ_energy[i] + occ_energy[j] for i, j in pairs])
        denom = (a[None, :, None] + b[None, None, :]) - occ[:, None, None]
        return (-total / denom).astype(BF)

    def reduce_part(segs, pairs, part):
        if not paired:
            total = lax.psum_scatter(segs[0].astype(F32), "v", scatter_dimension=0, tiled=True)
            total = lax.psum_scatter(total, "x", scatter_dimension=0, tiled=True)
            held = amplitude(total[0], pairs, part, v * 2 + x)
            held = lax.all_gather(held, "x")
            held = lax.all_gather(held, "v", axis=0, tiled=True)
            return [held[s] for s in range(2 * n_v)]
        out = []
        for h, (one, two) in enumerate((("x", "v"), ("v", "x"))):
            keep, send = segs[2 * h].astype(F32), segs[2 * h + 1]
            first = swap(send, one).astype(F32)
            second = swap((keep[1] + first[1]).astype(BF), two).astype(F32)
            a00 = amplitude(keep[0] + first[0] + second, pairs, part, h * 4 + x * 2 + v)
            a01 = swap(a00, two)
            a10 = swap(a00, one)
            a11 = swap(a01, one)
            out += [a00, a01, a10, a11]
        return out

    groups = []

    def group(pairs):
        parts = coulomb(own, sib, pairs, flips, blocks, a_block, a_rows, segments)
        groups.append((pairs, [reduce_part(parts[part], pairs, part) for part in range(2)]))

    lower, upper = {}, {}
    for at in range(occ_rows):
        mine, moved = fitted_pair(at)
        if at == 0:
            mine, moved = gather_z(mine), gather_z(moved)
        lower[at] = jnp.where(x == 0, mine, moved)
        upper[at] = jnp.where(x == 0, moved, mine)
        if at > 0:
            lower[at], upper[at] = gather_z(lower[at]), gather_z(upper[at])

    for at in range(occ_rows):
        for orbital, held in ((at, lower[at]), (at + occ_rows, upper[at])):
            seen = list(own)
            transform(orbital, held)
            if at == 0:
                continue
            group([tuple(sorted((s, orbital))) for s in seen] + [(orbital, orbital)])
        if at == 0:
            first, second = own
            group([(first, first), (first, second), (second, second)])

    def exchange(value):
        if not paired:
            value = lax.all_to_all(value, "v", 0, 0, tiled=True)
            value = lax.all_to_all(value, "x", 1, 1, tiled=True)
            return value.transpose(0, 2, 1, 3, 4, 5)

        def take(row, column):
            return lax.dynamic_slice(value, (row, column, 0, 0, 0, 0), (1, 1) + value.shape[2:])[0]

        parts = (
            (take(v, x), v, x),
            (swap(take(v, 1 - x), "x"), v, 1 - x),
            (swap(take(1 - v, x), "v"), 1 - v, x),
            (lax.ppermute(take(1 - v, 1 - x), ("v", "x"), [(k, 3 - k) for k in range(4)]), 1 - v, 1 - x),
        )
        held = jnp.zeros((2, 2, 2) + value.shape[3:], BF)
        for part, row, column in parts:
            held = lax.dynamic_update_slice(
                held, part.transpose(1, 0, 2, 3, 4)[None], (row, 0, column, 0, 0, 0)
            )
        return held

    results = []
    for part in range(2):
        value = contract(
            [(pairs, held[part]) for pairs, held in groups], own, sib, flips, blocks, c, n_v
        )
        value = exchange(value)
        value = value.reshape((n_z, 2 * n_v // n_z) + value.shape[2:])
        results.append(lax.all_to_all(value, "z", 0, 0, tiled=True))
    out = jnp.stack(results).transpose(1, 0, 5, 4, 2, 3, 6)
    return out.astype(F32).reshape(n_virt // (2 * n_v), occ_rows, -1)


def solution(mesh):
    n_ao, n_vir, n_occ = (mesh.shape[name] for name in ("ao", "vir", "occ"))
    fine = Mesh(mesh.devices.reshape(n_ao, n_vir // 2, 2, n_occ), ("z", "v", "c", "x"))
    vir = ("v", "c")
    return jax.shard_map(
        local,
        mesh=fine,
        in_specs=(P("x", None), P("z", "x", vir), P("z", None), P(vir, None), P(), P()),
        out_specs=P(vir, "x", "z"),
        check_vma=False,
    )
```

time: 1680 us -> 806 us (0.48)
  waiting for transfers between devices: 1220 us -> 343 us
  matrix products: 252 us -> 51.7 us
  Pallas kernels: 0 us -> 159 us
  starting transfers between devices: 0.21 us -> 93.8 us
  blocking collectives: 114 us -> 26.7 us
    reduce_scatter x2 -> x0, waiting for transfers between devices: 561 us -> none  [the longest x1 417 us: local(): lax.psum_scatter(lax.dot_general(columns, flat_half, (((0,), (0,)), ((),...]
    psum x1 -> x0, waiting for transfers between devices: 355 us -> none  [local(): coulomb = lax.psum(part.astype(jnp.bfloat16), 'ao').astype(jnp.float32)]
    ppermute x0 -> x82, waiting for transfers between devices: none -> 274 us  [the longest x80 273 us: swap(): return lax.ppermute(value, axis, [(0, 1), (1, 0)])]
    all_gather x3 -> x5, waiting for transfers between devices: 306 us -> 68.3 us  [the longest x4 68.3 us: gather_z(): return lax.all_gather(value, 'z', axis=0, tiled=True)]
    dot_general x8 -> x4, matrix products: 252 us -> 51.7 us  [transform(): own[orbital] = jnp.dot(coef, held, preferred_element_type=F32).astype(BF)]
    pallas_call x0 -> x9, Pallas kernels: none -> 159 us  [call(): pl.pallas_call(kernel, grid_spec=pltpu.PrefetchScalarGridSpec(num_scalar_...]
    ppermute x0 -> x82, starting transfers between devices: none -> 89.8 us  [the longest x80 87.8 us: swap(): return lax.ppermute(value, axis, [(0, 1), (1, 0)])]
    all_to_all x2 -> x1, blocking collectives: 114 us -> 26.7 us  [local(): results.append(lax.all_to_all(value, 'z', 0, 0, tiled=True))]
  transfers between devices with their start and end apart: 6 -> 88, of which waited for: 6 -> 39; matrix products, arithmetic and copies ran while one was open for 1% -> 13% of each run, Pallas kernels for 0% -> 17%
where the time goes in v1:
time: 806 us; the launch traced here: 796 us
  waiting for transfers between devices  343 us (43%)
  Pallas kernels  159 us (20%)
  starting transfers between devices  93.8 us (12%)
  local copies, waits for them, and re-layouts  78.2 us (10%)
  matrix products  51.7 us (6%)
  between operations  30.3 us (4%)
  blocking collectives  26.7 us (3%)
  other arithmetic  13.4 us (2%)
    ppermute x80, waiting for transfers between devices, swap(): return lax.ppermute(value, axis, [(0, 1), (1, 0)])  273 us
    pallas_call x9, Pallas kernels, call(): pl.pallas_call(kernel, grid_spec=pltpu.PrefetchScalarGridSpec(num_scalar_...  159 us
    ppermute x80, starting transfers between devices, swap(): return lax.ppermute(value, axis, [(0, 1), (1, 0)])  87.8 us
    all_gather x4, waiting for transfers between devices, gather_z(): return lax.all_gather(value, 'z', axis=0, tiled=True)  68.3 us
    dot_general x4, matrix products, transform(): own[orbital] = jnp.dot(coef, held, preferred_element_type=F32).astype(BF)  51.7 us
    all_to_all x1, blocking collectives, local(): results.append(lax.all_to_all(value, 'z', 0, 0, tiled=True))  26.7 us
    reshape x2, local copies, waits for them, and re-layouts, local(): return out.astype(F32).reshape(n_virt // (2 * n_v), occ_rows, -1)  17.9 us
  transfers between devices with their start and end apart: 88, of which 39 were waited for; matrix products, arithmetic and copies ran while one was open for 13% of the time, Pallas kernels for 17%

profile of v1, /device:TPU:0, one launch (start us, length us, event | category | flops | bytes accessed | tf_op | source)
XLA Modules:
  0.0 795.8 jit_solution(7849079435760460121)
XLA Ops:
  6.5 9.2 %fusion.96 = (bf16[640,1,1536]{2,1,0:T(2,128)(2,1)}, bf16[640,1,1536]{2,1,0:T(2,128)(2,1)S(1)}) fusion(bf16[640,2,1536]{2,1,0:T(2,128)(2,1)} %param.7), kind=kLoop, calls=%fused_computation.158 | loop fusion | bytes 7864320 | tf_op jit(solution)/shard_map/slice | solution.py:296
  16.2 3.0 collective-permute-start.5
  19.2 4.4 copy.29
  23.6 3.6 copy.30
  29.4 32.8 %collective-permute-done.5.refs_2_ = bf16[640,1536]{1,0:T(8,128)(2,1)} collective-permute-done((bf16[640,1536]{1,0:T(8,128)(2,1)S(1)}, bf16[640,1536]{1,0:T(8,128)(2,1)}, u32[]{:S(2)}, u32[]{:S(2)}) %collective-permute-start.5) | collective-permute-done | bytes 1966112 | tf_op jit(solution)/shard_map/ppermute | solution.py:17
  62.8 3.6 collective-permute-done.6.refs_3_
  66.4 12.5 %fit.4 = bf16[640,768]{1,0:T(8,128)(2,1)} custom-call(s32[5]{0:T(128)} %concatenate.36.index, bf16[640,1536]{1,0:T(8,128)(2,1)} %bitcast.238, bf16[640,1536]{1,0:T(8,128)(2,1)} %collective-permute-done.4.refs_1_, bf16[640,1536]{1,0:T(8,128)(2,1)} %collective-permute-done.5.refs_2_, bf16[640,1536]{1,0:T(8,128)(2,1)} %collective-permute-done.6.refs_3_, ...), custom_call_target="tpu_custom_call" | custom-call | flops 6039797760 | bytes 18284544 | tf_op jit(solution)/shard_map/fit/pallas_call | solution.py:29
  79.7 12.4 %fit.5 = bf16[640,768]{1,0:T(8,128)(2,1)} custom-call(s32[5]{0:T(128)} %concatenate.37.index, bf16[640,1536]{1,0:T(8,128)(2,1)} %bitcast.239, bf16[640,1536]{1,0:T(8,128)(2,1)} %collective-permute-done.4.refs_1_, bf16[640,1536]{1,0:T(8,128)(2,1)} %collective-permute-done.5.refs_2_, bf16[640,1536]{1,0:T(8,128)(2,1)} %collective-permute-done.6.refs_3_, ...), custom_call_target="tpu_custom_call" | custom-call | flops 6039797760 | bytes 18284544 | tf_op jit(solution)/shard_map/fit/pallas_call | solution.py:29
  93.9 22.3 %collective-permute-done.7 = bf16[640,768]{1,0:T(8,128)(2,1)S(1)} collective-permute-done((bf16[640,768]{1,0:T(8,128)(2,1)}, bf16[640,768]{1,0:T(8,128)(2,1)S(1)}, u32[]{:S(2)}, u32[]{:S(2)}) %collective-permute-start.7) | collective-permute-done | bytes 983072 | tf_op jit(solution)/shard_map/ppermute | solution.py:17
  117.2 2.6 copy.45
  121.6 42.4 %collective-permute-done.21.refs_2_ = bf16[640,1536]{1,0:T(8,128)(2,1)S(1)} collective-permute-done((bf16[640,1536]{1,0:T(8,128)(2,1)S(1)}, bf16[640,1536]{1,0:T(8,128)(2,1)S(1)}, u32[]{:S(2)}, u32[]{:S(2)}) %collective-permute-start.21) | collective-permute-done | bytes 1966112 | tf_op jit(solution)/shard_map/ppermute | solution.py:17
  164.0 4.1 collective-permute-done.22.refs_3_
  168.1 12.9 %fit.7 = bf16[640,768]{1,0:T(8,128)(2,1)} custom-call(s32[5]{0:T(128)} %concatenate.37.index, bf16[640,1536]{1,0:T(8,128)(2,1)} %bitcast.242, bf16[640,1536]{1,0:T(8,128)(2,1)} %copy-done.4, bf16[640,1536]{1,0:T(8,128)(2,1)} %copy-done.3, bf16[640,1536]{1,0:T(8,128)(2,1)} %collective-permute-done.22.refs_3_, bf16[1536,6144]{1,0:T(8,128)(2,1)} %refs_4_.7), custom_call_target="tpu_custom_call" | custom-call | flops 6039797760 | bytes 18284544 | tf_op jit(solution)/shard_map/fit/pallas_call | solution.py:29
  182.8 12.5 %fit.6 = bf16[640,768]{1,0:T(8,128)(2,1)} custom-call(s32[5]{0:T(128)} %concatenate.36.index, bf16[640,1536]{1,0:T(8,128)(2,1)} %bitcast.243, bf16[640,1536]{1,0:T(8,128)(2,1)} %copy-done.4, bf16[640,1536]{1,0:T(8,128)(2,1)} %copy-done.3, bf16[640,1536]{1,0:T(8,128)(2,1)} %collective-permute-done.22.refs_3_, bf16[1536,6144]{1,0:T(8,128)(2,1)} %refs_4_.7), custom_call_target="tpu_custom_call" | custom-call | flops 6039797760 | bytes 18284544 | tf_op jit(solution)/shard_map/fit/pallas_call | solution.py:29
  195.2 9.9 %collective-permute-done.23 = bf16[640,768]{1,0:T(8,128)(2,1)S(1)} collective-permute-done((bf16[640,768]{1,0:T(8,128)(2,1)}, bf16[640,768]{1,0:T(8,128)(2,1)S(1)}, u32[]{:S(2)}, u32[]{:S(2)}) %collective-permute-start.23) | collective-permute-done | bytes 983072 | tf_op jit(solution)/shard_map/ppermute | solution.py:17
  205.1 2.6 broadcast_select_fusion
  209.6 56.9 %collective-permute-done.1 = bf16[512,2560]{1,0:T(8,128)(2,1)} collective-permute-done((bf16[512,2560]{1,0:T(8,128)(2,1)}, bf16[512,2560]{1,0:T(8,128)(2,1)}, u32[]{:S(2)}, u32[]{:S(2)}) %collective-permute-start.1) | collective-permute-done | bytes 2621472 | tf_op jit(solution)/shard_map/ppermute | solution.py:17
  266.4 4.7 broadcast_in_dim.10
  272.9 3.5 bitcast_dynamic-update-slice_fusion.2
  276.4 3.4 bitcast_dynamic-update-slice_fusion.1
  279.8 3.5 bitcast_dynamic-update-slice_fusion
  283.2 12.5 %fusion.9.refs_1_.refs_5_.refs_2_.refs_8_.refs_10_.refs_26_ = bf16[2048,768]{1,0:T(8,128)(2,1)S(1)} fusion(bf16[2048,2560]{1,0:T(8,128)(2,1)} %bitcast.24, bf16[2560,768]{1,0:T(8,128)(2,1)} %all-gather.10.cloned.1.call-done, bf16[2560,768]{1,0:T(8,128)(2,1)} %all-gather.8.cloned.1.call-done, pred[]{:T(512)S(6)} %eq.42), kind=kOutput, calls=%fused_computation.8 | convolution fusion | flops 8056602624 | bytes 21495808 | tf_op jit(solution)/shard_map/dot_general | solution.py:327
  296.3 17.9 %all-gather.12.cloned.1.call-done = bf16[2560,768]{1,0:T(8,128)(2,1)} async-done(((bf16[640,768]{1,0:T(8,128)(2,1)}), bf16[2560,768]{1,0:T(8,128)(2,1)}) %all-gather.12.cloned.1.call-update) | async-done | bytes 3932176 | tf_op jit(solution)/shard_map/all_gather | solution.py:307
  314.2 13.4 %convolution_convert_fusion.1.refs_1_.refs_7_.refs_9_.refs_25_ = bf16[2048,768]{1,0:T(8,128)(2,1)} fusion(bf16[2048,2560]{1,0:T(8,128)(2,1)} %bitcast.24, bf16[2560,768]{1,0:T(8,128)(2,1)} %all-gather.12.cloned.1.call-done), kind=kOutput, calls=%fused_computation.10 | convolution fusion | flops 8054636544 | bytes 17563648 | tf_op jit(solution)/shard_map/dot_general | solution.py:327
  327.6 12.1 %fusion.6.refs_0_.refs_4_.refs_6_.refs_8_.refs_24_ = bf16[2048,768]{1,0:T(8,128)(2,1)} fusion(bf16[2048,2560]{1,0:T(8,128)(2,1)} %bitcast.24, bf16[2560,768]{1,0:T(8,128)(2,1)S(1)} %copy-done.63, bf16[2560,768]{1,0:T(8,128)(2,1)S(1)} %copy-done.64, pred[]{:T(512)S(6)} %eq.42), kind=kOutput, calls=%fused_computation.7 | convolution fusion | flops 8056602624 | bytes 21495808 | tf_op jit(solution)/shard_map/dot_general | solution.py:327
  340.3 50.3 %all-gather.14.cloned.1.call-done = bf16[2560,768]{1,0:T(8,128)(2,1)} async-done(((bf16[640,768]{1,0:T(8,128)(2,1)}), bf16[2560,768]{1,0:T(8,128)(2,1)}) %all-gather.14.cloned.1.call-update) | async-done | bytes 3932176 | tf_op jit(solution)/shard_map/all_gather | solution.py:307
  390.7 13.7 %convolution_convert_fusion.refs_3_.refs_11_.refs_27_ = bf16[2048,768]{1,0:T(8,128)(2,1)} fusion(bf16[2048,2560]{1,0:T(8,128)(2,1)} %bitcast.24, bf16[2560,768]{1,0:T(8,128)(2,1)} %all-gather.14.cloned.1.call-done), kind=kOutput, calls=%fused_computation.9 | convolution fusion | flops 8054636544 | bytes 17563648 | tf_op jit(solution)/shard_map/dot_general | solution.py:327
  426.9 16.8 %coulomb.4 = (bf16[2,3,128,256]{3,2,1,0:T(8,128)(2,1)}, bf16[2,3,128,256]{3,2,1,0:T(8,128)(2,1)}, bf16[2,3,128,256]{3,2,1,0:T(8,128)(2,1)}, bf16[2,3,128,256]{3,...) custom-call(s32[11]{0:T(128)} %concatenate.38.index, ...), custom_call_target="tpu_custom_call" | custom-call | flops 4831838208 | bytes 22020096 | tf_op jit(solution)/shard_map/coulomb/pallas_call | solution.py:29
  443.8 15.3 %coulomb.3 = (bf16[2,3,128,256]{3,2,1,0:T(8,128)(2,1)}, bf16[2,3,128,256]{3,2,1,0:T(8,128)(2,1)}, bf16[2,3,128,256]{3,2,1,0:T(8,128)(2,1)}, bf16[2,3,128,256]{3,...) custom-call(s32[10]{0:T(128)} %concatenate.35.index, ...), custom_call_target="tpu_custom_call" | custom-call | flops 4831838208 | bytes 15728640 | tf_op jit(solution)/shard_map/coulomb/pallas_call | solution.py:29
  462.9 21.4 %coulomb.5 = (bf16[2,4,128,256]{3,2,1,0:T(8,128)(2,1)}, bf16[2,4,128,256]{3,2,1,0:T(8,128)(2,1)}, bf16[2,4,128,256]{3,2,1,0:T(8,128)(2,1)}, bf16[2,4,128,256]{3,...) custom-call(s32[12]{0:T(128)} %concatenate.39.index, ...), custom_call_target="tpu_custom_call" | custom-call | flops 6442450944 | bytes 29360128 | tf_op jit(solution)/shard_map/coulomb/pallas_call | solution.py:29
  494.5 17.9 %collective-permute-done.30 = bf16[2,3,128,256]{3,2,1,0:T(8,128)(2,1)S(1)} collective-permute-done((bf16[2,3,128,256]{3,2,1,0:T(8,128)(2,1)S(1)}, bf16[2,3,128,256]{3,2,1,0:T(8,128)(2,1)S(1)}, u32[]{:S(2)}, u32[]{:S(2)}) %collective-permute-start.30) | collective-permute-done | bytes 393248 | tf_op jit(solution)/shard_map/ppermute | solution.py:17
  512.4 2.0 collective-permute-start.49
  514.6 3.8 collective-permute-done.15
  522.2 6.4 collective-permute-done.59
  531.0 2.0 collective-permute-start.55
  535.8 3.0 collective-permute-done.26
  538.7 2.2 collective-permute-done.11
  550.8 2.2 collective-permute-done.60
  554.7 2.5 collective-permute-done.12.refs_1_
  557.7 3.7 collective-permute-done.27.refs_9_
  562.5 6.6 collective-permute-done.13.refs_2_
  576.2 3.2 collective-permute-start.38
  581.2 2.7 collective-permute-done.32.refs_13_
  586.1 3.3 collective-permute-start.19
  589.4 4.3 collective-permute-done.14.refs_3_
  595.3 2.6 collective-permute-done.29.refs_11_
  597.9 2.6 collective-permute-start.44
  604.3 5.5 collective-permute-done.34.refs_15_
  611.4 27.7 %contract.2 = bf16[2,2,2,2,64,768]{5,4,3,2,1,0:T(8,128)(2,1)} custom-call(s32[15]{0:T(128)} %concatenate.34.index, bf16[3,128,256]{2,1,0:T(8,128)(2,1)} %copy-done.17, bf16[3,128,256]{2,1,0:T(8,128)(2,1)} %copy-done.43, bf16[3,128,256]{2,1,0:T(8,128)(2,1)} %copy-done.45, bf16[3,128,256]{2,1,0:T(8,128)(2,1)} %copy-done.55, bf16[3,128,256]{2,1,0:T(8,128)(2,1)} %copy-done.19, ...), custom_call_target="tpu_custom_call" | custom-call | flops 8053063680 | bytes 30408704 | tf_op jit(solution)/shard_map/contract/pallas_call | solution.py:29
  642.6 2.0 collective-permute-start.47
  649.0 7.7 collective-permute-done.56.refs_5_
  656.7 2.1 collective-permute-start.67
  663.2 5.5 collective-permute-done.67.refs_14_
  668.7 3.0 collective-permute-start.61
  673.8 2.2 collective-permute-start.58
  677.9 2.2 collective-permute-start.68
  683.1 3.8 all-to-all-start
  692.6 5.8 collective-permute-done.63.refs_11_
  700.1 27.5 %contract.3 = bf16[2,2,2,2,64,768]{5,4,3,2,1,0:T(8,128)(2,1)} custom-call(s32[15]{0:T(128)} %concatenate.34.index, bf16[3,128,256]{2,1,0:T(8,128)(2,1)} %copy-done.16, bf16[3,128,256]{2,1,0:T(8,128)(2,1)} %collective-permute-done.51.refs_1_, bf16[3,128,256]{2,1,0:T(8,128)(2,1)} %copy-done.53, bf16[3,128,256]{2,1,0:T(8,128)(2,1)} %collective-permute-done.53.refs_3_, ...), custom_call_target="tpu_custom_call" | custom-call | flops 8053063680 | bytes 30408704 | tf_op jit(solution)/shard_map/contract/pallas_call | solution.py:29
  733.6 3.1 collective-permute-done.79
  736.8 3.9 collective-permute-done.80
  742.3 26.7 %all_to_all.10 = bf16[4,1,2,2,64,768]{5,4,3,2,1,0:T(8,128)(2,1)S(1)} all-to-all(bf16[4,1,2,2,64,768]{5,4,3,2,1,0:T(8,128)(2,1)S(1)} %bitcast.246), channel_id=1, replica_groups=mesh['z'=4,'v'=2,'c'=2,'x'=2] {'z'}, dimensions={0} | all-to-all | bytes 3145728 | tf_op jit(solution)/shard_map/all_to_all | solution.py:431
  770.8 7.5 copy.39
  778.3 10.4 %reshape.321 = f32[512,2,1536]{2,1,0:T(2,128)} reshape(f32[4,2,64,2,1,2,768]{6,5,3,2,1,0,4:T(2,128)} %copy.39) | data formatting | bytes 12582912 | tf_op jit(solution)/shard_map/reshape | solution.py:433
  (360 shorter events, 111.7 us)
Async XLA Ops:
  6.5 201.3 %all-gather.6.cloned.1.call-start = ((), (), s32[]{:S(2)}) async-start(), calls=%async_computation.2 | async-start | bytes 3276800 | tf_op jit(solution)/shard_map/all_gather | solution.py:312
  16.2 46.0 %collective-permute-start.5 = (bf16[640,1536]{1,0:T(8,128)(2,1)S(1)}, bf16[640,1536]{1,0:T(8,128)(2,1)}, u32[]{:S(2)}, u32[]{:S(2)}) collective-permute-start(bf16[640,1536]{1,0:T(8,128)(2,1)S(1)} %bitcast.236), channel_id=1, source_target_pairs={{0,4},{4,0},{1,5},{5,1},{2,6},{6,2},{3,7},{7,3},{8,12},{12,8},{9,1... | collective-permute-start | bytes 5898248 | tf_op jit(solution)/shard_map/ppermute | solution.py:17
  29.2 254.0 %all-gather.8.cloned.1.call-start = ((), (), s32[]{:S(2)}) async-start(), calls=%async_computation.3 | async-start | bytes 4915200 | tf_op jit(solution)/shard_map/all_gather | solution.py:307
  29.3 33.5 %collective-permute-start.4 = (bf16[640,1536]{1,0:T(8,128)(2,1)S(1)}, bf16[640,1536]{1,0:T(8,128)(2,1)}, u32[]{:S(2)}, u32[]{:S(2)}) collective-permute-start(bf16[640,1536]{1,0:T(8,128)(2,1)S(1)} %bitcast.237), channel_id=1, source_target_pairs={{0,2},{2,0},{1,3},{3,1},{4,6},{6,4},{5,7},{7,5},{8,10},{10,8},{9,1... | collective-permute-start | bytes 5898248 | tf_op jit(solution)/shard_map/ppermute | solution.py:17
  79.0 204.2 %all-gather.10.cloned.1.call-start = ((), (), s32[]{:S(2)}) async-start(), calls=%async_computation.4 | async-start | bytes 4915200 | tf_op jit(solution)/shard_map/all_gather | solution.py:307
  92.2 24.0 %collective-permute-start.7 = (bf16[640,768]{1,0:T(8,128)(2,1)}, bf16[640,768]{1,0:T(8,128)(2,1)S(1)}, u32[]{:S(2)}, u32[]{:S(2)}) collective-permute-start(bf16[640,768]{1,0:T(8,128)(2,1)} %fit.5), channel_id=1, source_target_pairs={{0,1},{1,0},{2,3},{3,2},{4,5},{5,4},{6,7},{7,6},{8,9},{9,8},{10,11... | collective-permute-start | bytes 2949128 | tf_op jit(solution)/shard_map/ppermute | solution.py:17
  117.2 197.0 %all-gather.12.cloned.1.call-start = ((), (), s32[]{:S(2)}) async-start(), calls=%async_computation.5 | async-start | bytes 4915200 | tf_op jit(solution)/shard_map/all_gather | solution.py:307
  119.8 44.2 %collective-permute-start.21 = (bf16[640,1536]{1,0:T(8,128)(2,1)S(1)}, bf16[640,1536]{1,0:T(8,128)(2,1)S(1)}, u32[]{:S(2)}, u32[]{:S(2)}) collective-permute-start(bf16[640,1536]{1,0:T(8,128)(2,1)S(1)} %bitcast.240), channel_id=1, source_target_pairs={{0,4},{4,0},{1,5},{5,1},{2,6},{6,2},{3,7},{7,3},{8,12},{12,8},{9,1... | collective-permute-start | bytes 5898248 | tf_op jit(solution)/shard_map/ppermute | solution.py:17
  121.6 42.4 %collective-permute-start.20 = (bf16[640,1536]{1,0:T(8,128)(2,1)S(1)}, bf16[640,1536]{1,0:T(8,128)(2,1)S(1)}, u32[]{:S(2)}, u32[]{:S(2)}) collective-permute-start(bf16[640,1536]{1,0:T(8,128)(2,1)S(1)} %bitcast.241), channel_id=1, source_target_pairs={{0,2},{2,0},{1,3},{3,1},{4,6},{6,4},{5,7},{7,5},{8,10},{10,8},{9,1... | collective-permute-start | bytes 5898248 | tf_op jit(solution)/shard_map/ppermute | solution.py:17
  181.0 24.1 %collective-permute-start.23 = (bf16[640,768]{1,0:T(8,128)(2,1)}, bf16[640,768]{1,0:T(8,128)(2,1)S(1)}, u32[]{:S(2)}, u32[]{:S(2)}) collective-permute-start(bf16[640,768]{1,0:T(8,128)(2,1)} %fit.7), channel_id=1, source_target_pairs={{0,1},{1,0},{2,3},{3,2},{4,5},{5,4},{6,7},{7,6},{8,9},{9,8},{10,11... | collective-permute-start | bytes 2949128 | tf_op jit(solution)/shard_map/ppermute | solution.py:17
  207.7 182.9 %all-gather.14.cloned.1.call-start = ((), (), s32[]{:S(2)}) async-start(), calls=%async_computation.6 | async-start | bytes 4915200 | tf_op jit(solution)/shard_map/all_gather | solution.py:307
  207.8 58.6 %collective-permute-start.1 = (bf16[512,2560]{1,0:T(8,128)(2,1)}, bf16[512,2560]{1,0:T(8,128)(2,1)}, u32[]{:S(2)}, u32[]{:S(2)}) collective-permute-start(bf16[512,2560]{1,0:T(8,128)(2,1)} %all-gather.6.cloned.1.call-done), channel_id=1, source_target_pairs={{0,1},{1,0},{2,3},{3,2},{4,5},{5,4},{6,7},{7,6},{8,9},{9,8},{10,11... | collective-permute-start | bytes 7864328 | tf_op jit(solution)/shard_map/ppermute | solution.py:17
  209.6 66.8 %collective-permute-start.2 = (bf16[512,2560]{1,0:T(8,128)(2,1)}, bf16[512,2560]{1,0:T(8,128)(2,1)}, u32[]{:S(2)}, u32[]{:S(2)}) collective-permute-start(bf16[512,2560]{1,0:T(8,128)(2,1)} %all-gather.6.cloned.1.call-done), channel_id=1, source_target_pairs={{0,2},{2,0},{1,3},{3,1},{4,6},{6,4},{5,7},{7,5},{8,10},{10,8},{9,1... | collective-permute-start | bytes 7864328 | tf_op jit(solution)/shard_map/ppermute | solution.py:17
  266.4 13.3 %collective-permute-start.3 = (bf16[512,2560]{1,0:T(8,128)(2,1)}, bf16[512,2560]{1,0:T(8,128)(2,1)}, u32[]{:S(2)}, u32[]{:S(2)}) collective-permute-start(bf16[512,2560]{1,0:T(8,128)(2,1)} %collective-permute-done.1), channel_id=1, source_target_pairs={{0,2},{2,0},{1,3},{3,1},{4,6},{6,4},{5,7},{7,5},{8,10},{10,8},{9,1... | collective-permute-start | bytes 7864328 | tf_op jit(solution)/shard_map/ppermute | solution.py:17
  295.7 131.2 %collective-permute-start.9 = (bf16[2048,768]{1,0:T(8,128)(2,1)S(1)}, bf16[2048,768]{1,0:T(8,128)(2,1)}, u32[]{:S(2)}, u32[]{:S(2)}) collective-permute-start(bf16[2048,768]{1,0:T(8,128)(2,1)S(1)} %fusion.9.refs_1_.refs_5_.refs_2_.refs_8_.refs_10_.refs_26_), channel_id=1, source_target_pairs={{0,2},{2,0},{1,3},{3,1},{4,6},{6,4},{5,7},{7,5},{8,10},{10,8},{9,1... | collective-permute-start | bytes 9437192 | tf_op jit(solution)/shard_map/ppermute | solution.py:17
  327.6 99.3 %collective-permute-start.24 = (bf16[2048,768]{1,0:T(8,128)(2,1)}, bf16[2048,768]{1,0:T(8,128)(2,1)}, u32[]{:S(2)}, u32[]{:S(2)}) collective-permute-start(bf16[2048,768]{1,0:T(8,128)(2,1)} %convolution_convert_fusion.1.refs_1_.refs_7_.refs_9_.refs_25_), channel_id=1, source_target_pairs={{0,2},{2,0},{1,3},{3,1},{4,6},{6,4},{5,7},{7,5},{8,10},{10,8},{9,1... | collective-permute-start | bytes 9437192 | tf_op jit(solution)/shard_map/ppermute | solution.py:17
  339.8 87.1 %collective-permute-start.8 = (bf16[2048,768]{1,0:T(8,128)(2,1)}, bf16[2048,768]{1,0:T(8,128)(2,1)}, u32[]{:S(2)}, u32[]{:S(2)}) collective-permute-start(bf16[2048,768]{1,0:T(8,128)(2,1)} %fusion.6.refs_0_.refs_4_.refs_6_.refs_8_.refs_24_), channel_id=1, source_target_pairs={{0,2},{2,0},{1,3},{3,1},{4,6},{6,4},{5,7},{7,5},{8,10},{10,8},{9,1... | collective-permute-start | bytes 9437192 | tf_op jit(solution)/shard_map/ppermute | solution.py:17
  404.4 58.5 %collective-permute-start.35 = (bf16[2048,768]{1,0:T(8,128)(2,1)}, bf16[2048,768]{1,0:T(8,128)(2,1)}, u32[]{:S(2)}, u32[]{:S(2)}) collective-permute-start(bf16[2048,768]{1,0:T(8,128)(2,1)} %convolution_convert_fusion.refs_3_.refs_11_.refs_27_), channel_id=1, source_target_pairs={{0,2},{2,0},{1,3},{3,1},{4,6},{6,4},{5,7},{7,5},{8,10},{10,8},{9,1... | collective-permute-start | bytes 9437192 | tf_op jit(solution)/shard_map/ppermute | solution.py:17
  404.5 15.2 %collective-permute-start = (s32[5,2]{0,1:T(2,128)S(1)}, s32[5,2]{0,1:T(2,128)}, u32[]{:S(2)}, u32[]{:S(2)}) collective-permute-start(s32[5,2]{0,1:T(2,128)S(1)} %copy-done.62), channel_id=1, source_target_pairs={{0,1},{1,0},{2,3},{3,2},{4,5},{5,4},{6,7},{7,6},{8,9},{9,8},{10,11... | collective-permute-start | bytes 128 | tf_op jit(solution)/shard_map/ppermute | solution.py:17
  443.7 45.0 %collective-permute-start.25 = (bf16[2,3,128,256]{3,2,1,0:T(8,128)(2,1)}, bf16[2,3,128,256]{3,2,1,0:T(8,128)(2,1)S(1)}, u32[]{:S(2)}, u32[]{:S(2)}) collective-permute-start(bf16[2,3,128,256]{3,2,1,0:T(8,128)(2,1)} %get-tuple-element.34), channel_id=1, source_target_pairs={{0,1},{1,0},{2,3},{3,2},{4,5},{5,4},{6,7},{7,6},{8,9},{9,8},{10,11... | collective-permute-start | bytes 1179656 | tf_op jit(solution)/shard_map/ppermute | solution.py:17
  459.1 31.1 %collective-permute-start.10 = (bf16[2,3,128,256]{3,2,1,0:T(8,128)(2,1)}, bf16[2,3,128,256]{3,2,1,0:T(8,128)(2,1)S(1)}, u32[]{:S(2)}, u32[]{:S(2)}) collective-permute-start(bf16[2,3,128,256]{3,2,1,0:T(8,128)(2,1)} %get-tuple-element.30), channel_id=1, source_target_pairs={{0,1},{1,0},{2,3},{3,2},{4,5},{5,4},{6,7},{7,6},{8,9},{9,8},{10,11... | collective-permute-start | bytes 1179656 | tf_op jit(solution)/shard_map/ppermute | solution.py:17
  460.8 31.1 %collective-permute-start.54 = (bf16[2,3,128,256]{3,2,1,0:T(8,128)(2,1)}, bf16[2,3,128,256]{3,2,1,0:T(8,128)(2,1)S(1)}, u32[]{:S(2)}, u32[]{:S(2)}) collective-permute-start(bf16[2,3,128,256]{3,2,1,0:T(8,128)(2,1)} %get-tuple-element.44), channel_id=1, source_target_pairs={{0,4},{4,0},{1,5},{5,1},{2,6},{6,2},{3,7},{7,3},{8,12},{12,8},{9,1... | collective-permute-start | bytes 1179656 | tf_op jit(solution)/shard_map/ppermute | solution.py:17
  462.0 31.5 %collective-permute-start.64 = (bf16[2,3,128,256]{3,2,1,0:T(8,128)(2,1)S(1)}, bf16[2,3,128,256]{3,2,1,0:T(8,128)(2,1)S(1)}, u32[]{:S(2)}, u32[]{:S(2)}) collective-permute-start(bf16[2,3,128,256]{3,2,1,0:T(8,128)(2,1)S(1)} %copy-done.72), channel_id=1, source_target_pairs={{0,4},{4,0},{1,5},{5,1},{2,6},{6,2},{3,7},{7,3},{8,12},{12,8},{9,1... | collective-permute-start | bytes 1179656 | tf_op jit(solution)/shard_map/ppermute | solution.py:17
  484.3 45.5 %collective-permute-start.36 = (bf16[2,4,128,256]{3,2,1,0:T(8,128)(2,1)}, bf16[2,4,128,256]{3,2,1,0:T(8,128)(2,1)S(1)}, u32[]{:S(2)}, u32[]{:S(2)}) collective-permute-start(bf16[2,4,128,256]{3,2,1,0:T(8,128)(2,1)} %get-tuple-element.38), channel_id=1, source_target_pairs={{0,1},{1,0},{2,3},{3,2},{4,5},{5,4},{6,7},{7,6},{8,9},{9,8},{10,11... | collective-permute-start | bytes 1572872 | tf_op jit(solution)/shard_map/ppermute | solution.py:17
  489.1 41.9 %collective-permute-start.74 = (bf16[2,4,128,256]{3,2,1,0:T(8,128)(2,1)S(1)}, bf16[2,4,128,256]{3,2,1,0:T(8,128)(2,1)S(1)}, u32[]{:S(2)}, u32[]{:S(2)}) collective-permute-start(bf16[2,4,128,256]{3,2,1,0:T(8,128)(2,1)S(1)} %copy-done.67), channel_id=1, source_target_pairs={{0,4},{4,0},{1,5},{5,1},{2,6},{6,2},{3,7},{7,3},{8,12},{12,8},{9,1... | collective-permute-start | bytes 1572872 | tf_op jit(solution)/shard_map/ppermute | solution.py:17
  490.2 42.9 %collective-permute-start.69 = (bf16[2,4,128,256]{3,2,1,0:T(8,128)(2,1)S(1)}, bf16[2,4,128,256]{3,2,1,0:T(8,128)(2,1)S(1)}, u32[]{:S(2)}, u32[]{:S(2)}) collective-permute-start(bf16[2,4,128,256]{3,2,1,0:T(8,128)(2,1)S(1)} %copy-done.66), channel_id=1, source_target_pairs={{0,1},{1,0},{2,3},{3,2},{4,5},{5,4},{6,7},{7,6},{8,9},{9,8},{10,11... | collective-permute-start | bytes 1572872 | tf_op jit(solution)/shard_map/ppermute | solution.py:17
  492.0 20.4 %collective-permute-start.30 = (bf16[2,3,128,256]{3,2,1,0:T(8,128)(2,1)S(1)}, bf16[2,3,128,256]{3,2,1,0:T(8,128)(2,1)S(1)}, u32[]{:S(2)}, u32[]{:S(2)}) collective-permute-start(bf16[2,3,128,256]{3,2,1,0:T(8,128)(2,1)S(1)} %copy-done.70), channel_id=1, source_target_pairs={{0,4},{4,0},{1,5},{5,1},{2,6},{6,2},{3,7},{7,3},{8,12},{12,8},{9,1... | collective-permute-start | bytes 1179656 | tf_op jit(solution)/shard_map/ppermute | solution.py:17
  493.5 24.9 %collective-permute-start.15 = (bf16[2,3,128,256]{3,2,1,0:T(8,128)(2,1)S(1)}, bf16[2,3,128,256]{3,2,1,0:T(8,128)(2,1)S(1)}, u32[]{:S(2)}, u32[]{:S(2)}) collective-permute-start(bf16[2,3,128,256]{3,2,1,0:T(8,128)(2,1)S(1)} %copy-done.71), channel_id=1, source_target_pairs={{0,4},{4,0},{1,5},{5,1},{2,6},{6,2},{3,7},{7,3},{8,12},{12,8},{9,1... | collective-permute-start | bytes 1179656 | tf_op jit(solution)/shard_map/ppermute | solution.py:17
  521.6 13.7 %collective-permute-start.41 = (bf16[2,4,128,256]{3,2,1,0:T(8,128)(2,1)S(1)}, bf16[2,4,128,256]{3,2,1,0:T(8,128)(2,1)S(1)}, u32[]{:S(2)}, u32[]{:S(2)}) collective-permute-start(bf16[2,4,128,256]{3,2,1,0:T(8,128)(2,1)S(1)} %copy-done.65), channel_id=1, source_target_pairs={{0,4},{4,0},{1,5},{5,1},{2,6},{6,2},{3,7},{7,3},{8,12},{12,8},{9,1... | collective-permute-start | bytes 1572872 | tf_op jit(solution)/shard_map/ppermute | solution.py:17
  529.8 11.0 %collective-permute-start.11 = (bf16[3,128,256]{2,1,0:T(8,128)(2,1)S(1)}, bf16[3,128,256]{2,1,0:T(8,128)(2,1)S(1)}, u32[]{:S(2)}, u32[]{:S(2)}) collective-permute-start(bf16[3,128,256]{2,1,0:T(8,128)(2,1)S(1)} %fusion.88), channel_id=1, source_target_pairs={{0,4},{4,0},{1,5},{5,1},{2,6},{6,2},{3,7},{7,3},{8,12},{12,8},{9,1... | collective-permute-start | bytes 589832 | tf_op jit(solution)/shard_map/ppermute | solution.py:17
  531.0 11.6 %collective-permute-start.55 = (bf16[3,128,256]{2,1,0:T(8,128)(2,1)S(1)}, bf16[3,128,256]{2,1,0:T(8,128)(2,1)S(1)}, u32[]{:S(2)}, u32[]{:S(2)}) collective-permute-start(bf16[3,128,256]{2,1,0:T(8,128)(2,1)S(1)} %fusion.93), channel_id=1, source_target_pairs={{0,1},{1,0},{2,3},{3,2},{4,5},{5,4},{6,7},{7,6},{8,9},{9,8},{10,11... | collective-permute-start | bytes 589832 | tf_op jit(solution)/shard_map/ppermute | solution.py:17
  535.3 11.2 %collective-permute-start.31 = (bf16[3,128,256]{2,1,0:T(8,128)(2,1)S(1)}, bf16[3,128,256]{2,1,0:T(8,128)(2,1)S(1)}, u32[]{:S(2)}, u32[]{:S(2)}) collective-permute-start(bf16[3,128,256]{2,1,0:T(8,128)(2,1)S(1)} %fusion.91), channel_id=1, source_target_pairs={{0,1},{1,0},{2,3},{3,2},{4,5},{5,4},{6,7},{7,6},{8,9},{9,8},{10,11... | collective-permute-start | bytes 589832 | tf_op jit(solution)/shard_map/ppermute | solution.py:17
  542.6 10.3 %collective-permute-start.60 = (bf16[3,128,256]{2,1,0:T(8,128)(2,1)S(1)}, bf16[3,128,256]{2,1,0:T(8,128)(2,1)S(1)}, u32[]{:S(2)}, u32[]{:S(2)}) collective-permute-start(bf16[3,128,256]{2,1,0:T(8,128)(2,1)S(1)} %fusion.94), channel_id=1, source_target_pairs={{0,4},{4,0},{1,5},{5,1},{2,6},{6,2},{3,7},{7,3},{8,12},{12,8},{9,1... | collective-permute-start | bytes 589832 | tf_op jit(solution)/shard_map/ppermute | solution.py:17
  543.7 13.4 %collective-permute-start.12 = (bf16[3,128,256]{2,1,0:T(8,128)(2,1)S(1)}, bf16[3,128,256]{2,1,0:T(8,128)(2,1)S(1)}, u32[]{:S(2)}, u32[]{:S(2)}) collective-permute-start(bf16[3,128,256]{2,1,0:T(8,128)(2,1)S(1)} %get-tuple-element.83.refs_0_), channel_id=1, source_target_pairs={{0,4},{4,0},{1,5},{5,1},{2,6},{6,2},{3,7},{7,3},{8,12},{12,8},{9,1... | collective-permute-start | bytes 589832 | tf_op jit(solution)/shard_map/ppermute | solution.py:17
  546.5 14.8 %collective-permute-start.27 = (bf16[3,128,256]{2,1,0:T(8,128)(2,1)S(1)}, bf16[3,128,256]{2,1,0:T(8,128)(2,1)S(1)}, u32[]{:S(2)}, u32[]{:S(2)}) collective-permute-start(bf16[3,128,256]{2,1,0:T(8,128)(2,1)S(1)} %get-tuple-element.84.refs_8_), channel_id=1, source_target_pairs={{0,4},{4,0},{1,5},{5,1},{2,6},{6,2},{3,7},{7,3},{8,12},{12,8},{9,1... | collective-permute-start | bytes 589832 | tf_op jit(solution)/shard_map/ppermute | solution.py:17
  548.8 20.4 %collective-permute-start.37 = (bf16[4,128,256]{2,1,0:T(8,128)(2,1)S(1)}, bf16[4,128,256]{2,1,0:T(8,128)(2,1)S(1)}, u32[]{:S(2)}, u32[]{:S(2)}) collective-permute-start(bf16[4,128,256]{2,1,0:T(8,128)(2,1)S(1)} %fusion.84), channel_id=1, source_target_pairs={{0,4},{4,0},{1,5},{5,1},{2,6},{6,2},{3,7},{7,3},{8,12},{12,8},{9,1... | collective-permute-start | bytes 786440 | tf_op jit(solution)/shard_map/ppermute | solution.py:17
  549.0 22.2 %collective-permute-start.75 = (bf16[4,128,256]{2,1,0:T(8,128)(2,1)S(1)}, bf16[4,128,256]{2,1,0:T(8,128)(2,1)S(1)}, u32[]{:S(2)}, u32[]{:S(2)}) collective-permute-start(bf16[4,128,256]{2,1,0:T(8,128)(2,1)S(1)} %fusion.87), channel_id=1, source_target_pairs={{0,1},{1,0},{2,3},{3,2},{4,5},{5,4},{6,7},{7,6},{8,9},{9,8},{10,11... | collective-permute-start | bytes 786440 | tf_op jit(solution)/shard_map/ppermute | solution.py:17
  553.0 20.1 %collective-permute-start.70 = (bf16[4,128,256]{2,1,0:T(8,128)(2,1)S(1)}, bf16[4,128,256]{2,1,0:T(8,128)(2,1)S(1)}, u32[]{:S(2)}, u32[]{:S(2)}) collective-permute-start(bf16[4,128,256]{2,1,0:T(8,128)(2,1)S(1)} %fusion.86), channel_id=1, source_target_pairs={{0,4},{4,0},{1,5},{5,1},{2,6},{6,2},{3,7},{7,3},{8,12},{12,8},{9,1... | collective-permute-start | bytes 786440 | tf_op jit(solution)/shard_map/ppermute | solution.py:17
  557.2 16.0 %collective-permute-start.42 = (bf16[4,128,256]{2,1,0:T(8,128)(2,1)S(1)}, bf16[4,128,256]{2,1,0:T(8,128)(2,1)S(1)}, u32[]{:S(2)}, u32[]{:S(2)}) collective-permute-start(bf16[4,128,256]{2,1,0:T(8,128)(2,1)S(1)} %fusion.85), channel_id=1, source_target_pairs={{0,1},{1,0},{2,3},{3,2},{4,5},{5,4},{6,7},{7,6},{8,9},{9,8},{10,11... | collective-permute-start | bytes 786440 | tf_op jit(solution)/shard_map/ppermute | solution.py:17
  569.2 10.5 %collective-permute-start.17 = (bf16[3,128,256]{2,1,0:T(8,128)(2,1)S(1)}, bf16[3,128,256]{2,1,0:T(8,128)(2,1)S(1)}, u32[]{:S(2)}, u32[]{:S(2)}) collective-permute-start(bf16[3,128,256]{2,1,0:T(8,128)(2,1)S(1)} %get-tuple-element.81.refs_4_), channel_id=1, source_target_pairs={{0,1},{1,0},{2,3},{3,2},{4,5},{5,4},{6,7},{7,6},{8,9},{9,8},{10,11... | collective-permute-start | bytes 589832 | tf_op jit(solution)/shard_map/ppermute | solution.py:17
  571.1 14.4 %collective-permute-start.18 = (bf16[3,128,256]{2,1,0:T(8,128)(2,1)S(1)}, bf16[3,128,256]{2,1,0:T(8,128)(2,1)S(1)}, u32[]{:S(2)}, u32[]{:S(2)}) collective-permute-start(bf16[3,128,256]{2,1,0:T(8,128)(2,1)S(1)} %get-tuple-element.81.refs_4_), channel_id=1, source_target_pairs={{0,4},{4,0},{1,5},{5,1},{2,6},{6,2},{3,7},{7,3},{8,12},{12,8},{9,1... | collective-permute-start | bytes 589832 | tf_op jit(solution)/shard_map/ppermute | solution.py:17
  573.0 11.0 %collective-permute-start.32 = (bf16[3,128,256]{2,1,0:T(8,128)(2,1)S(1)}, bf16[3,128,256]{2,1,0:T(8,128)(2,1)}, u32[]{:S(2)}, u32[]{:S(2)}) collective-permute-start(bf16[3,128,256]{2,1,0:T(8,128)(2,1)S(1)} %get-tuple-element.82.refs_12_), channel_id=1, source_target_pairs={{0,1},{1,0},{2,3},{3,2},{4,5},{5,4},{6,7},{7,6},{8,9},{9,8},{10,11... | collective-permute-start | bytes 589832 | tf_op jit(solution)/shard_map/ppermute | solution.py:17
  573.1 12.9 %collective-permute-start.33 = (bf16[3,128,256]{2,1,0:T(8,128)(2,1)S(1)}, bf16[3,128,256]{2,1,0:T(8,128)(2,1)S(1)}, u32[]{:S(2)}, u32[]{:S(2)}) collective-permute-start(bf16[3,128,256]{2,1,0:T(8,128)(2,1)S(1)} %get-tuple-element.82.refs_12_), channel_id=1, source_target_pairs={{0,4},{4,0},{1,5},{5,1},{2,6},{6,2},{3,7},{7,3},{8,12},{12,8},{9,1... | collective-permute-start | bytes 589832 | tf_op jit(solution)/shard_map/ppermute | solution.py:17
  576.2 24.3 %collective-permute-start.38 = (bf16[4,128,256]{2,1,0:T(8,128)(2,1)S(1)}, bf16[4,128,256]{2,1,0:T(8,128)(2,1)S(1)}, u32[]{:S(2)}, u32[]{:S(2)}) collective-permute-start(bf16[4,128,256]{2,1,0:T(8,128)(2,1)S(1)} %get-tuple-element.94.refs_16_), channel_id=1, source_target_pairs={{0,4},{4,0},{1,5},{5,1},{2,6},{6,2},{3,7},{7,3},{8,12},{12,8},{9,1... | collective-permute-start | bytes 786440 | tf_op jit(solution)/shard_map/ppermute | solution.py:17
  579.7 21.2 %collective-permute-start.43 = (bf16[4,128,256]{2,1,0:T(8,128)(2,1)S(1)}, bf16[4,128,256]{2,1,0:T(8,128)(2,1)S(1)}, u32[]{:S(2)}, u32[]{:S(2)}) collective-permute-start(bf16[4,128,256]{2,1,0:T(8,128)(2,1)S(1)} %get-tuple-element.91.refs_20_), channel_id=1, source_target_pairs={{0,1},{1,0},{2,3},{3,2},{4,5},{5,4},{6,7},{7,6},{8,9},{9,8},{10,11... | collective-permute-start | bytes 786440 | tf_op jit(solution)/shard_map/ppermute | solution.py:17
  585.6 12.4 %collective-permute-start.29 = (bf16[3,128,256]{2,1,0:T(8,128)(2,1)S(1)}, bf16[3,128,256]{2,1,0:T(8,128)(2,1)S(1)}, u32[]{:S(2)}, u32[]{:S(2)}) collective-permute-start(bf16[3,128,256]{2,1,0:T(8,128)(2,1)S(1)} %collective-permute-done.27.refs_9_), channel_id=1, source_target_pairs={{0,1},{1,0},{2,3},{3,2},{4,5},{5,4},{6,7},{7,6},{8,9},{9,8},{10,11... | collective-permute-start | bytes 589832 | tf_op jit(solution)/shard_map/ppermute | solution.py:17
  586.1 15.5 %collective-permute-start.19 = (bf16[3,128,256]{2,1,0:T(8,128)(2,1)S(1)}, bf16[3,128,256]{2,1,0:T(8,128)(2,1)S(1)}, u32[]{:S(2)}, u32[]{:S(2)}) collective-permute-start(bf16[3,128,256]{2,1,0:T(8,128)(2,1)S(1)} %collective-permute-done.17.refs_5_), channel_id=1, source_target_pairs={{0,4},{4,0},{1,5},{5,1},{2,6},{6,2},{3,7},{7,3},{8,12},{12,8},{9,1... | collective-permute-start | bytes 589832 | tf_op jit(solution)/shard_map/ppermute | solution.py:17
  593.7 16.1 %collective-permute-start.39 = (bf16[4,128,256]{2,1,0:T(8,128)(2,1)S(1)}, bf16[4,128,256]{2,1,0:T(8,128)(2,1)S(1)}, u32[]{:S(2)}, u32[]{:S(2)}) collective-permute-start(bf16[4,128,256]{2,1,0:T(8,128)(2,1)S(1)} %get-tuple-element.94.refs_16_), channel_id=1, source_target_pairs={{0,1},{1,0},{2,3},{3,2},{4,5},{5,4},{6,7},{7,6},{8,9},{9,8},{10,11... | collective-permute-start | bytes 786440 | tf_op jit(solution)/shard_map/ppermute | solution.py:17
  597.9 11.9 %collective-permute-start.44 = (bf16[4,128,256]{2,1,0:T(8,128)(2,1)S(1)}, bf16[4,128,256]{2,1,0:T(8,128)(2,1)S(1)}, u32[]{:S(2)}, u32[]{:S(2)}) collective-permute-start(bf16[4,128,256]{2,1,0:T(8,128)(2,1)S(1)} %get-tuple-element.91.refs_20_), channel_id=1, source_target_pairs={{0,4},{4,0},{1,5},{5,1},{2,6},{6,2},{3,7},{7,3},{8,12},{12,8},{9,1... | collective-permute-start | bytes 786440 | tf_op jit(solution)/shard_map/ppermute | solution.py:17
  640.5 18.4 %collective-permute-start.46 = (bf16[1,2,2,64,768]{4,3,2,1,0:T(8,128)(2,1)S(1)}, bf16[1,2,2,64,768]{4,3,2,1,0:T(8,128)(2,1)S(1)}, u32[]{:S(2)}, u32[]{:S(2)}) collective-permute-start(bf16[1,2,2,64,768]{4,3,2,1,0:T(8,128)(2,1)S(1)} %get-tuple-element.65), channel_id=1, source_target_pairs={{0,1},{1,0},{2,3},{3,2},{4,5},{5,4},{6,7},{7,6},{8,9},{9,8},{10,11... | collective-permute-start | bytes 1179656 | tf_op jit(solution)/shard_map/ppermute | solution.py:17
  641.9 14.9 %collective-permute-start.56 = (bf16[3,128,256]{2,1,0:T(8,128)(2,1)S(1)}, bf16[3,128,256]{2,1,0:T(8,128)(2,1)S(1)}, u32[]{:S(2)}, u32[]{:S(2)}) collective-permute-start(bf16[3,128,256]{2,1,0:T(8,128)(2,1)S(1)} %get-tuple-element.74.refs_4_), channel_id=1, source_target_pairs={{0,1},{1,0},{2,3},{3,2},{4,5},{5,4},{6,7},{7,6},{8,9},{9,8},{10,11... | collective-permute-start | bytes 589832 | tf_op jit(solution)/shard_map/ppermute | solution.py:17
  642.6 29.1 %collective-permute-start.47 = (bf16[1,2,2,64,768]{4,3,2,1,0:T(8,128)(2,1)S(1)}, bf16[1,2,2,64,768]{4,3,2,1,0:T(8,128)(2,1)S(1)}, u32[]{:S(2)}, u32[]{:S(2)}) collective-permute-start(bf16[1,2,2,64,768]{4,3,2,1,0:T(8,128)(2,1)S(1)} %get-tuple-element.64), channel_id=1, source_target_pairs={{0,4},{4,0},{1,5},{5,1},{2,6},{6,2},{3,7},{7,3},{8,12},{12,8},{9,1... | collective-permute-start | bytes 1179656 | tf_op jit(solution)/shard_map/ppermute | solution.py:17
  644.6 16.8 %collective-permute-start.57 = (bf16[3,128,256]{2,1,0:T(8,128)(2,1)S(1)}, bf16[3,128,256]{2,1,0:T(8,128)(2,1)S(1)}, u32[]{:S(2)}, u32[]{:S(2)}) collective-permute-start(bf16[3,128,256]{2,1,0:T(8,128)(2,1)S(1)} %get-tuple-element.74.refs_4_), channel_id=1, source_target_pairs={{0,4},{4,0},{1,5},{5,1},{2,6},{6,2},{3,7},{7,3},{8,12},{12,8},{9,1... | collective-permute-start | bytes 589832 | tf_op jit(solution)/shard_map/ppermute | solution.py:17
  644.6 16.4 %collective-permute-start.66 = (bf16[3,128,256]{2,1,0:T(8,128)(2,1)S(1)}, bf16[3,128,256]{2,1,0:T(8,128)(2,1)}, u32[]{:S(2)}, u32[]{:S(2)}) collective-permute-start(bf16[3,128,256]{2,1,0:T(8,128)(2,1)S(1)} %get-tuple-element.73.refs_12_), channel_id=1, source_target_pairs={{0,1},{1,0},{2,3},{3,2},{4,5},{5,4},{6,7},{7,6},{8,9},{9,8},{10,11... | collective-permute-start | bytes 589832 | tf_op jit(solution)/shard_map/ppermute | solution.py:17
  656.7 11.9 %collective-permute-start.67 = (bf16[3,128,256]{2,1,0:T(8,128)(2,1)S(1)}, bf16[3,128,256]{2,1,0:T(8,128)(2,1)S(1)}, u32[]{:S(2)}, u32[]{:S(2)}) collective-permute-start(bf16[3,128,256]{2,1,0:T(8,128)(2,1)S(1)} %get-tuple-element.73.refs_12_), channel_id=1, source_target_pairs={{0,4},{4,0},{1,5},{5,1},{2,6},{6,2},{3,7},{7,3},{8,12},{12,8},{9,1... | collective-permute-start | bytes 589832 | tf_op jit(solution)/shard_map/ppermute | solution.py:17
  658.8 22.6 %collective-permute-start.48 = (bf16[1,2,2,64,768]{4,3,2,1,0:T(8,128)(2,1)S(1)}, bf16[1,2,2,64,768]{4,3,2,1,0:T(8,128)(2,1)S(1)}, u32[]{:S(2)}, u32[]{:S(2)}) collective-permute-start(bf16[1,2,2,64,768]{4,3,2,1,0:T(8,128)(2,1)S(1)} %get-tuple-element.63), channel_id=1, source_target_pairs={{0,5},{1,4},{4,1},{5,0},{2,7},{3,6},{6,3},{7,2},{8,13},{9,12},{12,... | collective-permute-start | bytes 1179656 | tf_op jit(solution)/shard_map/ppermute | solution.py:415
  661.0 12.8 %collective-permute-start.51 = (bf16[3,128,256]{2,1,0:T(8,128)(2,1)S(1)}, bf16[3,128,256]{2,1,0:T(8,128)(2,1)}, u32[]{:S(2)}, u32[]{:S(2)}) collective-permute-start(bf16[3,128,256]{2,1,0:T(8,128)(2,1)S(1)} %get-tuple-element.76.refs_0_), channel_id=1, source_target_pairs={{0,4},{4,0},{1,5},{5,1},{2,6},{6,2},{3,7},{7,3},{8,12},{12,8},{9,1... | collective-permute-start | bytes 589832 | tf_op jit(solution)/shard_map/ppermute | solution.py:17
  661.4 18.7 %collective-permute-start.52 = (bf16[3,128,256]{2,1,0:T(8,128)(2,1)S(1)}, bf16[3,128,256]{2,1,0:T(8,128)(2,1)S(1)}, u32[]{:S(2)}, u32[]{:S(2)}) collective-permute-start(bf16[3,128,256]{2,1,0:T(8,128)(2,1)S(1)} %get-tuple-element.76.refs_0_), channel_id=1, source_target_pairs={{0,1},{1,0},{2,3},{3,2},{4,5},{5,4},{6,7},{7,6},{8,9},{9,8},{10,11... | collective-permute-start | bytes 589832 | tf_op jit(solution)/shard_map/ppermute | solution.py:17
  673.8 13.1 %collective-permute-start.58 = (bf16[3,128,256]{2,1,0:T(8,128)(2,1)S(1)}, bf16[3,128,256]{2,1,0:T(8,128)(2,1)}, u32[]{:S(2)}, u32[]{:S(2)}) collective-permute-start(bf16[3,128,256]{2,1,0:T(8,128)(2,1)S(1)} %collective-permute-done.56.refs_5_), channel_id=1, source_target_pairs={{0,4},{4,0},{1,5},{5,1},{2,6},{6,2},{3,7},{7,3},{8,12},{12,8},{9,1... | collective-permute-start | bytes 589832 | tf_op jit(solution)/shard_map/ppermute | solution.py:17
  680.1 11.1 %collective-permute-start.53 = (bf16[3,128,256]{2,1,0:T(8,128)(2,1)}, bf16[3,128,256]{2,1,0:T(8,128)(2,1)}, u32[]{:S(2)}, u32[]{:S(2)}) collective-permute-start(bf16[3,128,256]{2,1,0:T(8,128)(2,1)} %collective-permute-done.51.refs_1_), channel_id=1, source_target_pairs={{0,1},{1,0},{2,3},{3,2},{4,5},{5,4},{6,7},{7,6},{8,9},{9,8},{10,11... | collective-permute-start | bytes 589832 | tf_op jit(solution)/shard_map/ppermute | solution.py:17
  683.1 59.2 %all-to-all-start = ((bf16[4,1,2,2,64,768]{5,4,3,2,1,0:T(8,128)(2,1)}), bf16[4,1,2,2,64,768]{5,4,3,2,1,0:T(8,128)(2,1)S(1)}, u32[]{:S(2)}, u32[]{:S(2)}) async-start(bf16[4,1,2,2,64,768]{5,4,3,2,1,0:T(8,128)(2,1)} %bitcast.54), calls=%async_computation | async-start | bytes 3145728 | tf_op jit(solution)/shard_map/all_to_all | solution.py:431
  686.9 11.5 %collective-permute-start.72 = (bf16[4,128,256]{2,1,0:T(8,128)(2,1)S(1)}, bf16[4,128,256]{2,1,0:T(8,128)(2,1)S(1)}, u32[]{:S(2)}, u32[]{:S(2)}) collective-permute-start(bf16[4,128,256]{2,1,0:T(8,128)(2,1)S(1)} %get-tuple-element.92.refs_16_), channel_id=1, source_target_pairs={{0,1},{1,0},{2,3},{3,2},{4,5},{5,4},{6,7},{7,6},{8,9},{9,8},{10,11... | collective-permute-start | bytes 786440 | tf_op jit(solution)/shard_map/ppermute | solution.py:17
  730.0 10.6 %collective-permute-start.80 = (bf16[1,2,2,64,768]{4,3,2,1,0:T(8,128)(2,1)S(1)}, bf16[1,2,2,64,768]{4,3,2,1,0:T(8,128)(2,1)S(1)}, u32[]{:S(2)}, u32[]{:S(2)}) collective-permute-start(bf16[1,2,2,64,768]{4,3,2,1,0:T(8,128)(2,1)S(1)} %get-tuple-element.67), channel_id=1, source_target_pairs={{0,4},{4,0},{1,5},{5,1},{2,6},{6,2},{3,7},{7,3},{8,12},{12,8},{9,1... | collective-permute-start | bytes 1179656 | tf_op jit(solution)/shard_map/ppermute | solution.py:17
  731.1 11.1 %collective-permute-start.81 = (bf16[1,2,2,64,768]{4,3,2,1,0:T(8,128)(2,1)S(1)}, bf16[1,2,2,64,768]{4,3,2,1,0:T(8,128)(2,1)S(1)}, u32[]{:S(2)}, u32[]{:S(2)}) collective-permute-start(bf16[1,2,2,64,768]{4,3,2,1,0:T(8,128)(2,1)S(1)} %get-tuple-element.66), channel_id=1, source_target_pairs={{0,5},{1,4},{4,1},{5,0},{2,7},{3,6},{6,3},{7,2},{8,13},{9,12},{12,... | collective-permute-start | bytes 1179656 | tf_op jit(solution)/shard_map/ppermute | solution.py:415
  (97 other events, 1745.5 us)
Sparse Core Ops, SparseCore 0:
  29.3 55.0 all-gather.5
  86.0 75.1 all-gather.7
  162.7 74.9 all-gather.9
  239.1 74.9 all-gather.11
  315.6 74.9 all-gather.13

commit v2 on v1

v2 whole, which is shorter than its diff:
```python
import functools

import jax
import jax.numpy as jnp
from jax import lax
from jax.experimental import pallas as pl
from jax.experimental.pallas import tpu as pltpu
from jax.sharding import Mesh, PartitionSpec as P

BF = jnp.bfloat16
F32 = jnp.float32
VMEM = 56 * 1024 * 1024
NT = (((1,), (1,)), ((), ()))


def swap(value, axis):
    return lax.ppermute(value, axis, [(0, 1), (1, 0)])


def tile_of(width):
    return 256 if width % 256 == 0 else width


def cost(flops, nbytes):
    return pl.CostEstimate(flops=int(flops), bytes_accessed=int(nbytes), transcendentals=0)


def call(kernel, prefetch, operands, grid, in_specs, out_specs, out_shape, scratch, estimate, name):
    return pl.pallas_call(
        kernel,
        grid_spec=pltpu.PrefetchScalarGridSpec(
            num_scalar_prefetch=1,
            grid=grid,
            in_specs=in_specs,
            out_specs=out_specs,
            scratch_shapes=scratch,
        ),
        out_shape=out_shape,
        compiler_params=pltpu.CompilerParams(vmem_limit_bytes=VMEM),
        cost_estimate=estimate,
        name=name,
    )(prefetch, *operands)


def fit(pieces, owners, metric, half):
    rows, depth = pieces[0].shape
    block, total = metric.shape
    width = block // 2
    tile = tile_of(width)
    steps = width // tile
    count = len(pieces)

    def kernel(index, *refs):
        held, metric_ref, out = refs[:count], refs[count], refs[count + 1]
        acc = None
        for at in range(count):
            columns = pl.ds(pl.multiple_of(index[1 + at] * depth, 128), depth)
            term = lax.dot_general(
                held[at][...], metric_ref[:, columns], NT, preferred_element_type=F32
            )
            acc = term if acc is None else acc + term
        out[...] = acc.astype(BF)

    return call(
        kernel,
        jnp.concatenate([jnp.reshape(half, (1,)), owners]).astype(jnp.int32),
        (*pieces, metric),
        (steps,),
        [pl.BlockSpec((rows, depth), lambda t, index: (0, 0))] * count
        + [pl.BlockSpec((tile, total), lambda t, index: (index[0] * steps + t, 0))],
        pl.BlockSpec((rows, tile), lambda t, index: (0, t)),
        jax.ShapeDtypeStruct((rows, width), BF),
        [],
        cost(2 * rows * total * width, 2 * (rows * total + width * total + rows * width)),
        "fit",
    )


def coulomb(own, sib, pairs, flips, blocks, bw, a_block, rows, segments):
    orbitals = sorted(own)
    n_virt, width = own[orbitals[0]].shape
    count = blocks.shape[0]
    n_orb, n_pairs = len(orbitals), len(pairs)
    n_seg = len(segments)
    mixed = [pair for pair in pairs if pair[0] != pair[1]]

    def kernel(index, *refs):
        left = [refs[at * n_orb : (at + 1) * n_orb] for at in range(2)]
        right = [refs[(2 + at) * n_orb : (3 + at) * n_orb] for at in range(2)]
        outs = refs[4 * n_orb : 4 * n_orb + n_seg]
        acc = refs[4 * n_orb + n_seg]
        step = pl.program_id(0)

        def product(first, second):
            total = None
            for side in range(2):
                term = lax.dot_general(
                    left[side][orbitals.index(first)][...],
                    right[side][orbitals.index(second)][...],
                    NT,
                    preferred_element_type=F32,
                )
                total = term if total is None else total + term
            return total.astype(BF)

        for at, (i, j) in enumerate(pairs):
            if i == j:
                acc[at] = product(i, j)
            else:
                flip = index[1 + count + mixed.index((i, j))]

                @pl.when(flip == 0)
                def _(at=at, i=i, j=j):
                    acc[at] = product(i, j)

                @pl.when(flip != 0)
                def _(at=at, i=i, j=j):
                    acc[at] = product(j, i)

        start = 0
        for seg, length in enumerate(segments):

            @pl.when((step >= start) & (step < start + length))
            def _(seg=seg):
                outs[seg][0] = acc[...]

            start += length

    starts = [sum(segments[:at]) for at in range(n_seg)]
    out_specs = [
        pl.BlockSpec(
            (1, n_pairs, rows, bw),
            lambda t, index, start=start, length=length: (
                jnp.clip(t - start, 0, length - 1),
                0,
                0,
                0,
            ),
        )
        for start, length in zip(starts, segments)
    ]
    out_shape = [
        jax.ShapeDtypeStruct((length, n_pairs, rows, bw), BF) for length in segments
    ]
    arrays = [own[o] for o in orbitals] + [sib[o] for o in orbitals]
    index = jnp.concatenate(
        [jnp.reshape(a_block, (1,)), blocks]
        + [jnp.reshape(flips[pair], (1,)) for pair in mixed]
    ).astype(jnp.int32)
    return call(
        kernel,
        index,
        (*arrays, *arrays),
        (count,),
        [pl.BlockSpec((rows, width), lambda t, index: (index[0], 0))] * (2 * n_orb)
        + [pl.BlockSpec((bw, width), lambda t, index: (index[1 + t], 0))] * (2 * n_orb),
        out_specs,
        out_shape,
        [pltpu.VMEM((n_pairs, rows, bw), BF)],
        cost(
            0.4 * n_pairs * rows * count * bw * width,
            0.4 * n_orb * count * bw * width + 0.2 * n_pairs * rows * count * bw,
        ),
        "coulomb",
    )


def contract(groups, own, sib, flips, blocks, core, n_v, first, steps):
    n_orb = len(own)
    n_virt, width = own[0].shape
    count = blocks.shape[0]
    bw = n_virt // count
    tile = tile_of(width)
    pairs = [pair for group, _ in groups for pair in group]
    mixed = [pair for pair in pairs if pair[0] != pair[1]]
    pieces = [piece for _, held in groups for piece in held]
    rows = pieces[0].shape[1]
    sub = rows // n_v
    half_orb = n_orb // 2

    def kernel(index, *refs):
        held = refs[: len(pieces)]
        sides = [
            refs[len(pieces) + side * n_orb : len(pieces) + (side + 1) * n_orb]
            for side in range(2)
        ]
        out, amp, acc = refs[len(pieces) + 2 * n_orb :]
        step = pl.program_id(0)

        @pl.when(step == 0)
        def _():
            base = at = 0
            for group, _ in groups:
                for block in range(count):
                    columns = pl.ds(pl.multiple_of(index[1 + block] * bw, 128), bw)
                    amp[base : base + len(group), :, columns] = held[at][...]
                    at += 1
                base += len(group)

        for side in range(2):

            @pl.when((step >= side * steps) & (step < (side + 1) * steps))
            def _(side=side):
                def product(p, j):
                    return jnp.dot(amp[p], sides[side][j][...], preferred_element_type=F32)

                for p, (i, j) in enumerate(pairs):
                    if i == j:
                        acc[i] = product(p, i)
                for p, (i, j) in enumerate(pairs):
                    if i != j:
                        flip = index[1 + count + mixed.index((i, j))]

                        @pl.when(flip == 0)
                        def _(p=p, i=i, j=j):
                            acc[i] += product(p, j)

                        @pl.when(flip != 0)
                        def _(p=p, i=i, j=j):
                            acc[j] += product(p, i)

        for i in range(n_orb):
            for v in range(n_v):
                value = acc[i, v * sub : (v + 1) * sub, :]
                out[v, i // half_orb, 0, i % half_orb] = value.astype(BF)

    index = jnp.concatenate(
        [jnp.reshape(core, (1,)), blocks] + [jnp.reshape(flips[pair], (1,)) for pair in mixed]
    ).astype(jnp.int32)

    def place(t, index):
        second = (t >= steps).astype(jnp.int32)
        return (0, 0, (index[0] + second) % 2, 0, 0, t - second * steps)

    return call(
        kernel,
        index,
        (*pieces, *[own[o] for o in range(n_orb)], *[sib[o] for o in range(n_orb)]),
        (2 * steps,),
        [
            pl.BlockSpec(
                piece.shape, lambda t, index: (0, 0, 0), pipeline_mode=pl.Buffered(1)
            )
            for piece in pieces
        ]
        + [
            pl.BlockSpec(
                (n_virt, tile), lambda t, index: (0, first + jnp.minimum(t, steps - 1))
            )
        ]
        * n_orb
        + [pl.BlockSpec((n_virt, tile), lambda t, index: (0, first + jnp.maximum(t - steps, 0)))]
        * n_orb,
        pl.BlockSpec((n_v, 2, 1, half_orb, sub, tile), place),
        jax.ShapeDtypeStruct((n_v, 2, 2, half_orb, sub, steps * tile), BF),
        [
            pltpu.VMEM((len(pairs), rows, n_virt), BF),
            pltpu.VMEM((n_orb, rows, tile), F32),
        ],
        cost(
            4 * len(pairs) * rows * n_virt * steps * tile,
            4 * n_orb * n_virt * steps * tile + 2 * len(pairs) * rows * n_virt,
        ),
        "contract",
    )


def finish(parts):
    n_z, m, n_x, n_i, rows, _ = parts[0].shape
    width = sum(part.shape[-1] for part in parts)
    if width % 128 or rows % 8:
        out = jnp.concatenate(parts, axis=-1).transpose(0, 4, 3, 1, 2, 5)
        return out.astype(F32).reshape(n_z * rows, n_i, m * n_x * width)

    def kernel(*refs):
        out = refs[-1]
        for mm in range(m):
            for xx in range(n_x):
                at = (mm * n_x + xx) * width
                for ref in refs[:-1]:
                    wide = ref.shape[-1]
                    for i in range(n_i):
                        out[:, i, at : at + wide] = ref[0, mm, xx, i].astype(F32)
                    at += wide

    return pl.pallas_call(
        kernel,
        grid=(n_z,),
        in_specs=[
            pl.BlockSpec((1,) + part.shape[1:], lambda z: (z, 0, 0, 0, 0, 0)) for part in parts
        ],
        out_specs=pl.BlockSpec((rows, n_i, m * n_x * width), lambda z: (z, 0, 0)),
        out_shape=jax.ShapeDtypeStruct((n_z * rows, n_i, m * n_x * width), F32),
        compiler_params=pltpu.CompilerParams(vmem_limit_bytes=VMEM),
        name="finish",
    )(*parts)


def after(value, *others):
    return lax.optimization_barrier((value, *others))[0]


def local(pair_list, half_ints, vir_coef, metric, occ_energy, vir_energy):
    n_z, n_v = lax.axis_size("z"), lax.axis_size("v")
    z, v, c, x = (lax.axis_index(name) for name in "zvcx")
    mu_rows, occ_rows, aux = half_ints.shape
    n_virt = vir_coef.shape[1]
    n_orb = 2 * occ_rows
    paired = n_v == 2
    a_rows = n_virt // (2 * n_z)
    sub = a_rows // n_v

    def order(value, axis=0):
        shape = value.shape
        split = value.reshape(shape[:axis] + (n_v, 2, n_z, sub) + shape[axis + 1 :])
        perm = [axis + 2, axis + 1, axis, axis + 3]
        rest = list(range(axis + 4, split.ndim))
        return split.transpose(list(range(axis)) + perm + rest).reshape(shape)

    listed = jnp.concatenate([pair_list, swap(pair_list, "x")])
    flips = {
        (i, j): jnp.any((listed[:, 0] == j) & (listed[:, 1] == i)).astype(jnp.int32)
        for i in range(n_orb)
        for j in range(i + 1, n_orb)
    }

    if paired:
        owners = jnp.stack([v * 2 + c, v * 2 + 1 - c, (1 - v) * 2 + c, (1 - v) * 2 + 1 - c])
    else:
        owners = jnp.arange(2 * n_v)

    def spread(block):
        if paired:
            far = swap(block, "v")
            return [block, swap(block, "c")], far, lambda value: [value, swap(value, "c")]
        gathered = lax.all_gather(block, ("v", "c"))
        return [], gathered, lambda value: [value[s] for s in range(2 * n_v)]

    def gather_z(value, axis=0):
        return lax.all_gather(value, "z", axis=axis, tiled=True)

    part_rows = n_virt // (4 * n_v)
    if paired and part_rows == n_v * sub:
        spot = (c * 2 + v) * 2 + x
        strip = n_virt // (2 * n_v)
        piece = jnp.concatenate(
            [
                lax.dynamic_slice_in_dim(
                    vir_coef, (w * 2 + spot % 2) * strip + spot // 2 * sub, sub, axis=1
                )
                for w in range(n_v)
            ],
            axis=1,
        ).T
        early = piece.reshape(1, part_rows, mu_rows)
        piece = gather_z(early, 2)

        def join(value, axis, low, *others):
            other = after(swap(value, axis), *others)
            return jnp.concatenate(
                [jnp.where(low, value, other), jnp.where(low, other, value)], axis=0
            )

        def coefficients(when):
            held = join(after(piece, *when[0]), "x", x == 0, *when[1])
            held = join(after(held, *when[2]), "v", v == 0, *when[3])
            return join(held, "c", c == 0).reshape(n_virt, mu_rows * n_z)
    else:
        early = vir_coef

        def coefficients(when):
            turned = order(vir_coef.T)
            held = lax.dynamic_slice_in_dim(turned, ((c * n_v + v) * 2 + x) * part_rows, part_rows)
            held = lax.all_gather(gather_z(held, 1), "x", axis=0, tiled=True)
            held = lax.all_gather(held, "v", axis=0, tiled=True)
            return lax.all_gather(held, "c", axis=0, tiled=True)

    own, sib = {}, {}

    def transform(orbital, held, *others):
        own[orbital] = jnp.dot(coef, held, preferred_element_type=F32).astype(BF)
        sib[orbital] = swap(after(own[orbital], *others), "c")

    energies = order(vir_energy)
    a_block = z * 2 + c
    if paired:
        sent, held = (
            jnp.stack(
                [
                    h * 4 + ((x ^ r1) * 2 + (v ^ r2) if h == 0 else (x ^ r2) * 2 + (v ^ r1))
                    for h in range(2)
                    for r2 in range(2)
                ]
            )
            for r1 in (1, 0)
        )
        blocks = jnp.concatenate([held[:2], sent[:2], held[2:], sent[2:]])
    else:
        blocks = jnp.arange(2 * n_v)
    bw = n_virt // blocks.shape[0]

    def amplitude(total, pairs, block):
        a = lax.dynamic_slice_in_dim(energies, a_block * a_rows, a_rows)
        b = lax.dynamic_slice_in_dim(energies, block * bw, bw)
        occ = jnp.stack([occ_energy[i] + occ_energy[j] for i, j in pairs])
        denom = (a[None, :, None] + b[None, None, :]) - occ[:, None, None]
        return (-total / denom).astype(BF)

    groups = []

    def group(pairs, others=()):
        part = functools.partial(coulomb, own, sib, pairs, flips)
        if not paired:
            (total,) = part(blocks, bw, a_block, a_rows, [2 * n_v])
            total = lax.psum_scatter(total.astype(F32), "v", scatter_dimension=0, tiled=True)
            total = lax.psum_scatter(total, "x", scatter_dimension=0, tiled=True)
            piece = lax.all_gather(amplitude(total[0], pairs, v * 2 + x), "x")
            piece = lax.all_gather(piece, "v", axis=0, tiled=True)
            groups.append((pairs, [piece[s] for s in range(2 * n_v)]))
            return [total], [total]
        ways = (("x", "v"), ("v", "x"))
        away = part(sent, bw, a_block, a_rows, [2, 2])
        firsts = [swap(after(away[h], *others), ways[h][0]).astype(F32) for h in range(2)]
        last = {o: after(value, *away) for o, value in own.items()}
        keep = coulomb(last, sib, pairs, flips, held, bw, a_block, a_rows, [2, 2])
        keep = [value.astype(F32) for value in keep]
        seconds = [swap((keep[h][1] + firsts[h][1]).astype(BF), ways[h][1]) for h in range(2)]
        totals = [keep[h][0] + firsts[h][0] + seconds[h].astype(F32) for h in range(2)]
        made = [amplitude(totals[h], pairs, h * 4 + x * 2 + v) for h in range(2)]
        pieces, nears = [], []
        for h in range(2):
            near = swap(made[h], ways[h][1])
            nears.append(near)
            pieces += [made[h], near, swap(made[h], ways[h][0]), swap(near, ways[h][0])]
        groups.append((pairs, pieces))
        return made, nears

    cut = mu_rows // 2
    block = half_ints[:, 0, :]
    near, far, widen = spread(block[:cut])
    near = near + widen(after(far, early))
    mine = [fit(near, owners, metric, x)]
    moved = [fit(near, owners, metric, 1 - x)]
    near, far, widen = spread(after(block[cut:], far))
    near = near + widen(after(far, *mine, *moved))
    mine.append(fit(near, owners, metric, x))
    moved.append(fit(near, owners, metric, 1 - x))
    later = []
    for at in range(1, occ_rows):
        near, far, widen = spread(after(half_ints, far)[:, at, :])
        later.append((near, far, widen, mine[-1], moved[-1]))
    moved = swap(jnp.concatenate(moved), "x")
    shared = jnp.concatenate(
        [gather_z(part).reshape(n_z, cut, -1) for part in mine], axis=1
    ).reshape(mu_rows * n_z, -1)
    following, marks, ready = {}, [], []
    for at in range(1, occ_rows):
        near, far, widen, *others = later[at - 1]
        near = near + widen(after(far, *others))
        here, away = fit(near, owners, metric, x), fit(near, owners, metric, 1 - x)
        marks += [here, away]
        away = swap(after(away, moved), "x")
        chosen = [jnp.where(x == 0, here, away), jnp.where(x == 0, away, here)]
        ready += chosen
        following[at] = [gather_z(value) for value in chosen]
    coef = coefficients((mine[:1], mine[1:], [far], marks))
    moved = gather_z(moved)
    moved = after(moved, *ready)
    transform(0, jnp.where(x == 0, shared, moved))
    transform(occ_rows, jnp.where(x == 0, moved, shared))
    made, nears = group([(0, 0), (0, occ_rows), (occ_rows, occ_rows)])
    for at in range(1, occ_rows):
        for orbital, value in zip((at, at + occ_rows), following[at]):
            seen = list(own)
            transform(orbital, after(value, *made), *nears)
            made, nears = group(
                [tuple(sorted((s, orbital))) for s in seen] + [(orbital, orbital)],
                groups[-1][1],
            )

    def exchange(value, *others):
        if not paired:
            value = lax.all_to_all(value, "v", 0, 0, tiled=True)
            value = lax.all_to_all(value, "x", 1, 1, tiled=True)
            return value.transpose(0, 2, 1, 3, 4, 5)

        def take(row, column):
            return lax.dynamic_slice(value, (row, column, 0, 0, 0, 0), (1, 1) + value.shape[2:])[0]

        parts = (
            (take(v, x), v, x),
            (swap(take(v, 1 - x), "x"), v, 1 - x),
            (swap(take(1 - v, x), "v"), 1 - v, x),
            (lax.ppermute(take(1 - v, 1 - x), ("v", "x"), [(k, 3 - k) for k in range(4)]), 1 - v, 1 - x),
        )
        whole = jnp.zeros((2, 2, 2) + value.shape[3:], BF)
        for part, row, column in parts:
            part = after(part, *others)
            whole = lax.dynamic_update_slice(
                whole, part.transpose(1, 0, 2, 3, 4)[None], (row, 0, column, 0, 0, 0)
            )
        return whole

    made, base = [], own
    for at in range(own[0].shape[1] // tile_of(own[0].shape[1])):
        made.append(contract(groups, base, sib, flips, blocks, c, n_v, at, 1))
        base = {o: after(array, made[-1]) for o, array in base.items()}
    results = []
    for at, value in enumerate(made):
        value = exchange(value, *made[at + 1 : at + 2])
        value = value.reshape((n_z, 2 * n_v // n_z) + value.shape[2:])
        value = after(value, *results[-1:])
        results.append(lax.all_to_all(value, "z", 0, 0, tiled=True))
    return finish(results)


def solution(mesh):
    n_ao, n_vir, n_occ = (mesh.shape[name] for name in ("ao", "vir", "occ"))
    fine = Mesh(mesh.devices.reshape(n_ao, n_vir // 2, 2, n_occ), ("z", "v", "c", "x"))
    vir = ("v", "c")
    return jax.shard_map(
        local,
        mesh=fine,
        in_specs=(P("x", None), P("z", "x", vir), P("z", None), P(vir, None), P(), P()),
        out_specs=P(vir, "x", "z"),
        check_vma=False,
    )
```

time: 806 us -> 623 us (0.77)
  waiting for transfers between devices: 343 us -> 186 us
  local copies, waits for them, and re-layouts: 78.2 us -> 26.2 us
  other arithmetic: 13.4 us -> 46.3 us
  Pallas kernels: 159 us -> 184 us
  starting transfers between devices: 93.8 us -> 70.8 us
    ppermute x80 -> x55, waiting for transfers between devices: 273 us -> 164 us  [swap(): return lax.ppermute(value, axis, [(0, 1), (1, 0)])]
    all_gather x5 -> x6, waiting for transfers between devices: 68.3 us -> 11.7 us  [gather_z(): return lax.all_gather(value, 'z', axis=axis, tiled=True)]
    ppermute x80 -> x55, starting transfers between devices: 87.8 us -> 56.8 us  [swap(): return lax.ppermute(value, axis, [(0, 1), (1, 0)])]
    pallas_call x9 -> x15, Pallas kernels: 159 us -> 178 us  [call(): pl.pallas_call(kernel, grid_spec=pltpu.PrefetchScalarGridSpec(num_scalar_...]
    reshape x4 -> x0, local copies, waits for them, and re-layouts: 18.1 us -> none  [the longest x2 17.9 us: local(): return out.astype(F32).reshape(n_virt // (2 * n_v), occ_rows, -1)]
    select_n x1 -> x5, other arithmetic: 2.6 us -> 16.9 us  [the longest x3 8.24 us: join(): jnp.where(low, value, other)]
    dynamic_update_slice x12, local copies, waits for them, and re-layouts: 17.3 us -> 3.15 us  [exchange(): lax.dynamic_update_slice(whole, part.transpose(1, 0, 2, 3, 4)[None], (row...]
    concatenate x0 -> x5, other arithmetic: none -> 11.2 us  [the longest x3 5.86 us: join(): jnp.concatenate([jnp.where(low, value, other), jnp.where(low, other, valu...]
  transfers between devices with their start and end apart: 88 -> 66, of which waited for: 39 -> 29; matrix products, arithmetic and copies ran while one was open for 13% -> 17% of each run, Pallas kernels for 17% -> 26%
where the time goes in v2:
time: 623 us; the launch traced here: 615 us
  waiting for transfers between devices  186 us (30%)
  Pallas kernels  184 us (30%)
  starting transfers between devices  70.8 us (11%)
  other arithmetic  46.3 us (7%)
  matrix products  45.2 us (7%)
  between operations  31 us (5%)
  local copies, waits for them, and re-layouts  26.2 us (4%)
  blocking collectives  25.4 us (4%)
    pallas_call x15, Pallas kernels, call(): pl.pallas_call(kernel, grid_spec=pltpu.PrefetchScalarGridSpec(num_scalar_...  178 us
    ppermute x55, waiting for transfers between devices, swap(): return lax.ppermute(value, axis, [(0, 1), (1, 0)])  164 us
    ppermute x55, starting transfers between devices, swap(): return lax.ppermute(value, axis, [(0, 1), (1, 0)])  56.8 us
    dot_general x4, matrix products, transform(): own[orbital] = jnp.dot(coef, held, preferred_element_type=F32).astype(BF)  45.2 us
    all_to_all x1, blocking collectives, local(): results.append(lax.all_to_all(value, 'z', 0, 0, tiled=True))  25.4 us
  transfers between devices with their start and end apart: 66, of which 29 were waited for; matrix products, arithmetic and copies ran while one was open for 17% of the time, Pallas kernels for 26%

profile of v2, /device:TPU:0, one launch (start us, length us, event | category | flops | bytes accessed | tf_op | source)
XLA Modules:
  0.0 615.1 jit_solution(12268564703170468085)
XLA Ops:
  6.5 5.4 fusion.42
  12.1 3.0 collective-permute-start.2
  17.4 19.5 %collective-permute-done.2.refs_2_ = bf16[320,1536]{1,0:T(8,128)(2,1)S(1)} collective-permute-done((bf16[320,1536]{1,0:T(8,128)(2,1)S(1)}, bf16[320,1536]{1,0:T(8,128)(2,1)S(1)}, u32[]{:S(2)}, u32[]{:S(2)}) %collective-permute-start.2) | collective-permute-done | bytes 983072 | tf_op jit(solution)/shard_map/ppermute | solution.py:17
  36.9 2.0 copy.27
  39.0 1.8 collective-permute-start.6
  41.4 8.8 %fit.6 = bf16[320,768]{1,0:T(8,128)(2,1)} custom-call(s32[5]{0:T(128)} %concatenate.79.index, bf16[320,1536]{1,0:T(8,128)(2,1)} %bitcast.180, bf16[320,1536]{1,0:T(8,128)(2,1)} %collective-permute-done.1.refs_1_, bf16[320,1536]{1,0:T(8,128)(2,1)} %copy-done.29, bf16[320,1536]{1,0:T(8,128)(2,1)} %collective-permute-done.3.refs_3_, bf16[1536,6144]{1,0:T(8,128)(2,1)} %refs_4_.11), custom_call_target="tpu_custom_call" | custom-call | flops 3019898880 | bytes 13860864 | tf_op jit(solution)/shard_map/fit/pallas_call | solution.py:29
  50.3 12.7 %collective-permute-done.6.refs_2_ = bf16[320,1536]{1,0:T(8,128)(2,1)} collective-permute-done((bf16[320,1536]{1,0:T(8,128)(2,1)S(1)}, bf16[320,1536]{1,0:T(8,128)(2,1)}, u32[]{:S(2)}, u32[]{:S(2)}) %collective-permute-start.6) | collective-permute-done | bytes 983072 | tf_op jit(solution)/shard_map/ppermute | solution.py:17
  63.0 2.7 copy.19
  65.8 1.8 collective-permute-start.8
  68.3 8.9 %fit.7 = bf16[320,768]{1,0:T(8,128)(2,1)} custom-call(s32[5]{0:T(128)} %concatenate.80.index, bf16[320,1536]{1,0:T(8,128)(2,1)} %bitcast.181, bf16[320,1536]{1,0:T(8,128)(2,1)} %collective-permute-done.1.refs_1_, bf16[320,1536]{1,0:T(8,128)(2,1)} %copy-done.29, bf16[320,1536]{1,0:T(8,128)(2,1)} %collective-permute-done.3.refs_3_, bf16[1536,6144]{1,0:T(8,128)(2,1)} %refs_4_.11), custom_call_target="tpu_custom_call" | custom-call | flops 3019898880 | bytes 13860864 | tf_op jit(solution)/shard_map/fit/pallas_call | solution.py:29
  80.2 8.8 %fit.8 = bf16[320,768]{1,0:T(8,128)(2,1)} custom-call(s32[5]{0:T(128)} %concatenate.79.index, bf16[320,1536]{1,0:T(8,128)(2,1)} %bitcast.183, bf16[320,1536]{1,0:T(8,128)(2,1)} %collective-permute-done.5.refs_1_, bf16[320,1536]{1,0:T(8,128)(2,1)} %collective-permute-done.6.refs_2_, bf16[320,1536]{1,0:T(8,128)(2,1)} %collective-permute-done.7.refs_3_, ...), custom_call_target="tpu_custom_call" | custom-call | flops 3019898880 | bytes 13860864 | tf_op jit(solution)/shard_map/fit/pallas_call | solution.py:29
  89.1 8.9 %fit.9 = bf16[320,768]{1,0:T(8,128)(2,1)} custom-call(s32[5]{0:T(128)} %concatenate.80.index, bf16[320,1536]{1,0:T(8,128)(2,1)} %bitcast.184, bf16[320,1536]{1,0:T(8,128)(2,1)} %collective-permute-done.5.refs_1_, bf16[320,1536]{1,0:T(8,128)(2,1)} %collective-permute-done.6.refs_2_, bf16[320,1536]{1,0:T(8,128)(2,1)} %collective-permute-done.7.refs_3_, ...), custom_call_target="tpu_custom_call" | custom-call | flops 3019898880 | bytes 13860864 | tf_op jit(solution)/shard_map/fit/pallas_call | solution.py:29
  98.0 10.7 %collective-permute-done.4 = bf16[1,256,2560]{2,1,0:T(8,128)(2,1)} collective-permute-done((bf16[1,256,2560]{2,1,0:T(8,128)(2,1)}, bf16[1,256,2560]{2,1,0:T(8,128)(2,1)}, u32[]{:S(2)}, u32[]{:S(2)}) %collective-permute-start.4) | collective-permute-done | bytes 1310752 | tf_op jit(solution)/shard_map/ppermute | solution.py:17
  113.3 1.7 collective-permute-start.9
  117.6 22.6 %collective-permute-done.13 = bf16[640,768]{1,0:T(8,128)(2,1)S(1)} collective-permute-done((bf16[640,768]{1,0:T(8,128)(2,1)}, bf16[640,768]{1,0:T(8,128)(2,1)S(1)}, u32[]{:S(2)}, u32[]{:S(2)}) %collective-permute-start.13) | collective-permute-done | bytes 983072 | tf_op jit(solution)/shard_map/ppermute | solution.py:17
  141.4 12.4 %fit.11 = bf16[640,768]{1,0:T(8,128)(2,1)} custom-call(s32[5]{0:T(128)} %concatenate.80.index, bf16[640,1536]{1,0:T(8,128)(2,1)} %copy-done.5, bf16[640,1536]{1,0:T(8,128)(2,1)} %collective-permute-done.10.refs_1_, bf16[640,1536]{1,0:T(8,128)(2,1)} %collective-permute-done.8.refs_2_, bf16[640,1536]{1,0:T(8,128)(2,1)} %collective-permute-done.11.refs_3_, ...), custom_call_target="tpu_custom_call" | custom-call | flops 6039797760 | bytes 18284544 | tf_op jit(solution)/shard_map/fit/pallas_call | solution.py:29
  153.8 12.5 %fit.10 = bf16[640,768]{1,0:T(8,128)(2,1)} custom-call(s32[5]{0:T(128)} %concatenate.79.index, bf16[640,1536]{1,0:T(8,128)(2,1)} %copy-done.5, bf16[640,1536]{1,0:T(8,128)(2,1)} %collective-permute-done.10.refs_1_, bf16[640,1536]{1,0:T(8,128)(2,1)} %collective-permute-done.8.refs_2_, bf16[640,1536]{1,0:T(8,128)(2,1)} %collective-permute-done.11.refs_3_, ...), custom_call_target="tpu_custom_call" | custom-call | flops 6039797760 | bytes 18284544 | tf_op jit(solution)/shard_map/fit/pallas_call | solution.py:29
  166.3 6.6 %collective-permute-done.9 = bf16[2,256,2560]{2,1,0:T(8,128)(2,1)} collective-permute-done((bf16[2,256,2560]{2,1,0:T(8,128)(2,1)}, bf16[2,256,2560]{2,1,0:T(8,128)(2,1)}, u32[]{:S(2)}, u32[]{:S(2)}) %collective-permute-start.9) | collective-permute-done | bytes 2621472 | tf_op jit(solution)/shard_map/ppermute | solution.py:17
  172.9 2.9 broadcast_select_fusion.3
  175.8 3.2 pad_maximum_fusion.1
  180.7 4.4 pad_maximum_fusion.2
  185.1 18.4 %collective-permute-done.14 = bf16[640,768]{1,0:T(8,128)(2,1)} collective-permute-done((bf16[640,768]{1,0:T(8,128)(2,1)}, bf16[640,768]{1,0:T(8,128)(2,1)}, u32[]{:S(2)}, u32[]{:S(2)}) %collective-permute-start.14) | collective-permute-done | bytes 983072 | tf_op jit(solution)/shard_map/ppermute | solution.py:17
  203.5 2.7 broadcast_select_fusion.6
  206.3 11.7 %all-gather.12.cloned.1.call-done = bf16[2560,768]{1,0:T(8,128)(2,1)} async-done(((bf16[640,768]{1,0:T(8,128)(2,1)}), bf16[2560,768]{1,0:T(8,128)(2,1)}) %all-gather.12.cloned.1.call-update) | async-done | bytes 3932176 | tf_op jit(solution)/shard_map/all_gather | solution.py:340
  218.1 5.9 bitcast_select_fusion
  224.0 3.9 broadcast_select_fusion.1
  228.8 11.1 %convolution_convert_fusion.2.refs_1_.refs_5_.refs_2_.refs_8_.refs_10_.refs_26_ = bf16[2048,768]{1,0:T(8,128)(2,1)S(1)} fusion(bf16[2048,2560]{1,0:T(8,128)(2,1)S(1)} %bitcast.174, bf16[2560,768]{1,0:T(8,128)(2,1)} %get-tuple-element.129), kind=kOutput, calls=%fused_computation.9 | convolution fusion | flops 8054636544 | bytes 17563648 | tf_op jit(solution)/shard_map/dot_general | solution.py:381
  240.0 9.6 %convolution_convert_fusion.3.refs_0_.refs_4_.refs_6_.refs_8_.refs_24_ = bf16[2048,768]{1,0:T(8,128)(2,1)} fusion(bf16[2048,2560]{1,0:T(8,128)(2,1)S(1)} %bitcast.175, bf16[2560,768]{1,0:T(8,128)(2,1)S(1)} %get-tuple-element.130), kind=kOutput, calls=%fused_computation.10 | convolution fusion | flops 8054636544 | bytes 17563648 | tf_op jit(solution)/shard_map/dot_general | solution.py:381
  251.7 2.0 collective-permute-done
  255.8 8.9 %coulomb.6 = (bf16[2,3,256,256]{3,2,1,0:T(8,128)(2,1)}, bf16[2,3,256,256]{3,2,1,0:T(8,128)(2,1)}) custom-call(s32[6]{0:T(128)} %concatenate.86.index, bf16[2048,768]{1,0:T(8,128)(2,1)} %convolution_convert_fusion.3.refs_0_.refs_4_.refs_6_.refs_8_.refs_24_, bf16[2048,768]{1,0:T(8,128)(2,1)} %copy-done, ...), custom_call_target="tpu_custom_call" | custom-call | flops 241591904 | bytes 786432 | tf_op jit(solution)/shard_map/coulomb/pallas_call | solution.py:29
  264.8 1.9 collective-permute-start.17
  272.9 9.2 %coulomb.7 = (bf16[2,3,256,256]{3,2,1,0:T(8,128)(2,1)}, bf16[2,3,256,256]{3,2,1,0:T(8,128)(2,1)}) custom-call(s32[6]{0:T(128)} %concatenate.77.index, bf16[2048,768]{1,0:T(8,128)(2,1)} %convolution_convert_fusion.3.refs_0_.refs_4_.refs_6_.refs_8_.refs_24_, bf16[2048,768]{1,0:T(8,128)(2,1)} %copy-done, ...), custom_call_target="tpu_custom_call" | custom-call | flops 241591904 | bytes 786432 | tf_op jit(solution)/shard_map/coulomb/pallas_call | solution.py:29
  290.2 1.7 collective-permute-start.23
  293.6 3.3 collective-permute-done.18
  296.9 4.2 collective-permute-done.23
  301.0 3.3 fusion.33
  304.9 1.8 collective-permute-start.24
  306.7 12.4 %convolution_convert_fusion.1.refs_1_.refs_7_.refs_9_.refs_25_ = bf16[2048,768]{1,0:T(8,128)(2,1)S(1)} fusion(bf16[2048,2560]{1,0:T(8,128)(2,1)} %bitcast.176, bf16[2560,768]{1,0:T(8,128)(2,1)} %all-gather.14.cloned.1.call-done), kind=kOutput, calls=%fused_computation.8 | convolution fusion | flops 8054636544 | bytes 17563648 | tf_op jit(solution)/shard_map/dot_general | solution.py:381
  320.9 1.7 collective-permute-start.21
  325.4 9.9 %coulomb.8 = (bf16[2,3,256,256]{3,2,1,0:T(8,128)(2,1)}, bf16[2,3,256,256]{3,2,1,0:T(8,128)(2,1)}) custom-call(s32[7]{0:T(128)} %concatenate.88.index, bf16[2048,768]{1,0:T(8,128)(2,1)} %convolution_convert_fusion.3.refs_0_.refs_4_.refs_6_.refs_8_.refs_24_, bf16[2048,768]{1,0:T(8,128)(2,1)} %copy-done.1, bf16[2048,768]{1,0:T(8,128)(2,1)} %copy-done, ...), custom_call_target="tpu_custom_call" | custom-call | flops 241591904 | bytes 1101004 | tf_op jit(solution)/shard_map/coulomb/pallas_call | solution.py:29
  335.3 4.1 collective-permute-done.21.refs_3_
  343.0 10.4 %coulomb.9 = (bf16[2,3,256,256]{3,2,1,0:T(8,128)(2,1)}, bf16[2,3,256,256]{3,2,1,0:T(8,128)(2,1)}) custom-call(s32[7]{0:T(128)} %concatenate.87.index, bf16[2048,768]{1,0:T(8,128)(2,1)} %convolution_convert_fusion.3.refs_0_.refs_4_.refs_6_.refs_8_.refs_24_, bf16[2048,768]{1,0:T(8,128)(2,1)} %copy-done.1, bf16[2048,768]{1,0:T(8,128)(2,1)} %copy-done, ...), custom_call_target="tpu_custom_call" | custom-call | flops 241591904 | bytes 1101004 | tf_op jit(solution)/shard_map/coulomb/pallas_call | solution.py:29
  354.9 3.9 collective-permute-done.28
  365.9 3.1 collective-permute-done.29
  373.3 12.1 %convolution_convert_fusion.refs_3_.refs_11_.refs_27_ = bf16[2048,768]{1,0:T(8,128)(2,1)S(1)} fusion(bf16[2048,2560]{1,0:T(8,128)(2,1)} %bitcast.177, bf16[2560,768]{1,0:T(8,128)(2,1)} %all-gather.16.cloned.1.call-done), kind=kOutput, calls=%fused_computation.7 | convolution fusion | flops 8054636544 | bytes 17563648 | tf_op jit(solution)/shard_map/dot_general | solution.py:381
  392.0 12.7 %coulomb.10 = (bf16[2,4,256,256]{3,2,1,0:T(8,128)(2,1)}, bf16[2,4,256,256]{3,2,1,0:T(8,128)(2,1)}) custom-call(s32[8]{0:T(128)} %concatenate.90.index, bf16[2048,768]{1,0:T(8,128)(2,1)} %convolution_convert_fusion.3.refs_0_.refs_4_.refs_6_.refs_8_.refs_24_, bf16[2048,768]{1,0:T(8,128)(2,1)} %copy-done.1, bf16[2048,768]{1,0:T(8,128)(2,1)} %copy-done, ...), custom_call_target="tpu_custom_call" | custom-call | flops 322122560 | bytes 1468006 | tf_op jit(solution)/shard_map/coulomb/pallas_call | solution.py:29
  409.4 12.8 %coulomb.11 = (bf16[2,4,256,256]{3,2,1,0:T(8,128)(2,1)}, bf16[2,4,256,256]{3,2,1,0:T(8,128)(2,1)}) custom-call(s32[8]{0:T(128)} %concatenate.89.index, bf16[2048,768]{1,0:T(8,128)(2,1)} %convolution_convert_fusion.3.refs_0_.refs_4_.refs_6_.refs_8_.refs_24_, bf16[2048,768]{1,0:T(8,128)(2,1)} %copy-done.1, bf16[2048,768]{1,0:T(8,128)(2,1)} %copy-done, ...), custom_call_target="tpu_custom_call" | custom-call | flops 322122560 | bytes 1468006 | tf_op jit(solution)/shard_map/coulomb/pallas_call | solution.py:29
  424.0 7.2 %collective-permute-done.39 = bf16[2,4,256,256]{3,2,1,0:T(8,128)(2,1)S(1)} collective-permute-done((bf16[2,4,256,256]{3,2,1,0:T(8,128)(2,1)}, bf16[2,4,256,256]{3,2,1,0:T(8,128)(2,1)S(1)}, u32[]{:S(2)}, u32[]{:S(2)}) %collective-permute-start.39) | collective-permute-done | bytes 1048608 | tf_op jit(solution)/shard_map/ppermute | solution.py:17
  439.5 4.4 collective-permute-done.40
  450.3 10.8 %collective-permute-done.41.refs_17_ = bf16[4,256,256]{2,1,0:T(8,128)(2,1)S(1)} collective-permute-done((bf16[4,256,256]{2,1,0:T(8,128)(2,1)S(1)}, bf16[4,256,256]{2,1,0:T(8,128)(2,1)S(1)}, u32[]{:S(2)}, u32[]{:S(2)}) %collective-permute-start.41) | collective-permute-done | bytes 524320 | tf_op jit(solution)/shard_map/ppermute | solution.py:17
  463.7 9.2 %collective-permute-done.42.refs_18_ = bf16[4,256,256]{2,1,0:T(8,128)(2,1)S(1)} collective-permute-done((bf16[4,256,256]{2,1,0:T(8,128)(2,1)S(1)}, bf16[4,256,256]{2,1,0:T(8,128)(2,1)S(1)}, u32[]{:S(2)}, u32[]{:S(2)}) %collective-permute-start.42) | collective-permute-done | bytes 524320 | tf_op jit(solution)/shard_map/ppermute | solution.py:17
  472.9 7.2 %collective-permute-done.43.refs_19_ = bf16[4,256,256]{2,1,0:T(8,128)(2,1)} collective-permute-done((bf16[4,256,256]{2,1,0:T(8,128)(2,1)S(1)}, bf16[4,256,256]{2,1,0:T(8,128)(2,1)}, u32[]{:S(2)}, u32[]{:S(2)}) %collective-permute-start.43) | collective-permute-done | bytes 524320 | tf_op jit(solution)/shard_map/ppermute | solution.py:17
  480.2 18.0 %contract.3 = bf16[2,2,2,2,128,256]{5,4,3,2,1,0:T(8,128)(2,1)} custom-call(s32[15]{0:T(128)} %concatenate.76.index, bf16[3,256,256]{2,1,0:T(8,128)(2,1)} %get-tuple-element.167.refs_0_, bf16[3,256,256]{2,1,0:T(8,128)(2,1)} %collective-permute-done.19.refs_1_, bf16[3,256,256]{2,1,0:T(8,128)(2,1)} %collective-permute-done.20.refs_2_, ...), custom_call_target="tpu_custom_call" | custom-call | flops 5368709120 | bytes 18874368 | tf_op jit(solution)/shard_map/contract/pallas_call | solution.py:29
  499.5 1.8 collective-permute-start.51
  503.1 18.0 %contract.4 = bf16[2,2,2,2,128,256]{5,4,3,2,1,0:T(8,128)(2,1)} custom-call(s32[15]{0:T(128)} %concatenate.76.index, bf16[3,256,256]{2,1,0:T(8,128)(2,1)} %get-tuple-element.167.refs_0_, bf16[3,256,256]{2,1,0:T(8,128)(2,1)} %collective-permute-done.19.refs_1_, bf16[3,256,256]{2,1,0:T(8,128)(2,1)} %collective-permute-done.20.refs_2_, ...), custom_call_target="tpu_custom_call" | custom-call | flops 5368709120 | bytes 18874368 | tf_op jit(solution)/shard_map/contract/pallas_call | solution.py:29
  525.2 3.8 all-to-all-start
  529.0 1.8 collective-permute-start.54
  532.6 17.9 %contract.5 = bf16[2,2,2,2,128,256]{5,4,3,2,1,0:T(8,128)(2,1)} custom-call(s32[15]{0:T(128)} %concatenate.76.index, bf16[3,256,256]{2,1,0:T(8,128)(2,1)} %get-tuple-element.167.refs_0_, bf16[3,256,256]{2,1,0:T(8,128)(2,1)} %collective-permute-done.19.refs_1_, bf16[3,256,256]{2,1,0:T(8,128)(2,1)} %collective-permute-done.20.refs_2_, ...), custom_call_target="tpu_custom_call" | custom-call | flops 5368709120 | bytes 18874368 | tf_op jit(solution)/shard_map/contract/pallas_call | solution.py:29
  551.8 5.1 all-to-all-start.1
  560.7 2.7 collective-permute-done.55
  563.4 2.6 collective-permute-done.56
  567.2 9.5 %all-to-all-done.1.refs_1_ = bf16[4,1,2,2,128,256]{5,4,3,2,1,0:T(8,128)(2,1)S(1)} async-done(((bf16[4,1,2,2,128,256]{5,4,3,2,1,0:T(8,128)(2,1)}), bf16[4,1,2,2,128,256]{5,4,3,2,1,0:T(8,128)(2,1)S(1)}, u32[]{:S(2)}, u32[]{:S(2)}) %all-to-all-start.1) | async-done | bytes 1048608 | tf_op jit(solution)/shard_map/all_to_all | solution.py:513
  576.7 25.4 %all_to_all.15.refs_2_ = bf16[4,1,2,2,128,256]{5,4,3,2,1,0:T(8,128)(2,1)} all-to-all(bf16[4,1,2,2,128,256]{5,4,3,2,1,0:T(8,128)(2,1)S(1)} %bitcast.186), channel_id=1, replica_groups=mesh['z'=4,'v'=2,'c'=2,'x'=2] {'z'}, dimensions={0} | all-to-all | bytes 2097152 | tf_op jit(solution)/shard_map/all_to_all | solution.py:513
  602.1 5.7 finish.1
  (253 shorter events, 88.7 us)
Async XLA Ops:
  6.5 71.1 %all-gather.18.cloned.1.call-start = ((), (), s32[]{:S(2)}) async-start(), calls=%async_computation.8 | async-start | bytes 1638400 | tf_op jit(solution)/shard_map/all_gather | solution.py:340
  12.1 24.8 %collective-permute-start.2 = (bf16[320,1536]{1,0:T(8,128)(2,1)S(1)}, bf16[320,1536]{1,0:T(8,128)(2,1)S(1)}, u32[]{:S(2)}, u32[]{:S(2)}) collective-permute-start(bf16[320,1536]{1,0:T(8,128)(2,1)S(1)} %bitcast.178), channel_id=1, source_target_pairs={{0,4},{4,0},{1,5},{5,1},{2,6},{6,2},{3,7},{7,3},{8,12},{12,8},{9,1... | collective-permute-start | bytes 2949128 | tf_op jit(solution)/shard_map/ppermute | solution.py:17
  17.3 163.4 %all-gather.8.cloned.1.call-start = ((), (), s32[]{:S(2)}) async-start(), calls=%async_computation.3 | async-start | bytes 2457600 | tf_op jit(solution)/shard_map/all_gather | solution.py:340
  17.3 24.1 %collective-permute-start.1 = (bf16[320,1536]{1,0:T(8,128)(2,1)S(1)}, bf16[320,1536]{1,0:T(8,128)(2,1)}, u32[]{:S(2)}, u32[]{:S(2)}) collective-permute-start(bf16[320,1536]{1,0:T(8,128)(2,1)S(1)} %bitcast.179), channel_id=1, source_target_pairs={{0,2},{2,0},{1,3},{3,1},{4,6},{6,4},{5,7},{7,5},{8,10},{10,8},{9,1... | collective-permute-start | bytes 2949128 | tf_op jit(solution)/shard_map/ppermute | solution.py:17
  36.9 4.5 collective-permute-start.3
  39.0 24.0 %collective-permute-start.6 = (bf16[320,1536]{1,0:T(8,128)(2,1)S(1)}, bf16[320,1536]{1,0:T(8,128)(2,1)}, u32[]{:S(2)}, u32[]{:S(2)}) collective-permute-start(bf16[320,1536]{1,0:T(8,128)(2,1)S(1)} %bitcast.182), channel_id=1, source_target_pairs={{0,4},{4,0},{1,5},{5,1},{2,6},{6,2},{3,7},{7,3},{8,12},{12,8},{9,1... | collective-permute-start | bytes 2949128 | tf_op jit(solution)/shard_map/ppermute | solution.py:17
  50.2 130.5 %all-gather.10.cloned.1.call-start = ((), (), s32[]{:S(2)}) async-start(), calls=%async_computation.4 | async-start | bytes 2457600 | tf_op jit(solution)/shard_map/all_gather | solution.py:340
  65.8 44.2 %collective-permute-start.8 = (bf16[640,1536]{1,0:T(8,128)(2,1)S(1)}, bf16[640,1536]{1,0:T(8,128)(2,1)}, u32[]{:S(2)}, u32[]{:S(2)}) collective-permute-start(bf16[640,1536]{1,0:T(8,128)(2,1)S(1)} %slice_bitcast_fusion.refs_0_), channel_id=1, source_target_pairs={{0,4},{4,0},{1,5},{5,1},{2,6},{6,2},{3,7},{7,3},{8,12},{12,8},{9,1... | collective-permute-start | bytes 5898248 | tf_op jit(solution)/shard_map/ppermute | solution.py:17
  68.3 10.9 %collective-permute-start.5 = (bf16[320,1536]{1,0:T(8,128)(2,1)S(1)}, bf16[320,1536]{1,0:T(8,128)(2,1)}, u32[]{:S(2)}, u32[]{:S(2)}) collective-permute-start(bf16[320,1536]{1,0:T(8,128)(2,1)S(1)} %bitcast.185), channel_id=1, source_target_pairs={{0,2},{2,0},{1,3},{3,1},{4,6},{6,4},{5,7},{7,5},{8,10},{10,8},{9,1... | collective-permute-start | bytes 2949128 | tf_op jit(solution)/shard_map/ppermute | solution.py:17
  77.6 31.1 %collective-permute-start.4 = (bf16[1,256,2560]{2,1,0:T(8,128)(2,1)}, bf16[1,256,2560]{2,1,0:T(8,128)(2,1)}, u32[]{:S(2)}, u32[]{:S(2)}) collective-permute-start(bf16[1,256,2560]{2,1,0:T(8,128)(2,1)} %bitcast.190), channel_id=1, source_target_pairs={{0,1},{1,0},{2,3},{3,2},{4,5},{5,4},{6,7},{7,6},{8,9},{9,8},{10,11... | collective-permute-start | bytes 3932168 | tf_op jit(solution)/shard_map/ppermute | solution.py:17
  79.1 62.2 %collective-permute-start.10 = (bf16[640,1536]{1,0:T(8,128)(2,1)S(1)}, bf16[640,1536]{1,0:T(8,128)(2,1)}, u32[]{:S(2)}, u32[]{:S(2)}) collective-permute-start(bf16[640,1536]{1,0:T(8,128)(2,1)S(1)} %slice_bitcast_fusion.refs_0_), channel_id=1, source_target_pairs={{0,2},{2,0},{1,3},{3,1},{4,6},{6,4},{5,7},{7,5},{8,10},{10,8},{9,1... | collective-permute-start | bytes 5898248 | tf_op jit(solution)/shard_map/ppermute | solution.py:17
  89.0 129.0 %all-gather.12.cloned.1.call-start = ((), (), s32[]{:S(2)}) async-start(), calls=%async_computation.5 | async-start | bytes 4915200 | tf_op jit(solution)/shard_map/all_gather | solution.py:340
  110.1 31.3 %collective-permute-start.11 = (bf16[640,1536]{1,0:T(8,128)(2,1)}, bf16[640,1536]{1,0:T(8,128)(2,1)}, u32[]{:S(2)}, u32[]{:S(2)}) collective-permute-start(bf16[640,1536]{1,0:T(8,128)(2,1)} %collective-permute-done.8.refs_2_), channel_id=1, source_target_pairs={{0,2},{2,0},{1,3},{3,1},{4,6},{6,4},{5,7},{7,5},{8,10},{10,8},{9,1... | collective-permute-start | bytes 5898248 | tf_op jit(solution)/shard_map/ppermute | solution.py:17
  113.3 59.6 %collective-permute-start.9 = (bf16[2,256,2560]{2,1,0:T(8,128)(2,1)}, bf16[2,256,2560]{2,1,0:T(8,128)(2,1)}, u32[]{:S(2)}, u32[]{:S(2)}) collective-permute-start(bf16[2,256,2560]{2,1,0:T(8,128)(2,1)} %pad_maximum_fusion.3), channel_id=1, source_target_pairs={{0,4},{4,0},{1,5},{5,1},{2,6},{6,2},{3,7},{7,3},{8,12},{12,8},{9,1... | collective-permute-start | bytes 7864328 | tf_op jit(solution)/shard_map/ppermute | solution.py:17
  116.1 24.1 %collective-permute-start.13 = (bf16[640,768]{1,0:T(8,128)(2,1)}, bf16[640,768]{1,0:T(8,128)(2,1)S(1)}, u32[]{:S(2)}, u32[]{:S(2)}) collective-permute-start(bf16[640,768]{1,0:T(8,128)(2,1)} %pad_maximum_fusion.4), channel_id=1, source_target_pairs={{0,1},{1,0},{2,3},{3,2},{4,5},{5,4},{6,7},{7,6},{8,9},{9,8},{10,11... | collective-permute-start | bytes 2949128 | tf_op jit(solution)/shard_map/ppermute | solution.py:17
  141.2 165.5 %all-gather.14.cloned.1.call-start = ((), (), s32[]{:S(2)}) async-start(), calls=%async_computation.6 | async-start | bytes 4915200 | tf_op jit(solution)/shard_map/all_gather | solution.py:340
  179.0 44.9 %collective-permute-start.12 = (bf16[4,256,2560]{2,1,0:T(8,128)(2,1)}, bf16[4,256,2560]{2,1,0:T(8,128)(2,1)}, u32[]{:S(2)}, u32[]{:S(2)}) collective-permute-start(bf16[4,256,2560]{2,1,0:T(8,128)(2,1)} %pad_maximum_fusion.1), channel_id=1, source_target_pairs={{0,2},{2,0},{1,3},{3,1},{4,6},{6,4},{5,7},{7,5},{8,10},{10,8},{9,1... | collective-permute-start | bytes 15728648 | tf_op jit(solution)/shard_map/ppermute | solution.py:17
  179.0 24.5 %collective-permute-start.14 = (bf16[640,768]{1,0:T(8,128)(2,1)}, bf16[640,768]{1,0:T(8,128)(2,1)}, u32[]{:S(2)}, u32[]{:S(2)}) collective-permute-start(bf16[640,768]{1,0:T(8,128)(2,1)} %fit.11), channel_id=1, source_target_pairs={{0,1},{1,0},{2,3},{3,2},{4,5},{5,4},{6,7},{7,6},{8,9},{9,8},{10,11... | collective-permute-start | bytes 2949128 | tf_op jit(solution)/shard_map/ppermute | solution.py:17
  206.3 167.0 %all-gather.16.cloned.1.call-start = ((), (), s32[]{:S(2)}) async-start(), calls=%async_computation.7 | async-start | bytes 4915200 | tf_op jit(solution)/shard_map/all_gather | solution.py:340
  239.9 15.9 %collective-permute-start.16 = (bf16[2048,768]{1,0:T(8,128)(2,1)S(1)}, bf16[2048,768]{1,0:T(8,128)(2,1)}, u32[]{:S(2)}, u32[]{:S(2)}) collective-permute-start(bf16[2048,768]{1,0:T(8,128)(2,1)S(1)} %convolution_convert_fusion.2.refs_1_.refs_5_.refs_2_.refs_8_.refs_10_.refs_26_), channel_id=1, source_target_pairs={{0,2},{2,0},{1,3},{3,1},{4,6},{6,4},{5,7},{7,5},{8,10},{10,8},{9,1... | collective-permute-start | bytes 9437192 | tf_op jit(solution)/shard_map/ppermute | solution.py:17
  249.6 6.2 %collective-permute-start.15 = (bf16[2048,768]{1,0:T(8,128)(2,1)}, bf16[2048,768]{1,0:T(8,128)(2,1)}, u32[]{:S(2)}, u32[]{:S(2)}) collective-permute-start(bf16[2048,768]{1,0:T(8,128)(2,1)} %convolution_convert_fusion.3.refs_0_.refs_4_.refs_6_.refs_8_.refs_24_), channel_id=1, source_target_pairs={{0,2},{2,0},{1,3},{3,1},{4,6},{6,4},{5,7},{7,5},{8,10},{10,8},{9,1... | collective-permute-start | bytes 9437192 | tf_op jit(solution)/shard_map/ppermute | solution.py:17
  264.8 20.0 %collective-permute-start.17 = (bf16[2,3,256,256]{3,2,1,0:T(8,128)(2,1)}, bf16[2,3,256,256]{3,2,1,0:T(8,128)(2,1)}, u32[]{:S(2)}, u32[]{:S(2)}) collective-permute-start(bf16[2,3,256,256]{3,2,1,0:T(8,128)(2,1)} %get-tuple-element.74), channel_id=1, source_target_pairs={{0,1},{1,0},{2,3},{3,2},{4,5},{5,4},{6,7},{7,6},{8,9},{9,8},{10,11... | collective-permute-start | bytes 2359304 | tf_op jit(solution)/shard_map/ppermute | solution.py:17
  266.6 21.3 %collective-permute-start.22 = (bf16[2,3,256,256]{3,2,1,0:T(8,128)(2,1)}, bf16[2,3,256,256]{3,2,1,0:T(8,128)(2,1)}, u32[]{:S(2)}, u32[]{:S(2)}) collective-permute-start(bf16[2,3,256,256]{3,2,1,0:T(8,128)(2,1)} %get-tuple-element.75), channel_id=1, source_target_pairs={{0,4},{4,0},{1,5},{5,1},{2,6},{6,2},{3,7},{7,3},{8,12},{12,8},{9,1... | collective-permute-start | bytes 2359304 | tf_op jit(solution)/shard_map/ppermute | solution.py:17
  286.2 10.7 %collective-permute-start.18 = (bf16[3,256,256]{2,1,0:T(8,128)(2,1)S(1)}, bf16[3,256,256]{2,1,0:T(8,128)(2,1)}, u32[]{:S(2)}, u32[]{:S(2)}) collective-permute-start(bf16[3,256,256]{2,1,0:T(8,128)(2,1)S(1)} %fusion.38), channel_id=1, source_target_pairs={{0,4},{4,0},{1,5},{5,1},{2,6},{6,2},{3,7},{7,3},{8,12},{12,8},{9,1... | collective-permute-start | bytes 1179656 | tf_op jit(solution)/shard_map/ppermute | solution.py:17
  290.2 10.9 %collective-permute-start.23 = (bf16[3,256,256]{2,1,0:T(8,128)(2,1)}, bf16[3,256,256]{2,1,0:T(8,128)(2,1)}, u32[]{:S(2)}, u32[]{:S(2)}) collective-permute-start(bf16[3,256,256]{2,1,0:T(8,128)(2,1)} %fusion.39), channel_id=1, source_target_pairs={{0,1},{1,0},{2,3},{3,2},{4,5},{5,4},{6,7},{7,6},{8,9},{9,8},{10,11... | collective-permute-start | bytes 1179656 | tf_op jit(solution)/shard_map/ppermute | solution.py:17
  304.4 14.7 %collective-permute-start.19 = (bf16[3,256,256]{2,1,0:T(8,128)(2,1)}, bf16[3,256,256]{2,1,0:T(8,128)(2,1)}, u32[]{:S(2)}, u32[]{:S(2)}) collective-permute-start(bf16[3,256,256]{2,1,0:T(8,128)(2,1)} %get-tuple-element.167.refs_0_), channel_id=1, source_target_pairs={{0,4},{4,0},{1,5},{5,1},{2,6},{6,2},{3,7},{7,3},{8,12},{12,8},{9,1... | collective-permute-start | bytes 1179656 | tf_op jit(solution)/shard_map/ppermute | solution.py:17
  304.9 14.2 %collective-permute-start.24 = (bf16[3,256,256]{2,1,0:T(8,128)(2,1)S(1)}, bf16[3,256,256]{2,1,0:T(8,128)(2,1)}, u32[]{:S(2)}, u32[]{:S(2)}) collective-permute-start(bf16[3,256,256]{2,1,0:T(8,128)(2,1)S(1)} %get-tuple-element.166.refs_4_), channel_id=1, source_target_pairs={{0,1},{1,0},{2,3},{3,2},{4,5},{5,4},{6,7},{7,6},{8,9},{9,8},{10,11... | collective-permute-start | bytes 1179656 | tf_op jit(solution)/shard_map/ppermute | solution.py:17
  319.1 6.3 %collective-permute-start.27 = (bf16[2048,768]{1,0:T(8,128)(2,1)S(1)}, bf16[2048,768]{1,0:T(8,128)(2,1)}, u32[]{:S(2)}, u32[]{:S(2)}) collective-permute-start(bf16[2048,768]{1,0:T(8,128)(2,1)S(1)} %convolution_convert_fusion.1.refs_1_.refs_7_.refs_9_.refs_25_), channel_id=1, source_target_pairs={{0,2},{2,0},{1,3},{3,1},{4,6},{6,4},{5,7},{7,5},{8,10},{10,8},{9,1... | collective-permute-start | bytes 9437192 | tf_op jit(solution)/shard_map/ppermute | solution.py:17
  319.2 16.1 %collective-permute-start.20 = (bf16[3,256,256]{2,1,0:T(8,128)(2,1)}, bf16[3,256,256]{2,1,0:T(8,128)(2,1)}, u32[]{:S(2)}, u32[]{:S(2)}) collective-permute-start(bf16[3,256,256]{2,1,0:T(8,128)(2,1)} %get-tuple-element.167.refs_0_), channel_id=1, source_target_pairs={{0,1},{1,0},{2,3},{3,2},{4,5},{5,4},{6,7},{7,6},{8,9},{9,8},{10,11... | collective-permute-start | bytes 1179656 | tf_op jit(solution)/shard_map/ppermute | solution.py:17
  319.5 15.8 %collective-permute-start.25 = (bf16[3,256,256]{2,1,0:T(8,128)(2,1)S(1)}, bf16[3,256,256]{2,1,0:T(8,128)(2,1)}, u32[]{:S(2)}, u32[]{:S(2)}) collective-permute-start(bf16[3,256,256]{2,1,0:T(8,128)(2,1)S(1)} %get-tuple-element.166.refs_4_), channel_id=1, source_target_pairs={{0,4},{4,0},{1,5},{5,1},{2,6},{6,2},{3,7},{7,3},{8,12},{12,8},{9,1... | collective-permute-start | bytes 1179656 | tf_op jit(solution)/shard_map/ppermute | solution.py:17
  320.9 18.5 %collective-permute-start.21 = (bf16[3,256,256]{2,1,0:T(8,128)(2,1)}, bf16[3,256,256]{2,1,0:T(8,128)(2,1)}, u32[]{:S(2)}, u32[]{:S(2)}) collective-permute-start(bf16[3,256,256]{2,1,0:T(8,128)(2,1)} %collective-permute-done.19.refs_1_), channel_id=1, source_target_pairs={{0,1},{1,0},{2,3},{3,2},{4,5},{5,4},{6,7},{7,6},{8,9},{9,8},{10,11... | collective-permute-start | bytes 1179656 | tf_op jit(solution)/shard_map/ppermute | solution.py:17
  322.7 16.7 %collective-permute-start.26 = (bf16[3,256,256]{2,1,0:T(8,128)(2,1)}, bf16[3,256,256]{2,1,0:T(8,128)(2,1)}, u32[]{:S(2)}, u32[]{:S(2)}) collective-permute-start(bf16[3,256,256]{2,1,0:T(8,128)(2,1)} %collective-permute-done.24.refs_5_), channel_id=1, source_target_pairs={{0,4},{4,0},{1,5},{5,1},{2,6},{6,2},{3,7},{7,3},{8,12},{12,8},{9,1... | collective-permute-start | bytes 1179656 | tf_op jit(solution)/shard_map/ppermute | solution.py:17
  339.4 19.3 %collective-permute-start.28 = (bf16[2,3,256,256]{3,2,1,0:T(8,128)(2,1)}, bf16[2,3,256,256]{3,2,1,0:T(8,128)(2,1)S(1)}, u32[]{:S(2)}, u32[]{:S(2)}) collective-permute-start(bf16[2,3,256,256]{3,2,1,0:T(8,128)(2,1)} %get-tuple-element.88), channel_id=1, source_target_pairs={{0,1},{1,0},{2,3},{3,2},{4,5},{5,4},{6,7},{7,6},{8,9},{9,8},{10,11... | collective-permute-start | bytes 2359304 | tf_op jit(solution)/shard_map/ppermute | solution.py:17
  341.0 19.6 %collective-permute-start.33 = (bf16[2,3,256,256]{3,2,1,0:T(8,128)(2,1)}, bf16[2,3,256,256]{3,2,1,0:T(8,128)(2,1)S(1)}, u32[]{:S(2)}, u32[]{:S(2)}) collective-permute-start(bf16[2,3,256,256]{3,2,1,0:T(8,128)(2,1)} %get-tuple-element.90), channel_id=1, source_target_pairs={{0,4},{4,0},{1,5},{5,1},{2,6},{6,2},{3,7},{7,3},{8,12},{12,8},{9,1... | collective-permute-start | bytes 2359304 | tf_op jit(solution)/shard_map/ppermute | solution.py:17
  359.0 10.0 %collective-permute-start.29 = (bf16[3,256,256]{2,1,0:T(8,128)(2,1)S(1)}, bf16[3,256,256]{2,1,0:T(8,128)(2,1)S(1)}, u32[]{:S(2)}, u32[]{:S(2)}) collective-permute-start(bf16[3,256,256]{2,1,0:T(8,128)(2,1)S(1)} %fusion.40), channel_id=1, source_target_pairs={{0,4},{4,0},{1,5},{5,1},{2,6},{6,2},{3,7},{7,3},{8,12},{12,8},{9,1... | collective-permute-start | bytes 1179656 | tf_op jit(solution)/shard_map/ppermute | solution.py:17
  360.8 9.7 %collective-permute-start.34 = (bf16[3,256,256]{2,1,0:T(8,128)(2,1)S(1)}, bf16[3,256,256]{2,1,0:T(8,128)(2,1)S(1)}, u32[]{:S(2)}, u32[]{:S(2)}) collective-permute-start(bf16[3,256,256]{2,1,0:T(8,128)(2,1)S(1)} %fusion.41), channel_id=1, source_target_pairs={{0,1},{1,0},{2,3},{3,2},{4,5},{5,4},{6,7},{7,6},{8,9},{9,8},{10,11... | collective-permute-start | bytes 1179656 | tf_op jit(solution)/shard_map/ppermute | solution.py:17
  371.8 13.6 %collective-permute-start.30 = (bf16[3,256,256]{2,1,0:T(8,128)(2,1)}, bf16[3,256,256]{2,1,0:T(8,128)(2,1)}, u32[]{:S(2)}, u32[]{:S(2)}) collective-permute-start(bf16[3,256,256]{2,1,0:T(8,128)(2,1)} %get-tuple-element.165.refs_8_), channel_id=1, source_target_pairs={{0,4},{4,0},{1,5},{5,1},{2,6},{6,2},{3,7},{7,3},{8,12},{12,8},{9,1... | collective-permute-start | bytes 1179656 | tf_op jit(solution)/shard_map/ppermute | solution.py:17
  372.4 13.0 %collective-permute-start.35 = (bf16[3,256,256]{2,1,0:T(8,128)(2,1)S(1)}, bf16[3,256,256]{2,1,0:T(8,128)(2,1)}, u32[]{:S(2)}, u32[]{:S(2)}) collective-permute-start(bf16[3,256,256]{2,1,0:T(8,128)(2,1)S(1)} %get-tuple-element.164.refs_12_), channel_id=1, source_target_pairs={{0,1},{1,0},{2,3},{3,2},{4,5},{5,4},{6,7},{7,6},{8,9},{9,8},{10,11... | collective-permute-start | bytes 1179656 | tf_op jit(solution)/shard_map/ppermute | solution.py:17
  385.5 6.6 %collective-permute-start.38 = (bf16[2048,768]{1,0:T(8,128)(2,1)S(1)}, bf16[2048,768]{1,0:T(8,128)(2,1)}, u32[]{:S(2)}, u32[]{:S(2)}) collective-permute-start(bf16[2048,768]{1,0:T(8,128)(2,1)S(1)} %convolution_convert_fusion.refs_3_.refs_11_.refs_27_), channel_id=1, source_target_pairs={{0,2},{2,0},{1,3},{3,1},{4,6},{6,4},{5,7},{7,5},{8,10},{10,8},{9,1... | collective-permute-start | bytes 9437192 | tf_op jit(solution)/shard_map/ppermute | solution.py:17
  385.6 19.2 %collective-permute-start.31 = (bf16[3,256,256]{2,1,0:T(8,128)(2,1)}, bf16[3,256,256]{2,1,0:T(8,128)(2,1)}, u32[]{:S(2)}, u32[]{:S(2)}) collective-permute-start(bf16[3,256,256]{2,1,0:T(8,128)(2,1)} %get-tuple-element.165.refs_8_), channel_id=1, source_target_pairs={{0,1},{1,0},{2,3},{3,2},{4,5},{5,4},{6,7},{7,6},{8,9},{9,8},{10,11... | collective-permute-start | bytes 1179656 | tf_op jit(solution)/shard_map/ppermute | solution.py:17
  386.8 17.9 %collective-permute-start.36 = (bf16[3,256,256]{2,1,0:T(8,128)(2,1)S(1)}, bf16[3,256,256]{2,1,0:T(8,128)(2,1)}, u32[]{:S(2)}, u32[]{:S(2)}) collective-permute-start(bf16[3,256,256]{2,1,0:T(8,128)(2,1)S(1)} %get-tuple-element.164.refs_12_), channel_id=1, source_target_pairs={{0,4},{4,0},{1,5},{5,1},{2,6},{6,2},{3,7},{7,3},{8,12},{12,8},{9,1... | collective-permute-start | bytes 1179656 | tf_op jit(solution)/shard_map/ppermute | solution.py:17
  388.2 17.6 %collective-permute-start.32 = (bf16[3,256,256]{2,1,0:T(8,128)(2,1)}, bf16[3,256,256]{2,1,0:T(8,128)(2,1)}, u32[]{:S(2)}, u32[]{:S(2)}) collective-permute-start(bf16[3,256,256]{2,1,0:T(8,128)(2,1)} %collective-permute-done.30.refs_9_), channel_id=1, source_target_pairs={{0,1},{1,0},{2,3},{3,2},{4,5},{5,4},{6,7},{7,6},{8,9},{9,8},{10,11... | collective-permute-start | bytes 1179656 | tf_op jit(solution)/shard_map/ppermute | solution.py:17
  389.1 17.4 %collective-permute-start.37 = (bf16[3,256,256]{2,1,0:T(8,128)(2,1)}, bf16[3,256,256]{2,1,0:T(8,128)(2,1)}, u32[]{:S(2)}, u32[]{:S(2)}) collective-permute-start(bf16[3,256,256]{2,1,0:T(8,128)(2,1)} %collective-permute-done.35.refs_13_), channel_id=1, source_target_pairs={{0,4},{4,0},{1,5},{5,1},{2,6},{6,2},{3,7},{7,3},{8,12},{12,8},{9,1... | collective-permute-start | bytes 1179656 | tf_op jit(solution)/shard_map/ppermute | solution.py:17
  406.5 24.6 %collective-permute-start.39 = (bf16[2,4,256,256]{3,2,1,0:T(8,128)(2,1)}, bf16[2,4,256,256]{3,2,1,0:T(8,128)(2,1)S(1)}, u32[]{:S(2)}, u32[]{:S(2)}) collective-permute-start(bf16[2,4,256,256]{3,2,1,0:T(8,128)(2,1)} %get-tuple-element.100), channel_id=1, source_target_pairs={{0,1},{1,0},{2,3},{3,2},{4,5},{5,4},{6,7},{7,6},{8,9},{9,8},{10,11... | collective-permute-start | bytes 3145736 | tf_op jit(solution)/shard_map/ppermute | solution.py:17
  407.4 25.7 %collective-permute-start.44 = (bf16[2,4,256,256]{3,2,1,0:T(8,128)(2,1)}, bf16[2,4,256,256]{3,2,1,0:T(8,128)(2,1)S(1)}, u32[]{:S(2)}, u32[]{:S(2)}) collective-permute-start(bf16[2,4,256,256]{3,2,1,0:T(8,128)(2,1)} %get-tuple-element.102), channel_id=1, source_target_pairs={{0,4},{4,0},{1,5},{5,1},{2,6},{6,2},{3,7},{7,3},{8,12},{12,8},{9,1... | collective-permute-start | bytes 3145736 | tf_op jit(solution)/shard_map/ppermute | solution.py:17
  431.5 12.3 %collective-permute-start.40 = (bf16[4,256,256]{2,1,0:T(8,128)(2,1)S(1)}, bf16[4,256,256]{2,1,0:T(8,128)(2,1)S(1)}, u32[]{:S(2)}, u32[]{:S(2)}) collective-permute-start(bf16[4,256,256]{2,1,0:T(8,128)(2,1)S(1)} %fusion.36), channel_id=1, source_target_pairs={{0,4},{4,0},{1,5},{5,1},{2,6},{6,2},{3,7},{7,3},{8,12},{12,8},{9,1... | collective-permute-start | bytes 1572872 | tf_op jit(solution)/shard_map/ppermute | solution.py:17
  433.4 12.0 %collective-permute-start.45 = (bf16[4,256,256]{2,1,0:T(8,128)(2,1)S(1)}, bf16[4,256,256]{2,1,0:T(8,128)(2,1)S(1)}, u32[]{:S(2)}, u32[]{:S(2)}) collective-permute-start(bf16[4,256,256]{2,1,0:T(8,128)(2,1)S(1)} %fusion.37), channel_id=1, source_target_pairs={{0,1},{1,0},{2,3},{3,2},{4,5},{5,4},{6,7},{7,6},{8,9},{9,8},{10,11... | collective-permute-start | bytes 1572872 | tf_op jit(solution)/shard_map/ppermute | solution.py:17
  446.2 14.9 %collective-permute-start.41 = (bf16[4,256,256]{2,1,0:T(8,128)(2,1)S(1)}, bf16[4,256,256]{2,1,0:T(8,128)(2,1)S(1)}, u32[]{:S(2)}, u32[]{:S(2)}) collective-permute-start(bf16[4,256,256]{2,1,0:T(8,128)(2,1)S(1)} %get-tuple-element.159.refs_16_), channel_id=1, source_target_pairs={{0,4},{4,0},{1,5},{5,1},{2,6},{6,2},{3,7},{7,3},{8,12},{12,8},{9,1... | collective-permute-start | bytes 1572872 | tf_op jit(solution)/shard_map/ppermute | solution.py:17
  446.8 15.1 %collective-permute-start.46 = (bf16[4,256,256]{2,1,0:T(8,128)(2,1)S(1)}, bf16[4,256,256]{2,1,0:T(8,128)(2,1)S(1)}, u32[]{:S(2)}, u32[]{:S(2)}) collective-permute-start(bf16[4,256,256]{2,1,0:T(8,128)(2,1)S(1)} %get-tuple-element.158.refs_20_), channel_id=1, source_target_pairs={{0,1},{1,0},{2,3},{3,2},{4,5},{5,4},{6,7},{7,6},{8,9},{9,8},{10,11... | collective-permute-start | bytes 1572872 | tf_op jit(solution)/shard_map/ppermute | solution.py:17
  447.7 25.2 %collective-permute-start.42 = (bf16[4,256,256]{2,1,0:T(8,128)(2,1)S(1)}, bf16[4,256,256]{2,1,0:T(8,128)(2,1)S(1)}, u32[]{:S(2)}, u32[]{:S(2)}) collective-permute-start(bf16[4,256,256]{2,1,0:T(8,128)(2,1)S(1)} %get-tuple-element.159.refs_16_), channel_id=1, source_target_pairs={{0,1},{1,0},{2,3},{3,2},{4,5},{5,4},{6,7},{7,6},{8,9},{9,8},{10,11... | collective-permute-start | bytes 1572872 | tf_op jit(solution)/shard_map/ppermute | solution.py:17
  448.9 24.1 %collective-permute-start.47 = (bf16[4,256,256]{2,1,0:T(8,128)(2,1)S(1)}, bf16[4,256,256]{2,1,0:T(8,128)(2,1)S(1)}, u32[]{:S(2)}, u32[]{:S(2)}) collective-permute-start(bf16[4,256,256]{2,1,0:T(8,128)(2,1)S(1)} %get-tuple-element.158.refs_20_), channel_id=1, source_target_pairs={{0,4},{4,0},{1,5},{5,1},{2,6},{6,2},{3,7},{7,3},{8,12},{12,8},{9,1... | collective-permute-start | bytes 1572872 | tf_op jit(solution)/shard_map/ppermute | solution.py:17
  461.1 19.1 %collective-permute-start.43 = (bf16[4,256,256]{2,1,0:T(8,128)(2,1)S(1)}, bf16[4,256,256]{2,1,0:T(8,128)(2,1)}, u32[]{:S(2)}, u32[]{:S(2)}) collective-permute-start(bf16[4,256,256]{2,1,0:T(8,128)(2,1)S(1)} %collective-permute-done.41.refs_17_), channel_id=1, source_target_pairs={{0,1},{1,0},{2,3},{3,2},{4,5},{5,4},{6,7},{7,6},{8,9},{9,8},{10,11... | collective-permute-start | bytes 1572872 | tf_op jit(solution)/shard_map/ppermute | solution.py:17
  462.0 18.2 %collective-permute-start.48 = (bf16[4,256,256]{2,1,0:T(8,128)(2,1)S(1)}, bf16[4,256,256]{2,1,0:T(8,128)(2,1)}, u32[]{:S(2)}, u32[]{:S(2)}) collective-permute-start(bf16[4,256,256]{2,1,0:T(8,128)(2,1)S(1)} %collective-permute-done.46.refs_21_), channel_id=1, source_target_pairs={{0,4},{4,0},{1,5},{5,1},{2,6},{6,2},{3,7},{7,3},{8,12},{12,8},{9,1... | collective-permute-start | bytes 1572872 | tf_op jit(solution)/shard_map/ppermute | solution.py:17
  499.5 23.4 %collective-permute-start.51 = (bf16[1,2,2,128,256]{4,3,2,1,0:T(8,128)(2,1)S(1)}, bf16[1,2,2,128,256]{4,3,2,1,0:T(8,128)(2,1)S(1)}, u32[]{:S(2)}, u32[]{:S(2)}) collective-permute-start(bf16[1,2,2,128,256]{4,3,2,1,0:T(8,128)(2,1)S(1)} %get-tuple-element.149), channel_id=1, source_target_pairs={{0,5},{1,4},{4,1},{5,0},{2,7},{3,6},{6,3},{7,2},{8,13},{9,12},{12,... | collective-permute-start | bytes 786440 | tf_op jit(solution)/shard_map/ppermute | solution.py:494
  501.3 21.6 %collective-permute-start.50 = (bf16[1,2,2,128,256]{4,3,2,1,0:T(8,128)(2,1)S(1)}, bf16[1,2,2,128,256]{4,3,2,1,0:T(8,128)(2,1)S(1)}, u32[]{:S(2)}, u32[]{:S(2)}) collective-permute-start(bf16[1,2,2,128,256]{4,3,2,1,0:T(8,128)(2,1)S(1)} %get-tuple-element.150), channel_id=1, source_target_pairs={{0,4},{4,0},{1,5},{5,1},{2,6},{6,2},{3,7},{7,3},{8,12},{12,8},{9,1... | collective-permute-start | bytes 786440 | tf_op jit(solution)/shard_map/ppermute | solution.py:17
  501.9 21.0 %collective-permute-start.49 = (bf16[1,2,2,128,256]{4,3,2,1,0:T(8,128)(2,1)S(1)}, bf16[1,2,2,128,256]{4,3,2,1,0:T(8,128)(2,1)S(1)}, u32[]{:S(2)}, u32[]{:S(2)}) collective-permute-start(bf16[1,2,2,128,256]{4,3,2,1,0:T(8,128)(2,1)S(1)} %get-tuple-element.151), channel_id=1, source_target_pairs={{0,1},{1,0},{2,3},{3,2},{4,5},{5,4},{6,7},{7,6},{8,9},{9,8},{10,11... | collective-permute-start | bytes 786440 | tf_op jit(solution)/shard_map/ppermute | solution.py:17
  525.2 25.7 %all-to-all-start = ((bf16[4,1,2,2,128,256]{5,4,3,2,1,0:T(8,128)(2,1)}), bf16[4,1,2,2,128,256]{5,4,3,2,1,0:T(8,128)(2,1)S(1)}, u32[]{:S(2)}, u32[]{:S(2)}) async-start(bf16[4,1,2,2,128,256]{5,4,3,2,1,0:T(8,128)(2,1)} %bitcast.54), calls=%async_computation | async-start | bytes 2097152 | tf_op jit(solution)/shard_map/all_to_all | solution.py:513
  529.0 21.7 %collective-permute-start.54 = (bf16[1,2,2,128,256]{4,3,2,1,0:T(8,128)(2,1)S(1)}, bf16[1,2,2,128,256]{4,3,2,1,0:T(8,128)(2,1)S(1)}, u32[]{:S(2)}, u32[]{:S(2)}) collective-permute-start(bf16[1,2,2,128,256]{4,3,2,1,0:T(8,128)(2,1)S(1)} %get-tuple-element.145), channel_id=1, source_target_pairs={{0,5},{1,4},{4,1},{5,0},{2,7},{3,6},{6,3},{7,2},{8,13},{9,12},{12,... | collective-permute-start | bytes 786440 | tf_op jit(solution)/shard_map/ppermute | solution.py:494
  530.8 19.9 %collective-permute-start.53 = (bf16[1,2,2,128,256]{4,3,2,1,0:T(8,128)(2,1)S(1)}, bf16[1,2,2,128,256]{4,3,2,1,0:T(8,128)(2,1)S(1)}, u32[]{:S(2)}, u32[]{:S(2)}) collective-permute-start(bf16[1,2,2,128,256]{4,3,2,1,0:T(8,128)(2,1)S(1)} %get-tuple-element.146), channel_id=1, source_target_pairs={{0,4},{4,0},{1,5},{5,1},{2,6},{6,2},{3,7},{7,3},{8,12},{12,8},{9,1... | collective-permute-start | bytes 786440 | tf_op jit(solution)/shard_map/ppermute | solution.py:17
  531.4 19.3 %collective-permute-start.52 = (bf16[1,2,2,128,256]{4,3,2,1,0:T(8,128)(2,1)S(1)}, bf16[1,2,2,128,256]{4,3,2,1,0:T(8,128)(2,1)S(1)}, u32[]{:S(2)}, u32[]{:S(2)}) collective-permute-start(bf16[1,2,2,128,256]{4,3,2,1,0:T(8,128)(2,1)S(1)} %get-tuple-element.147), channel_id=1, source_target_pairs={{0,1},{1,0},{2,3},{3,2},{4,5},{5,4},{6,7},{7,6},{8,9},{9,8},{10,11... | collective-permute-start | bytes 786440 | tf_op jit(solution)/shard_map/ppermute | solution.py:17
  551.8 24.9 %all-to-all-start.1 = ((bf16[4,1,2,2,128,256]{5,4,3,2,1,0:T(8,128)(2,1)}), bf16[4,1,2,2,128,256]{5,4,3,2,1,0:T(8,128)(2,1)S(1)}, u32[]{:S(2)}, u32[]{:S(2)}) async-start(bf16[4,1,2,2,128,256]{5,4,3,2,1,0:T(8,128)(2,1)} %bitcast.187), calls=%async_computation.1 | async-start | bytes 2097152 | tf_op jit(solution)/shard_map/all_to_all | solution.py:513
  556.9 6.4 %collective-permute-start.55 = (bf16[1,2,2,128,256]{4,3,2,1,0:T(8,128)(2,1)S(1)}, bf16[1,2,2,128,256]{4,3,2,1,0:T(8,128)(2,1)S(1)}, u32[]{:S(2)}, u32[]{:S(2)}) collective-permute-start(bf16[1,2,2,128,256]{4,3,2,1,0:T(8,128)(2,1)S(1)} %get-tuple-element.143), channel_id=1, source_target_pairs={{0,1},{1,0},{2,3},{3,2},{4,5},{5,4},{6,7},{7,6},{8,9},{9,8},{10,11... | collective-permute-start | bytes 786440 | tf_op jit(solution)/shard_map/ppermute | solution.py:17
  557.9 8.1 %collective-permute-start.56 = (bf16[1,2,2,128,256]{4,3,2,1,0:T(8,128)(2,1)S(1)}, bf16[1,2,2,128,256]{4,3,2,1,0:T(8,128)(2,1)S(1)}, u32[]{:S(2)}, u32[]{:S(2)}) collective-permute-start(bf16[1,2,2,128,256]{4,3,2,1,0:T(8,128)(2,1)S(1)} %get-tuple-element.142), channel_id=1, source_target_pairs={{0,4},{4,0},{1,5},{5,1},{2,6},{6,2},{3,7},{7,3},{8,12},{12,8},{9,1... | collective-permute-start | bytes 786440 | tf_op jit(solution)/shard_map/ppermute | solution.py:17
  559.3 7.8 %collective-permute-start.57 = (bf16[1,2,2,128,256]{4,3,2,1,0:T(8,128)(2,1)S(1)}, bf16[1,2,2,128,256]{4,3,2,1,0:T(8,128)(2,1)S(1)}, u32[]{:S(2)}, u32[]{:S(2)}) collective-permute-start(bf16[1,2,2,128,256]{4,3,2,1,0:T(8,128)(2,1)S(1)} %get-tuple-element.141), channel_id=1, source_target_pairs={{0,5},{1,4},{4,1},{5,0},{2,7},{3,6},{6,3},{7,2},{8,13},{9,12},{12,... | collective-permute-start | bytes 786440 | tf_op jit(solution)/shard_map/ppermute | solution.py:494
  (43 other events, 449.6 us)
Sparse Core Ops, SparseCore 0:
  17.4 32.5 all-gather.17
  51.6 42.9 all-gather.7
  96.2 42.3 all-gather.9
  141.3 76.7 all-gather.11
  219.5 74.9 all-gather.13
  296.0 74.9 all-gather.15

commit v3 on v2

--- a/solution.py
+++ b/solution.py
@@ -165,9 +165,9 @@
     )
 
 
-def contract(groups, own, sib, flips, blocks, core, n_v, first, steps):
-    n_orb = len(own)
-    n_virt, width = own[0].shape
+def contract(groups, own, sib, flips, blocks, core, n_v, first, steps, n_orb, base=None, last=True):
+    used = sorted({o for group, _ in groups for pair in group for o in pair})
+    n_virt, width = own[used[0]].shape
     count = blocks.shape[0]
     bw = n_virt // count
     tile = tile_of(width)
@@ -181,10 +181,9 @@
     def kernel(index, *refs):
         held = refs[: len(pieces)]
         sides = [
-            refs[len(pieces) + side * n_orb : len(pieces) + (side + 1) * n_orb]
-            for side in range(2)
+            dict(zip(used, refs[len(pieces) + side * len(used) :])) for side in range(2)
         ]
-        out, amp, acc = refs[len(pieces) + 2 * n_orb :]
+        out, amp, acc = refs[-3:]
         step = pl.program_id(0)
 
         @pl.when(step == 0)
@@ -197,6 +196,8 @@
                     at += 1
                 base += len(group)
 
+        acc[...] = jnp.zeros_like(acc) if base is None else refs[-4][...]
+
         for side in range(2):
 
             @pl.when((step >= side * steps) & (step < (side + 1) * steps))
@@ -206,9 +207,8 @@
 
                 for p, (i, j) in enumerate(pairs):
                     if i == j:
-                        acc[i] = product(p, i)
-                for p, (i, j) in enumerate(pairs):
-                    if i != j:
+                        acc[i] += product(p, i)
+                    else:
                         flip = index[1 + count + mixed.index((i, j))]
 
                         @pl.when(flip == 0)
@@ -219,6 +219,9 @@
                         def _(p=p, i=i, j=j):
                             acc[j] += product(p, i)
 
+        if not last:
+            out[...] = acc[...]
+            return
         for i in range(n_orb):
             for v in range(n_v):
                 value = acc[i, v * sub : (v + 1) * sub, :]
@@ -232,10 +235,21 @@
         second = (t >= steps).astype(jnp.int32)
         return (0, 0, (index[0] + second) % 2, 0, 0, t - second * steps)
 
+    stored = steps if base is None else base.shape[0] // 2
+
+    def column(t, index):
+        second = (t >= steps).astype(jnp.int32)
+        return (first + second * (stored - steps) + t, 0, 0, 0)
+
     return call(
         kernel,
         index,
-        (*pieces, *[own[o] for o in range(n_orb)], *[sib[o] for o in range(n_orb)]),
+        (
+            *pieces,
+            *[own[o] for o in used],
+            *[sib[o] for o in used],
+            *([] if base is None else [base]),
+        ),
         (2 * steps,),
         [
             pl.BlockSpec(
@@ -248,18 +262,23 @@
                 (n_virt, tile), lambda t, index: (0, first + jnp.minimum(t, steps - 1))
             )
         ]
-        * n_orb
+        * len(used)
         + [pl.BlockSpec((n_virt, tile), lambda t, index: (0, first + jnp.maximum(t - steps, 0)))]
-        * n_orb,
-        pl.BlockSpec((n_v, 2, 1, half_orb, sub, tile), place),
-        jax.ShapeDtypeStruct((n_v, 2, 2, half_orb, sub, steps * tile), BF),
+        * len(used)
+        + ([] if base is None else [pl.BlockSpec((None, n_orb, rows, tile), column)]),
+        pl.BlockSpec((n_v, 2, 1, half_orb, sub, tile), place)
+        if last
+        else pl.BlockSpec((None, n_orb, rows, tile), column),
+        jax.ShapeDtypeStruct((n_v, 2, 2, half_orb, sub, steps * tile), BF)
+        if last
+        else jax.ShapeDtypeStruct((2 * steps, n_orb, rows, tile), F32),
         [
             pltpu.VMEM((len(pairs), rows, n_virt), BF),
             pltpu.VMEM((n_orb, rows, tile), F32),
         ],
         cost(
             4 * len(pairs) * rows * n_virt * steps * tile,
-            4 * n_orb * n_virt * steps * tile + 2 * len(pairs) * rows * n_virt,
+            4 * len(used) * n_virt * steps * tile + 2 * len(pairs) * rows * n_virt,
         ),
         "contract",
     )
@@ -408,7 +427,7 @@
 
     groups = []
 
-    def group(pairs, others=()):
+    def group(pairs, others=(), fill=()):
         part = functools.partial(coulomb, own, sib, pairs, flips)
         if not paired:
             (total,) = part(blocks, bw, a_block, a_rows, [2 * n_v])
@@ -431,9 +450,14 @@
         for h in range(2):
             near = swap(made[h], ways[h][1])
             nears.append(near)
-            pieces += [made[h], near, swap(made[h], ways[h][0]), swap(near, ways[h][0])]
+            direct = swap(made[h], ways[h][0])
+            far = swap(after(near, *fill, *([direct] if fill else [])), ways[h][0])
+            pieces += [made[h], near, direct, far]
         groups.append((pairs, pieces))
         return made, nears
+
+    half = metric.shape[0] // 2
+    steps = half // tile_of(half)
 
     cut = mu_rows // 2
     block = half_ints[:, 0, :]
@@ -465,17 +489,27 @@
         following[at] = [gather_z(value) for value in chosen]
     coef = coefficients((mine[:1], mine[1:], [far], marks))
     moved = gather_z(moved)
-    moved = after(moved, *ready)
-    transform(0, jnp.where(x == 0, shared, moved))
-    transform(occ_rows, jnp.where(x == 0, moved, shared))
+    transform(0, shared)
+    transform(occ_rows, after(moved, *ready, own[0]))
+    for side in (own, sib):
+        here, away = side[0], side[occ_rows]
+        side[0] = jnp.where(x == 0, here, away)
+        side[occ_rows] = jnp.where(x == 0, away, here)
+    sums = []
     made, nears = group([(0, 0), (0, occ_rows), (occ_rows, occ_rows)])
     for at in range(1, occ_rows):
         for orbital, value in zip((at, at + occ_rows), following[at]):
             seen = list(own)
             transform(orbital, after(value, *made), *nears)
+            if len(own) == n_orb:
+                wide = max(1, steps - 1)
+                sums.append(
+                    contract(groups[:], own, sib, flips, blocks, c, n_v, 0, wide, n_orb, last=False)
+                )
             made, nears = group(
                 [tuple(sorted((s, orbital))) for s in seen] + [(orbital, orbital)],
                 groups[-1][1],
+                tuple(sums),
             )
 
     def exchange(value, *others):
@@ -493,19 +527,18 @@
             (swap(take(1 - v, x), "v"), 1 - v, x),
             (lax.ppermute(take(1 - v, 1 - x), ("v", "x"), [(k, 3 - k) for k in range(4)]), 1 - v, 1 - x),
         )
-        whole = jnp.zeros((2, 2, 2) + value.shape[3:], BF)
-        for part, row, column in parts:
-            part = after(part, *others)
-            whole = lax.dynamic_update_slice(
-                whole, part.transpose(1, 0, 2, 3, 4)[None], (row, 0, column, 0, 0, 0)
-            )
-        return whole
-
-    made, base = [], own
-    for at in range(own[0].shape[1] // tile_of(own[0].shape[1])):
-        made.append(contract(groups, base, sib, flips, blocks, c, n_v, at, 1))
-        base = {o: after(array, made[-1]) for o, array in base.items()}
+        near, beside, above, across = (after(part, *others)[0] for part, _, _ in parts)
+        mine = [jnp.where(x == 0, near, beside), jnp.where(x == 0, beside, near)]
+        other = [jnp.where(x == 0, above, across), jnp.where(x == 0, across, above)]
+        mine, other = jnp.stack(mine, axis=1), jnp.stack(other, axis=1)
+        return jnp.stack([jnp.where(v == 0, mine, other), jnp.where(v == 0, other, mine)])
+
     results = []
+    made, held = [], own
+    for at in range(steps):
+        chosen, base = (groups[-1:], sums[0]) if at < wide else (groups, None)
+        made.append(contract(chosen, held, sib, flips, blocks, c, n_v, at, 1, n_orb, base))
+        held = {o: after(array, made[-1]) for o, array in held.items()}
     for at, value in enumerate(made):
         value = exchange(value, *made[at + 1 : at + 2])
         value = value.reshape((n_z, 2 * n_v // n_z) + value.shape[2:])

time: 623 us -> 619 us (level)
  waiting for transfers between devices: 186 us -> 156 us
  matrix products: 45.2 us -> 61.3 us
  other arithmetic: 46.3 us -> 52.7 us
    ppermute x55, waiting for transfers between devices: 164 us -> 143 us  [swap(): return lax.ppermute(value, axis, [(0, 1), (1, 0)])]
    dot_general x4, matrix products: 45.2 us -> 61.3 us  [transform(): own[orbital] = jnp.dot(coef, held, preferred_element_type=F32).astype(BF)]
    all_gather x6, waiting for transfers between devices: 11.7 us -> 0.01 us  [gather_z(): return lax.all_gather(value, 'z', axis=axis, tiled=True)]
    unnamed x86 -> x80, local copies, waits for them, and re-layouts: 4.7 us -> 11.1 us
    pallas_call x15 -> x16, Pallas kernels: 178 us -> 184 us  [call(): pl.pallas_call(kernel, grid_spec=pltpu.PrefetchScalarGridSpec(num_scalar_...]
  transfers between devices with their start and end apart: 66 -> 66, of which waited for: 29 -> 28; matrix products, arithmetic and copies ran while one was open for 17% -> 20% of each run, Pallas kernels for 26% -> 28%
where the time goes in v3:
time: 619 us; the launch traced here: 617 us
  Pallas kernels  190 us (31%)
  waiting for transfers between devices  156 us (25%)
  starting transfers between devices  68.7 us (11%)
  matrix products  61.3 us (10%)
  other arithmetic  52.7 us (9%)
  local copies, waits for them, and re-layouts  31.6 us (5%)
  between operations  30.8 us (5%)
  blocking collectives  25.4 us (4%)
    pallas_call x16, Pallas kernels, call(): pl.pallas_call(kernel, grid_spec=pltpu.PrefetchScalarGridSpec(num_scalar_...  184 us
    ppermute x55, waiting for transfers between devices, swap(): return lax.ppermute(value, axis, [(0, 1), (1, 0)])  143 us
    dot_general x4, matrix products, transform(): own[orbital] = jnp.dot(coef, held, preferred_element_type=F32).astype(BF)  61.3 us
    ppermute x55, starting transfers between devices, swap(): return lax.ppermute(value, axis, [(0, 1), (1, 0)])  52.7 us
    all_to_all x1, blocking collectives, local(): results.append(lax.all_to_all(value, 'z', 0, 0, tiled=True))  25.4 us
  transfers between devices with their start and end apart: 66, of which 28 were waited for; matrix products, arithmetic and copies ran while one was open for 20% of the time, Pallas kernels for 28%

profile of v3, /device:TPU:0, one launch (start us, length us, event | category | flops | bytes accessed | tf_op | source)
XLA Modules:
  0.0 616.6 jit_solution(11784811170207331375)
XLA Ops:
  6.5 5.4 fusion.42
  12.1 3.0 collective-permute-start.2
  17.4 19.5 %collective-permute-done.2.refs_2_ = bf16[320,1536]{1,0:T(8,128)(2,1)S(1)} collective-permute-done((bf16[320,1536]{1,0:T(8,128)(2,1)S(1)}, bf16[320,1536]{1,0:T(8,128)(2,1)S(1)}, u32[]{:S(2)}, u32[]{:S(2)}) %collective-permute-start.2) | collective-permute-done | bytes 983072 | tf_op jit(solution)/shard_map/ppermute | solution.py:17
  36.9 2.0 copy.48
  39.0 1.8 collective-permute-start.6
  41.4 8.8 %fit.6 = bf16[320,768]{1,0:T(8,128)(2,1)} custom-call(s32[5]{0:T(128)} %concatenate.171.index, bf16[320,1536]{1,0:T(8,128)(2,1)} %bitcast.184, bf16[320,1536]{1,0:T(8,128)(2,1)} %collective-permute-done.1.refs_1_, bf16[320,1536]{1,0:T(8,128)(2,1)} %copy-done.28, bf16[320,1536]{1,0:T(8,128)(2,1)} %collective-permute-done.3.refs_3_, bf16[1536,6144]{1,0:T(8,128)(2,1)} %refs_4_.11), custom_call_target="tpu_custom_call" | custom-call | flops 3019898880 | bytes 13860864 | tf_op jit(solution)/shard_map/fit/pallas_call | solution.py:29
  50.3 12.6 %collective-permute-done.6.refs_2_ = bf16[320,1536]{1,0:T(8,128)(2,1)} collective-permute-done((bf16[320,1536]{1,0:T(8,128)(2,1)S(1)}, bf16[320,1536]{1,0:T(8,128)(2,1)}, u32[]{:S(2)}, u32[]{:S(2)}) %collective-permute-start.6) | collective-permute-done | bytes 983072 | tf_op jit(solution)/shard_map/ppermute | solution.py:17
  62.9 2.7 copy.33
  65.8 1.8 collective-permute-start.8
  68.2 8.8 %fit.7 = bf16[320,768]{1,0:T(8,128)(2,1)} custom-call(s32[5]{0:T(128)} %concatenate.172.index, bf16[320,1536]{1,0:T(8,128)(2,1)} %bitcast.185, bf16[320,1536]{1,0:T(8,128)(2,1)} %collective-permute-done.1.refs_1_, bf16[320,1536]{1,0:T(8,128)(2,1)} %copy-done.28, bf16[320,1536]{1,0:T(8,128)(2,1)} %collective-permute-done.3.refs_3_, bf16[1536,6144]{1,0:T(8,128)(2,1)} %refs_4_.11), custom_call_target="tpu_custom_call" | custom-call | flops 3019898880 | bytes 13860864 | tf_op jit(solution)/shard_map/fit/pallas_call | solution.py:29
  80.1 8.8 %fit.8 = bf16[320,768]{1,0:T(8,128)(2,1)} custom-call(s32[5]{0:T(128)} %concatenate.171.index, bf16[320,1536]{1,0:T(8,128)(2,1)} %bitcast.187, bf16[320,1536]{1,0:T(8,128)(2,1)} %collective-permute-done.5.refs_1_, bf16[320,1536]{1,0:T(8,128)(2,1)} %collective-permute-done.6.refs_2_, bf16[320,1536]{1,0:T(8,128)(2,1)} %collective-permute-done.7.refs_3_, ...), custom_call_target="tpu_custom_call" | custom-call | flops 3019898880 | bytes 13860864 | tf_op jit(solution)/shard_map/fit/pallas_call | solution.py:29
  89.1 9.1 %fit.9 = bf16[320,768]{1,0:T(8,128)(2,1)} custom-call(s32[5]{0:T(128)} %concatenate.172.index, bf16[320,1536]{1,0:T(8,128)(2,1)} %bitcast.188, bf16[320,1536]{1,0:T(8,128)(2,1)} %collective-permute-done.5.refs_1_, bf16[320,1536]{1,0:T(8,128)(2,1)} %collective-permute-done.6.refs_2_, bf16[320,1536]{1,0:T(8,128)(2,1)} %collective-permute-done.7.refs_3_, ...), custom_call_target="tpu_custom_call" | custom-call | flops 3019898880 | bytes 13860864 | tf_op jit(solution)/shard_map/fit/pallas_call | solution.py:29
  98.1 10.5 %collective-permute-done.4 = bf16[1,256,2560]{2,1,0:T(8,128)(2,1)} collective-permute-done((bf16[1,256,2560]{2,1,0:T(8,128)(2,1)}, bf16[1,256,2560]{2,1,0:T(8,128)(2,1)}, u32[]{:S(2)}, u32[]{:S(2)}) %collective-permute-start.4) | collective-permute-done | bytes 1310752 | tf_op jit(solution)/shard_map/ppermute | solution.py:17
  117.6 22.6 %collective-permute-done.13 = bf16[640,768]{1,0:T(8,128)(2,1)S(1)} collective-permute-done((bf16[640,768]{1,0:T(8,128)(2,1)}, bf16[640,768]{1,0:T(8,128)(2,1)S(1)}, u32[]{:S(2)}, u32[]{:S(2)}) %collective-permute-start.13) | collective-permute-done | bytes 983072 | tf_op jit(solution)/shard_map/ppermute | solution.py:17
  141.6 12.4 %fit.11 = bf16[640,768]{1,0:T(8,128)(2,1)} custom-call(s32[5]{0:T(128)} %concatenate.172.index, bf16[640,1536]{1,0:T(8,128)(2,1)} %copy-done.3, bf16[640,1536]{1,0:T(8,128)(2,1)} %collective-permute-done.10.refs_1_, bf16[640,1536]{1,0:T(8,128)(2,1)} %collective-permute-done.8.refs_2_, bf16[640,1536]{1,0:T(8,128)(2,1)} %collective-permute-done.11.refs_3_, ...), custom_call_target="tpu_custom_call" | custom-call | flops 6039797760 | bytes 18284544 | tf_op jit(solution)/shard_map/fit/pallas_call | solution.py:29
  154.0 12.5 %fit.10 = bf16[640,768]{1,0:T(8,128)(2,1)} custom-call(s32[5]{0:T(128)} %concatenate.171.index, bf16[640,1536]{1,0:T(8,128)(2,1)} %copy-done.3, bf16[640,1536]{1,0:T(8,128)(2,1)} %collective-permute-done.10.refs_1_, bf16[640,1536]{1,0:T(8,128)(2,1)} %collective-permute-done.8.refs_2_, bf16[640,1536]{1,0:T(8,128)(2,1)} %collective-permute-done.11.refs_3_, ...), custom_call_target="tpu_custom_call" | custom-call | flops 6039797760 | bytes 18284544 | tf_op jit(solution)/shard_map/fit/pallas_call | solution.py:29
  166.4 6.4 %collective-permute-done.9 = bf16[2,256,2560]{2,1,0:T(8,128)(2,1)} collective-permute-done((bf16[2,256,2560]{2,1,0:T(8,128)(2,1)}, bf16[2,256,2560]{2,1,0:T(8,128)(2,1)}, u32[]{:S(2)}, u32[]{:S(2)}) %collective-permute-start.9) | collective-permute-done | bytes 2621472 | tf_op jit(solution)/shard_map/ppermute | solution.py:17
  172.9 2.9 broadcast_select_fusion.7
  175.8 3.1 pad_maximum_fusion.1
  180.7 4.4 pad_maximum_fusion.2
  185.1 18.4 %collective-permute-done.14 = bf16[640,768]{1,0:T(8,128)(2,1)} collective-permute-done((bf16[640,768]{1,0:T(8,128)(2,1)}, bf16[640,768]{1,0:T(8,128)(2,1)}, u32[]{:S(2)}, u32[]{:S(2)}) %collective-permute-start.14) | collective-permute-done | bytes 983072 | tf_op jit(solution)/shard_map/ppermute | solution.py:17
  203.5 2.8 broadcast_select_fusion.10
  206.3 4.1 broadcast_select_fusion.1
  211.4 3.9 copy-done.4
  215.3 9.6 %convolution_convert_fusion.3 = bf16[2048,768]{1,0:T(8,128)(2,1)} fusion(bf16[2048,2560]{1,0:T(8,128)(2,1)S(1)} %bitcast.178, bf16[2560,768]{1,0:T(8,128)(2,1)S(1)} %bitcast.192), kind=kOutput, calls=%fused_computation.8 | convolution fusion | flops 8054636544 | bytes 17563648 | tf_op jit(solution)/shard_map/dot_general | solution.py:400
  224.9 15.4 %broadcast_select_fusion.4 = (bf16[2048,768]{1,0:T(8,128)(2,1)}, bf16[2048,768]{1,0:T(8,128)(2,1)}, bf16[2048,768]{1,0:T(8,128)(2,1)}) fusion(bf16[2048,768]{1,0:T(8,128)(2,1)} %convolution_convert_fusion.3, pred[]{:T(512)S(6)} %eq.28, bf16[2048,2560]{1,0:T(8,128)(2,1)} %bitcast.179, bf16[2560,768]{1,0:T(8,128)(2,1)} %all-gather.12.cloned.1.call-done), kind=kOutput, calls=%fused_computation.11 | convolution fusion | flops 8057782272 | bytes 27000832 | tf_op jit(solution)/shard_map/dot_general | solution.py:400
  242.5 1.9 collective-permute-done
  246.5 5.0 broadcast_select_fusion.2
  251.6 9.0 %coulomb.6 = (bf16[2,3,256,256]{3,2,1,0:T(8,128)(2,1)}, bf16[2,3,256,256]{3,2,1,0:T(8,128)(2,1)}) custom-call(s32[6]{0:T(128)} %concatenate.180.index, bf16[2048,768]{1,0:T(8,128)(2,1)} %get-tuple-element.115.refs_0_.refs_4_.refs_6_.refs_8_.refs_16_.refs_24_, bf16[2048,768]{1,0:T(8,128)(2,1)} %get-tuple-element.117.refs_1_.refs_5_.refs_2_.refs_8_.refs_10_.refs_18_.refs_26_, ...), custom_call_target="tpu_custom_call" | custom-call | flops 241591904 | bytes 786432 | tf_op jit(solution)/shard_map/coulomb/pallas_call | solution.py:29
  260.6 1.9 collective-permute-start.17
  268.6 9.1 %coulomb.7 = (bf16[2,3,256,256]{3,2,1,0:T(8,128)(2,1)}, bf16[2,3,256,256]{3,2,1,0:T(8,128)(2,1)}) custom-call(s32[6]{0:T(128)} %concatenate.179.index, bf16[2048,768]{1,0:T(8,128)(2,1)} %get-tuple-element.115.refs_0_.refs_4_.refs_6_.refs_8_.refs_16_.refs_24_, bf16[2048,768]{1,0:T(8,128)(2,1)} %get-tuple-element.117.refs_1_.refs_5_.refs_2_.refs_8_.refs_10_.refs_18_.refs_26_, ...), custom_call_target="tpu_custom_call" | custom-call | flops 241591904 | bytes 786432 | tf_op jit(solution)/shard_map/coulomb/pallas_call | solution.py:29
  283.9 1.8 collective-permute-start.18
  291.7 3.1 collective-permute-done.18
  294.7 5.0 collective-permute-done.20
  299.7 3.2 fusion.33
  304.8 24.1 %convolution_convert_fusion.1.refs_1_.refs_7_.refs_9_.refs_17_.refs_25_ = bf16[2048,768]{1,0:T(8,128)(2,1)S(1)} fusion(bf16[2048,2560]{1,0:T(8,128)(2,1)} %bitcast.180, bf16[2560,768]{1,0:T(8,128)(2,1)} %all-gather.14.cloned.1.call-done), kind=kOutput, calls=%fused_computation.6 | convolution fusion | flops 8054636544 | bytes 17563648 | tf_op jit(solution)/shard_map/dot_general | solution.py:400
  329.1 1.9 collective-permute-start.26
  331.4 1.8 collective-permute-start.25
  335.1 10.0 %coulomb.8 = (bf16[2,3,256,256]{3,2,1,0:T(8,128)(2,1)}, bf16[2,3,256,256]{3,2,1,0:T(8,128)(2,1)}) custom-call(s32[7]{0:T(128)} %concatenate.182.index, bf16[2048,768]{1,0:T(8,128)(2,1)} %get-tuple-element.115.refs_0_.refs_4_.refs_6_.refs_8_.refs_16_.refs_24_, bf16[2048,768]{1,0:T(8,128)(2,1)} %copy-done, ...), custom_call_target="tpu_custom_call" | custom-call | flops 241591904 | bytes 1101004 | tf_op jit(solution)/shard_map/coulomb/pallas_call | solution.py:29
  345.0 4.4 collective-permute-done.27.refs_7_
  352.2 10.4 %coulomb.9 = (bf16[2,3,256,256]{3,2,1,0:T(8,128)(2,1)}, bf16[2,3,256,256]{3,2,1,0:T(8,128)(2,1)}) custom-call(s32[7]{0:T(128)} %concatenate.181.index, bf16[2048,768]{1,0:T(8,128)(2,1)} %get-tuple-element.115.refs_0_.refs_4_.refs_6_.refs_8_.refs_16_.refs_24_, bf16[2048,768]{1,0:T(8,128)(2,1)} %copy-done, ...), custom_call_target="tpu_custom_call" | custom-call | flops 241591904 | bytes 1101004 | tf_op jit(solution)/shard_map/coulomb/pallas_call | solution.py:29
  365.1 4.9 collective-permute-done.28
  376.0 3.8 collective-permute-done.29
  383.7 12.1 %convolution_convert_fusion.refs_3_.refs_11_.refs_27_ = bf16[2048,768]{1,0:T(8,128)(2,1)S(1)} fusion(bf16[2048,2560]{1,0:T(8,128)(2,1)} %bitcast.181, bf16[2560,768]{1,0:T(8,128)(2,1)} %all-gather.16.cloned.1.call-done), kind=kOutput, calls=%fused_computation.5 | convolution fusion | flops 8054636544 | bytes 17563648 | tf_op jit(solution)/shard_map/dot_general | solution.py:400
  402.8 12.2 %coulomb.10 = (bf16[2,4,256,256]{3,2,1,0:T(8,128)(2,1)}, bf16[2,4,256,256]{3,2,1,0:T(8,128)(2,1)}) custom-call(s32[8]{0:T(128)} %concatenate.178.index, bf16[2048,768]{1,0:T(8,128)(2,1)} %get-tuple-element.115.refs_0_.refs_4_.refs_6_.refs_8_.refs_16_.refs_24_, bf16[2048,768]{1,0:T(8,128)(2,1)} %copy-done, ...), custom_call_target="tpu_custom_call" | custom-call | flops 322122560 | bytes 1468006 | tf_op jit(solution)/shard_map/coulomb/pallas_call | solution.py:29
  420.4 12.8 %coulomb.11 = (bf16[2,4,256,256]{3,2,1,0:T(8,128)(2,1)}, bf16[2,4,256,256]{3,2,1,0:T(8,128)(2,1)}) custom-call(s32[8]{0:T(128)} %concatenate.169.index, bf16[2048,768]{1,0:T(8,128)(2,1)} %get-tuple-element.115.refs_0_.refs_4_.refs_6_.refs_8_.refs_16_.refs_24_, bf16[2048,768]{1,0:T(8,128)(2,1)} %copy-done, ...), custom_call_target="tpu_custom_call" | custom-call | flops 322122560 | bytes 1468006 | tf_op jit(solution)/shard_map/coulomb/pallas_call | solution.py:29
  434.9 6.7 %collective-permute-done.39 = bf16[2,4,256,256]{3,2,1,0:T(8,128)(2,1)S(1)} collective-permute-done((bf16[2,4,256,256]{3,2,1,0:T(8,128)(2,1)}, bf16[2,4,256,256]{3,2,1,0:T(8,128)(2,1)S(1)}, u32[]{:S(2)}, u32[]{:S(2)}) %collective-permute-start.39) | collective-permute-done | bytes 1048608 | tf_op jit(solution)/shard_map/ppermute | solution.py:17
  454.6 3.3 collective-permute-done.45
  457.9 2.8 fusion.11
  464.9 19.2 %contract.4.refs_16_ = f32[4,4,256,256]{3,2,1,0:T(8,128)} custom-call(s32[12]{0:T(128)} %concatenate.183.index, bf16[3,256,256]{2,1,0:T(8,128)(2,1)} %get-tuple-element.191.refs_0_, bf16[3,256,256]{2,1,0:T(8,128)(2,1)} %collective-permute-done.21.refs_1_, bf16[3,256,256]{2,1,0:T(8,128)(2,1)} %collective-permute-done.24.refs_2_, ...), custom_call_target="tpu_custom_call" | custom-call | flops 6442450944 | bytes 18874368 | tf_op jit(solution)/shard_map/contract/pallas_call | solution.py:29
  488.2 7.0 %collective-permute-done.43.refs_3_.refs_19_ = bf16[4,256,256]{2,1,0:T(8,128)(2,1)S(1)} collective-permute-done((bf16[4,256,256]{2,1,0:T(8,128)(2,1)S(1)}, bf16[4,256,256]{2,1,0:T(8,128)(2,1)S(1)}, u32[]{:S(2)}, u32[]{:S(2)}) %collective-permute-start.43) | collective-permute-done | bytes 524320 | tf_op jit(solution)/shard_map/ppermute | solution.py:17
  496.8 11.0 %contract.5 = bf16[2,2,2,2,128,256]{5,4,3,2,1,0:T(8,128)(2,1)} custom-call(s32[12]{0:T(128)} %concatenate.168.index, bf16[4,256,256]{2,1,0:T(8,128)(2,1)} %copy-done.9, bf16[4,256,256]{2,1,0:T(8,128)(2,1)} %copy-done.18, bf16[4,256,256]{2,1,0:T(8,128)(2,1)} %copy-done.17, bf16[4,256,256]{2,1,0:T(8,128)(2,1)} %copy-done.19, bf16[4,256,256]{2,1,0:T(8,128)(2,1)} %copy-done.8, ...), custom_call_target="tpu_custom_call" | custom-call | flops 2147483648 | bytes 12582912 | tf_op jit(solution)/shard_map/contract/pallas_call | solution.py:29
  509.2 2.2 collective-permute-start.51
  512.7 11.4 %contract.6 = bf16[2,2,2,2,128,256]{5,4,3,2,1,0:T(8,128)(2,1)} custom-call(s32[12]{0:T(128)} %concatenate.168.index, bf16[4,256,256]{2,1,0:T(8,128)(2,1)} %copy-done.9, bf16[4,256,256]{2,1,0:T(8,128)(2,1)} %copy-done.18, bf16[4,256,256]{2,1,0:T(8,128)(2,1)} %copy-done.17, bf16[4,256,256]{2,1,0:T(8,128)(2,1)} %copy-done.19, bf16[4,256,256]{2,1,0:T(8,128)(2,1)} %copy-done.8, ...), custom_call_target="tpu_custom_call" | custom-call | flops 2147483648 | bytes 12582912 | tf_op jit(solution)/shard_map/contract/pallas_call | solution.py:29
  525.5 4.0 all-to-all-start
  530.3 2.1 collective-permute-start.54
  533.8 18.7 %contract.7 = bf16[2,2,2,2,128,256]{5,4,3,2,1,0:T(8,128)(2,1)} custom-call(s32[15]{0:T(128)} %concatenate.184.index, bf16[3,256,256]{2,1,0:T(8,128)(2,1)} %get-tuple-element.191.refs_0_, bf16[3,256,256]{2,1,0:T(8,128)(2,1)} %collective-permute-done.21.refs_1_, bf16[3,256,256]{2,1,0:T(8,128)(2,1)} %collective-permute-done.24.refs_2_, ...), custom_call_target="tpu_custom_call" | custom-call | flops 5368709120 | bytes 18874368 | tf_op jit(solution)/shard_map/contract/pallas_call | solution.py:29
  554.0 5.1 all-to-all-start.1
  559.1 2.1 collective-permute-start.57
  562.7 3.9 collective-permute-done.57
  566.6 2.7 collective-permute-done.56
  569.6 8.9 %all-to-all-done.1.refs_1_ = bf16[4,1,2,2,128,256]{5,4,3,2,1,0:T(8,128)(2,1)S(1)} async-done(((bf16[4,1,2,2,128,256]{5,4,3,2,1,0:T(8,128)(2,1)}), bf16[4,1,2,2,128,256]{5,4,3,2,1,0:T(8,128)(2,1)S(1)}, u32[]{:S(2)}, u32[]{:S(2)}) %all-to-all-start.1) | async-done | bytes 1048608 | tf_op jit(solution)/shard_map/all_to_all | solution.py:546
  578.5 25.4 %all_to_all.15.refs_2_ = bf16[4,1,2,2,128,256]{5,4,3,2,1,0:T(8,128)(2,1)} all-to-all(bf16[4,1,2,2,128,256]{5,4,3,2,1,0:T(8,128)(2,1)S(1)} %bitcast.191), channel_id=1, replica_groups=mesh['z'=4,'v'=2,'c'=2,'x'=2] {'z'}, dimensions={0} | all-to-all | bytes 2097152 | tf_op jit(solution)/shard_map/all_to_all | solution.py:546
  603.9 5.7 finish.1
  (249 shorter events, 91.4 us)
Async XLA Ops:
  6.5 71.1 %all-gather.18.cloned.1.call-start = ((), (), s32[]{:S(2)}) async-start(), calls=%async_computation.8 | async-start | bytes 1638400 | tf_op jit(solution)/shard_map/all_gather | solution.py:359
  12.1 24.8 %collective-permute-start.2 = (bf16[320,1536]{1,0:T(8,128)(2,1)S(1)}, bf16[320,1536]{1,0:T(8,128)(2,1)S(1)}, u32[]{:S(2)}, u32[]{:S(2)}) collective-permute-start(bf16[320,1536]{1,0:T(8,128)(2,1)S(1)} %bitcast.182), channel_id=1, source_target_pairs={{0,4},{4,0},{1,5},{5,1},{2,6},{6,2},{3,7},{7,3},{8,12},{12,8},{9,1... | collective-permute-start | bytes 2949128 | tf_op jit(solution)/shard_map/ppermute | solution.py:17
  17.3 163.4 %all-gather.8.cloned.1.call-start = ((), (), s32[]{:S(2)}) async-start(), calls=%async_computation.3 | async-start | bytes 2457600 | tf_op jit(solution)/shard_map/all_gather | solution.py:359
  17.3 24.0 %collective-permute-start.1 = (bf16[320,1536]{1,0:T(8,128)(2,1)S(1)}, bf16[320,1536]{1,0:T(8,128)(2,1)}, u32[]{:S(2)}, u32[]{:S(2)}) collective-permute-start(bf16[320,1536]{1,0:T(8,128)(2,1)S(1)} %bitcast.183), channel_id=1, source_target_pairs={{0,2},{2,0},{1,3},{3,1},{4,6},{6,4},{5,7},{7,5},{8,10},{10,8},{9,1... | collective-permute-start | bytes 2949128 | tf_op jit(solution)/shard_map/ppermute | solution.py:17
  36.9 4.5 collective-permute-start.3
  39.0 24.0 %collective-permute-start.6 = (bf16[320,1536]{1,0:T(8,128)(2,1)S(1)}, bf16[320,1536]{1,0:T(8,128)(2,1)}, u32[]{:S(2)}, u32[]{:S(2)}) collective-permute-start(bf16[320,1536]{1,0:T(8,128)(2,1)S(1)} %bitcast.186), channel_id=1, source_target_pairs={{0,4},{4,0},{1,5},{5,1},{2,6},{6,2},{3,7},{7,3},{8,12},{12,8},{9,1... | collective-permute-start | bytes 2949128 | tf_op jit(solution)/shard_map/ppermute | solution.py:17
  50.3 130.4 %all-gather.10.cloned.1.call-start = ((), (), s32[]{:S(2)}) async-start(), calls=%async_computation.4 | async-start | bytes 2457600 | tf_op jit(solution)/shard_map/all_gather | solution.py:359
  65.8 44.2 %collective-permute-start.8 = (bf16[640,1536]{1,0:T(8,128)(2,1)S(1)}, bf16[640,1536]{1,0:T(8,128)(2,1)}, u32[]{:S(2)}, u32[]{:S(2)}) collective-permute-start(bf16[640,1536]{1,0:T(8,128)(2,1)S(1)} %slice_bitcast_fusion.refs_0_), channel_id=1, source_target_pairs={{0,4},{4,0},{1,5},{5,1},{2,6},{6,2},{3,7},{7,3},{8,12},{12,8},{9,1... | collective-permute-start | bytes 5898248 | tf_op jit(solution)/shard_map/ppermute | solution.py:17
  68.2 10.9 %collective-permute-start.5 = (bf16[320,1536]{1,0:T(8,128)(2,1)S(1)}, bf16[320,1536]{1,0:T(8,128)(2,1)}, u32[]{:S(2)}, u32[]{:S(2)}) collective-permute-start(bf16[320,1536]{1,0:T(8,128)(2,1)S(1)} %bitcast.189), channel_id=1, source_target_pairs={{0,2},{2,0},{1,3},{3,1},{4,6},{6,4},{5,7},{7,5},{8,10},{10,8},{9,1... | collective-permute-start | bytes 2949128 | tf_op jit(solution)/shard_map/ppermute | solution.py:17
  77.6 31.1 %collective-permute-start.4 = (bf16[1,256,2560]{2,1,0:T(8,128)(2,1)}, bf16[1,256,2560]{2,1,0:T(8,128)(2,1)}, u32[]{:S(2)}, u32[]{:S(2)}) collective-permute-start(bf16[1,256,2560]{2,1,0:T(8,128)(2,1)} %bitcast.195), channel_id=1, source_target_pairs={{0,1},{1,0},{2,3},{3,2},{4,5},{5,4},{6,7},{7,6},{8,9},{9,8},{10,11... | collective-permute-start | bytes 3932168 | tf_op jit(solution)/shard_map/ppermute | solution.py:17
  79.1 62.5 %collective-permute-start.10 = (bf16[640,1536]{1,0:T(8,128)(2,1)S(1)}, bf16[640,1536]{1,0:T(8,128)(2,1)}, u32[]{:S(2)}, u32[]{:S(2)}) collective-permute-start(bf16[640,1536]{1,0:T(8,128)(2,1)S(1)} %slice_bitcast_fusion.refs_0_), channel_id=1, source_target_pairs={{0,2},{2,0},{1,3},{3,1},{4,6},{6,4},{5,7},{7,5},{8,10},{10,8},{9,1... | collective-permute-start | bytes 5898248 | tf_op jit(solution)/shard_map/ppermute | solution.py:17
  89.0 135.9 %all-gather.12.cloned.1.call-start = ((), (), s32[]{:S(2)}) async-start(), calls=%async_computation.5 | async-start | bytes 4915200 | tf_op jit(solution)/shard_map/all_gather | solution.py:359
  110.1 31.5 %collective-permute-start.11 = (bf16[640,1536]{1,0:T(8,128)(2,1)}, bf16[640,1536]{1,0:T(8,128)(2,1)}, u32[]{:S(2)}, u32[]{:S(2)}) collective-permute-start(bf16[640,1536]{1,0:T(8,128)(2,1)} %collective-permute-done.8.refs_2_), channel_id=1, source_target_pairs={{0,2},{2,0},{1,3},{3,1},{4,6},{6,4},{5,7},{7,5},{8,10},{10,8},{9,1... | collective-permute-start | bytes 5898248 | tf_op jit(solution)/shard_map/ppermute | solution.py:17
  113.3 59.6 %collective-permute-start.9 = (bf16[2,256,2560]{2,1,0:T(8,128)(2,1)}, bf16[2,256,2560]{2,1,0:T(8,128)(2,1)}, u32[]{:S(2)}, u32[]{:S(2)}) collective-permute-start(bf16[2,256,2560]{2,1,0:T(8,128)(2,1)} %pad_maximum_fusion.3), channel_id=1, source_target_pairs={{0,4},{4,0},{1,5},{5,1},{2,6},{6,2},{3,7},{7,3},{8,12},{12,8},{9,1... | collective-permute-start | bytes 7864328 | tf_op jit(solution)/shard_map/ppermute | solution.py:17
  116.1 24.1 %collective-permute-start.13 = (bf16[640,768]{1,0:T(8,128)(2,1)}, bf16[640,768]{1,0:T(8,128)(2,1)S(1)}, u32[]{:S(2)}, u32[]{:S(2)}) collective-permute-start(bf16[640,768]{1,0:T(8,128)(2,1)} %pad_maximum_fusion.7), channel_id=1, source_target_pairs={{0,1},{1,0},{2,3},{3,2},{4,5},{5,4},{6,7},{7,6},{8,9},{9,8},{10,11... | collective-permute-start | bytes 2949128 | tf_op jit(solution)/shard_map/ppermute | solution.py:17
  141.2 163.6 %all-gather.14.cloned.1.call-start = ((), (), s32[]{:S(2)}) async-start(), calls=%async_computation.6 | async-start | bytes 4915200 | tf_op jit(solution)/shard_map/all_gather | solution.py:359
  179.0 27.3 %collective-permute-start.12 = (bf16[4,256,2560]{2,1,0:T(8,128)(2,1)}, bf16[4,256,2560]{2,1,0:T(8,128)(2,1)}, u32[]{:S(2)}, u32[]{:S(2)}) collective-permute-start(bf16[4,256,2560]{2,1,0:T(8,128)(2,1)} %pad_maximum_fusion.1), channel_id=1, source_target_pairs={{0,2},{2,0},{1,3},{3,1},{4,6},{6,4},{5,7},{7,5},{8,10},{10,8},{9,1... | collective-permute-start | bytes 15728648 | tf_op jit(solution)/shard_map/ppermute | solution.py:17
  179.0 24.5 %collective-permute-start.14 = (bf16[640,768]{1,0:T(8,128)(2,1)}, bf16[640,768]{1,0:T(8,128)(2,1)}, u32[]{:S(2)}, u32[]{:S(2)}) collective-permute-start(bf16[640,768]{1,0:T(8,128)(2,1)} %fit.11), channel_id=1, source_target_pairs={{0,1},{1,0},{2,3},{3,2},{4,5},{5,4},{6,7},{7,6},{8,9},{9,8},{10,11... | collective-permute-start | bytes 2949128 | tf_op jit(solution)/shard_map/ppermute | solution.py:17
  206.2 177.5 %all-gather.16.cloned.1.call-start = ((), (), s32[]{:S(2)}) async-start(), calls=%async_computation.7 | async-start | bytes 4915200 | tf_op jit(solution)/shard_map/all_gather | solution.py:359
  224.9 21.6 %collective-permute-start.15 = (bf16[2048,768]{1,0:T(8,128)(2,1)}, bf16[2048,768]{1,0:T(8,128)(2,1)S(1)}, u32[]{:S(2)}, u32[]{:S(2)}) collective-permute-start(bf16[2048,768]{1,0:T(8,128)(2,1)} %convolution_convert_fusion.3), channel_id=1, source_target_pairs={{0,2},{2,0},{1,3},{3,1},{4,6},{6,4},{5,7},{7,5},{8,10},{10,8},{9,1... | collective-permute-start | bytes 9437192 | tf_op jit(solution)/shard_map/ppermute | solution.py:17
  240.3 6.2 %collective-permute-start.16 = (bf16[2048,768]{1,0:T(8,128)(2,1)}, bf16[2048,768]{1,0:T(8,128)(2,1)}, u32[]{:S(2)}, u32[]{:S(2)}) collective-permute-start(bf16[2048,768]{1,0:T(8,128)(2,1)} %get-tuple-element.192), channel_id=1, source_target_pairs={{0,2},{2,0},{1,3},{3,1},{4,6},{6,4},{5,7},{7,5},{8,10},{10,8},{9,1... | collective-permute-start | bytes 9437192 | tf_op jit(solution)/shard_map/ppermute | solution.py:17
  260.6 20.0 %collective-permute-start.17 = (bf16[2,3,256,256]{3,2,1,0:T(8,128)(2,1)}, bf16[2,3,256,256]{3,2,1,0:T(8,128)(2,1)}, u32[]{:S(2)}, u32[]{:S(2)}) collective-permute-start(bf16[2,3,256,256]{3,2,1,0:T(8,128)(2,1)} %get-tuple-element.76), channel_id=1, source_target_pairs={{0,1},{1,0},{2,3},{3,2},{4,5},{5,4},{6,7},{7,6},{8,9},{9,8},{10,11... | collective-permute-start | bytes 2359304 | tf_op jit(solution)/shard_map/ppermute | solution.py:17
  262.5 23.1 %collective-permute-start.19 = (bf16[2,3,256,256]{3,2,1,0:T(8,128)(2,1)}, bf16[2,3,256,256]{3,2,1,0:T(8,128)(2,1)}, u32[]{:S(2)}, u32[]{:S(2)}) collective-permute-start(bf16[2,3,256,256]{3,2,1,0:T(8,128)(2,1)} %get-tuple-element.77), channel_id=1, source_target_pairs={{0,4},{4,0},{1,5},{5,1},{2,6},{6,2},{3,7},{7,3},{8,12},{12,8},{9,1... | collective-permute-start | bytes 2359304 | tf_op jit(solution)/shard_map/ppermute | solution.py:17
  283.9 10.9 %collective-permute-start.18 = (bf16[3,256,256]{2,1,0:T(8,128)(2,1)}, bf16[3,256,256]{2,1,0:T(8,128)(2,1)}, u32[]{:S(2)}, u32[]{:S(2)}) collective-permute-start(bf16[3,256,256]{2,1,0:T(8,128)(2,1)} %fusion.38), channel_id=1, source_target_pairs={{0,4},{4,0},{1,5},{5,1},{2,6},{6,2},{3,7},{7,3},{8,12},{12,8},{9,1... | collective-permute-start | bytes 1179656 | tf_op jit(solution)/shard_map/ppermute | solution.py:17
  288.9 10.8 %collective-permute-start.20 = (bf16[3,256,256]{2,1,0:T(8,128)(2,1)}, bf16[3,256,256]{2,1,0:T(8,128)(2,1)}, u32[]{:S(2)}, u32[]{:S(2)}) collective-permute-start(bf16[3,256,256]{2,1,0:T(8,128)(2,1)} %fusion.39), channel_id=1, source_target_pairs={{0,1},{1,0},{2,3},{3,2},{4,5},{5,4},{6,7},{7,6},{8,9},{9,8},{10,11... | collective-permute-start | bytes 1179656 | tf_op jit(solution)/shard_map/ppermute | solution.py:17
  303.0 26.0 %collective-permute-start.22 = (bf16[3,256,256]{2,1,0:T(8,128)(2,1)}, bf16[3,256,256]{2,1,0:T(8,128)(2,1)}, u32[]{:S(2)}, u32[]{:S(2)}) collective-permute-start(bf16[3,256,256]{2,1,0:T(8,128)(2,1)} %get-tuple-element.190.refs_4_), channel_id=1, source_target_pairs={{0,1},{1,0},{2,3},{3,2},{4,5},{5,4},{6,7},{7,6},{8,9},{9,8},{10,11... | collective-permute-start | bytes 1179656 | tf_op jit(solution)/shard_map/ppermute | solution.py:17
  304.7 24.3 %collective-permute-start.21 = (bf16[3,256,256]{2,1,0:T(8,128)(2,1)}, bf16[3,256,256]{2,1,0:T(8,128)(2,1)}, u32[]{:S(2)}, u32[]{:S(2)}) collective-permute-start(bf16[3,256,256]{2,1,0:T(8,128)(2,1)} %get-tuple-element.191.refs_0_), channel_id=1, source_target_pairs={{0,4},{4,0},{1,5},{5,1},{2,6},{6,2},{3,7},{7,3},{8,12},{12,8},{9,1... | collective-permute-start | bytes 1179656 | tf_op jit(solution)/shard_map/ppermute | solution.py:17
  329.0 6.1 collective-permute-start.23
  329.1 15.9 %collective-permute-start.26 = (bf16[3,256,256]{2,1,0:T(8,128)(2,1)}, bf16[3,256,256]{2,1,0:T(8,128)(2,1)}, u32[]{:S(2)}, u32[]{:S(2)}) collective-permute-start(bf16[3,256,256]{2,1,0:T(8,128)(2,1)} %get-tuple-element.190.refs_4_), channel_id=1, source_target_pairs={{0,4},{4,0},{1,5},{5,1},{2,6},{6,2},{3,7},{7,3},{8,12},{12,8},{9,1... | collective-permute-start | bytes 1179656 | tf_op jit(solution)/shard_map/ppermute | solution.py:17
  331.0 14.0 %collective-permute-start.24 = (bf16[3,256,256]{2,1,0:T(8,128)(2,1)}, bf16[3,256,256]{2,1,0:T(8,128)(2,1)}, u32[]{:S(2)}, u32[]{:S(2)}) collective-permute-start(bf16[3,256,256]{2,1,0:T(8,128)(2,1)} %get-tuple-element.191.refs_0_), channel_id=1, source_target_pairs={{0,1},{1,0},{2,3},{3,2},{4,5},{5,4},{6,7},{7,6},{8,9},{9,8},{10,11... | collective-permute-start | bytes 1179656 | tf_op jit(solution)/shard_map/ppermute | solution.py:17
  331.3 18.2 %collective-permute-start.27 = (bf16[3,256,256]{2,1,0:T(8,128)(2,1)}, bf16[3,256,256]{2,1,0:T(8,128)(2,1)}, u32[]{:S(2)}, u32[]{:S(2)}) collective-permute-start(bf16[3,256,256]{2,1,0:T(8,128)(2,1)} %collective-permute-done.22.refs_5_), channel_id=1, source_target_pairs={{0,4},{4,0},{1,5},{5,1},{2,6},{6,2},{3,7},{7,3},{8,12},{12,8},{9,1... | collective-permute-start | bytes 1179656 | tf_op jit(solution)/shard_map/ppermute | solution.py:17
  331.4 19.5 %collective-permute-start.25 = (bf16[3,256,256]{2,1,0:T(8,128)(2,1)}, bf16[3,256,256]{2,1,0:T(8,128)(2,1)}, u32[]{:S(2)}, u32[]{:S(2)}) collective-permute-start(bf16[3,256,256]{2,1,0:T(8,128)(2,1)} %collective-permute-done.21.refs_1_), channel_id=1, source_target_pairs={{0,1},{1,0},{2,3},{3,2},{4,5},{5,4},{6,7},{7,6},{8,9},{9,8},{10,11... | collective-permute-start | bytes 1179656 | tf_op jit(solution)/shard_map/ppermute | solution.py:17
  350.9 19.0 %collective-permute-start.28 = (bf16[2,3,256,256]{3,2,1,0:T(8,128)(2,1)}, bf16[2,3,256,256]{3,2,1,0:T(8,128)(2,1)S(1)}, u32[]{:S(2)}, u32[]{:S(2)}) collective-permute-start(bf16[2,3,256,256]{3,2,1,0:T(8,128)(2,1)} %get-tuple-element.90), channel_id=1, source_target_pairs={{0,1},{1,0},{2,3},{3,2},{4,5},{5,4},{6,7},{7,6},{8,9},{9,8},{10,11... | collective-permute-start | bytes 2359304 | tf_op jit(solution)/shard_map/ppermute | solution.py:17
  351.2 19.7 %collective-permute-start.30 = (bf16[2,3,256,256]{3,2,1,0:T(8,128)(2,1)}, bf16[2,3,256,256]{3,2,1,0:T(8,128)(2,1)S(1)}, u32[]{:S(2)}, u32[]{:S(2)}) collective-permute-start(bf16[2,3,256,256]{3,2,1,0:T(8,128)(2,1)} %get-tuple-element.92), channel_id=1, source_target_pairs={{0,4},{4,0},{1,5},{5,1},{2,6},{6,2},{3,7},{7,3},{8,12},{12,8},{9,1... | collective-permute-start | bytes 2359304 | tf_op jit(solution)/shard_map/ppermute | solution.py:17
  370.2 9.6 %collective-permute-start.29 = (bf16[3,256,256]{2,1,0:T(8,128)(2,1)S(1)}, bf16[3,256,256]{2,1,0:T(8,128)(2,1)S(1)}, u32[]{:S(2)}, u32[]{:S(2)}) collective-permute-start(bf16[3,256,256]{2,1,0:T(8,128)(2,1)S(1)} %fusion.40), channel_id=1, source_target_pairs={{0,4},{4,0},{1,5},{5,1},{2,6},{6,2},{3,7},{7,3},{8,12},{12,8},{9,1... | collective-permute-start | bytes 1179656 | tf_op jit(solution)/shard_map/ppermute | solution.py:17
  371.2 9.7 %collective-permute-start.31 = (bf16[3,256,256]{2,1,0:T(8,128)(2,1)S(1)}, bf16[3,256,256]{2,1,0:T(8,128)(2,1)S(1)}, u32[]{:S(2)}, u32[]{:S(2)}) collective-permute-start(bf16[3,256,256]{2,1,0:T(8,128)(2,1)S(1)} %fusion.41), channel_id=1, source_target_pairs={{0,1},{1,0},{2,3},{3,2},{4,5},{5,4},{6,7},{7,6},{8,9},{9,8},{10,11... | collective-permute-start | bytes 1179656 | tf_op jit(solution)/shard_map/ppermute | solution.py:17
  382.4 13.5 %collective-permute-start.33 = (bf16[3,256,256]{2,1,0:T(8,128)(2,1)}, bf16[3,256,256]{2,1,0:T(8,128)(2,1)}, u32[]{:S(2)}, u32[]{:S(2)}) collective-permute-start(bf16[3,256,256]{2,1,0:T(8,128)(2,1)} %get-tuple-element.188.refs_12_), channel_id=1, source_target_pairs={{0,1},{1,0},{2,3},{3,2},{4,5},{5,4},{6,7},{7,6},{8,9},{9,8},{10,11... | collective-permute-start | bytes 1179656 | tf_op jit(solution)/shard_map/ppermute | solution.py:17
  382.8 13.1 %collective-permute-start.32 = (bf16[3,256,256]{2,1,0:T(8,128)(2,1)}, bf16[3,256,256]{2,1,0:T(8,128)(2,1)}, u32[]{:S(2)}, u32[]{:S(2)}) collective-permute-start(bf16[3,256,256]{2,1,0:T(8,128)(2,1)} %get-tuple-element.189.refs_8_), channel_id=1, source_target_pairs={{0,4},{4,0},{1,5},{5,1},{2,6},{6,2},{3,7},{7,3},{8,12},{12,8},{9,1... | collective-permute-start | bytes 1179656 | tf_op jit(solution)/shard_map/ppermute | solution.py:17
  395.9 6.8 %collective-permute-start.34 = (bf16[2048,768]{1,0:T(8,128)(2,1)S(1)}, bf16[2048,768]{1,0:T(8,128)(2,1)}, u32[]{:S(2)}, u32[]{:S(2)}) collective-permute-start(bf16[2048,768]{1,0:T(8,128)(2,1)S(1)} %convolution_convert_fusion.refs_3_.refs_11_.refs_27_), channel_id=1, source_target_pairs={{0,2},{2,0},{1,3},{3,1},{4,6},{6,4},{5,7},{7,5},{8,10},{10,8},{9,1... | collective-permute-start | bytes 9437192 | tf_op jit(solution)/shard_map/ppermute | solution.py:17
  396.0 19.0 %collective-permute-start.37 = (bf16[3,256,256]{2,1,0:T(8,128)(2,1)}, bf16[3,256,256]{2,1,0:T(8,128)(2,1)}, u32[]{:S(2)}, u32[]{:S(2)}) collective-permute-start(bf16[3,256,256]{2,1,0:T(8,128)(2,1)} %get-tuple-element.188.refs_12_), channel_id=1, source_target_pairs={{0,4},{4,0},{1,5},{5,1},{2,6},{6,2},{3,7},{7,3},{8,12},{12,8},{9,1... | collective-permute-start | bytes 1179656 | tf_op jit(solution)/shard_map/ppermute | solution.py:17
  397.1 17.9 %collective-permute-start.35 = (bf16[3,256,256]{2,1,0:T(8,128)(2,1)}, bf16[3,256,256]{2,1,0:T(8,128)(2,1)}, u32[]{:S(2)}, u32[]{:S(2)}) collective-permute-start(bf16[3,256,256]{2,1,0:T(8,128)(2,1)} %get-tuple-element.189.refs_8_), channel_id=1, source_target_pairs={{0,1},{1,0},{2,3},{3,2},{4,5},{5,4},{6,7},{7,6},{8,9},{9,8},{10,11... | collective-permute-start | bytes 1179656 | tf_op jit(solution)/shard_map/ppermute | solution.py:17
  398.7 17.5 %collective-permute-start.38 = (bf16[3,256,256]{2,1,0:T(8,128)(2,1)}, bf16[3,256,256]{2,1,0:T(8,128)(2,1)}, u32[]{:S(2)}, u32[]{:S(2)}) collective-permute-start(bf16[3,256,256]{2,1,0:T(8,128)(2,1)} %collective-permute-done.33.refs_13_), channel_id=1, source_target_pairs={{0,4},{4,0},{1,5},{5,1},{2,6},{6,2},{3,7},{7,3},{8,12},{12,8},{9,1... | collective-permute-start | bytes 1179656 | tf_op jit(solution)/shard_map/ppermute | solution.py:17
  399.8 17.3 %collective-permute-start.36 = (bf16[3,256,256]{2,1,0:T(8,128)(2,1)}, bf16[3,256,256]{2,1,0:T(8,128)(2,1)}, u32[]{:S(2)}, u32[]{:S(2)}) collective-permute-start(bf16[3,256,256]{2,1,0:T(8,128)(2,1)} %collective-permute-done.32.refs_9_), channel_id=1, source_target_pairs={{0,1},{1,0},{2,3},{3,2},{4,5},{5,4},{6,7},{7,6},{8,9},{9,8},{10,11... | collective-permute-start | bytes 1179656 | tf_op jit(solution)/shard_map/ppermute | solution.py:17
  417.1 24.6 %collective-permute-start.39 = (bf16[2,4,256,256]{3,2,1,0:T(8,128)(2,1)}, bf16[2,4,256,256]{3,2,1,0:T(8,128)(2,1)S(1)}, u32[]{:S(2)}, u32[]{:S(2)}) collective-permute-start(bf16[2,4,256,256]{3,2,1,0:T(8,128)(2,1)} %get-tuple-element.102), channel_id=1, source_target_pairs={{0,1},{1,0},{2,3},{3,2},{4,5},{5,4},{6,7},{7,6},{8,9},{9,8},{10,11... | collective-permute-start | bytes 3145736 | tf_op jit(solution)/shard_map/ppermute | solution.py:17
  418.7 24.4 %collective-permute-start.44 = (bf16[2,4,256,256]{3,2,1,0:T(8,128)(2,1)}, bf16[2,4,256,256]{3,2,1,0:T(8,128)(2,1)}, u32[]{:S(2)}, u32[]{:S(2)}) collective-permute-start(bf16[2,4,256,256]{3,2,1,0:T(8,128)(2,1)} %get-tuple-element.105), channel_id=1, source_target_pairs={{0,4},{4,0},{1,5},{5,1},{2,6},{6,2},{3,7},{7,3},{8,12},{12,8},{9,1... | collective-permute-start | bytes 3145736 | tf_op jit(solution)/shard_map/ppermute | solution.py:17
  442.1 12.5 %collective-permute-start.40 = (bf16[4,256,256]{2,1,0:T(8,128)(2,1)S(1)}, bf16[4,256,256]{2,1,0:T(8,128)(2,1)}, u32[]{:S(2)}, u32[]{:S(2)}) collective-permute-start(bf16[4,256,256]{2,1,0:T(8,128)(2,1)S(1)} %fusion.36), channel_id=1, source_target_pairs={{0,4},{4,0},{1,5},{5,1},{2,6},{6,2},{3,7},{7,3},{8,12},{12,8},{9,1... | collective-permute-start | bytes 1572872 | tf_op jit(solution)/shard_map/ppermute | solution.py:17
  445.6 12.4 %collective-permute-start.45 = (bf16[4,256,256]{2,1,0:T(8,128)(2,1)}, bf16[4,256,256]{2,1,0:T(8,128)(2,1)}, u32[]{:S(2)}, u32[]{:S(2)}) collective-permute-start(bf16[4,256,256]{2,1,0:T(8,128)(2,1)} %fusion.37), channel_id=1, source_target_pairs={{0,1},{1,0},{2,3},{3,2},{4,5},{5,4},{6,7},{7,6},{8,9},{9,8},{10,11... | collective-permute-start | bytes 1572872 | tf_op jit(solution)/shard_map/ppermute | solution.py:17
  460.7 23.4 %collective-permute-start.47 = (bf16[4,256,256]{2,1,0:T(8,128)(2,1)S(1)}, bf16[4,256,256]{2,1,0:T(8,128)(2,1)S(1)}, u32[]{:S(2)}, u32[]{:S(2)}) collective-permute-start(bf16[4,256,256]{2,1,0:T(8,128)(2,1)S(1)} %get-tuple-element.182.refs_4_.refs_20_), channel_id=1, source_target_pairs={{0,4},{4,0},{1,5},{5,1},{2,6},{6,2},{3,7},{7,3},{8,12},{12,8},{9,1... | collective-permute-start | bytes 1572872 | tf_op jit(solution)/shard_map/ppermute | solution.py:17
  461.9 22.2 %collective-permute-start.46 = (bf16[4,256,256]{2,1,0:T(8,128)(2,1)S(1)}, bf16[4,256,256]{2,1,0:T(8,128)(2,1)S(1)}, u32[]{:S(2)}, u32[]{:S(2)}) collective-permute-start(bf16[4,256,256]{2,1,0:T(8,128)(2,1)S(1)} %get-tuple-element.182.refs_4_.refs_20_), channel_id=1, source_target_pairs={{0,1},{1,0},{2,3},{3,2},{4,5},{5,4},{6,7},{7,6},{8,9},{9,8},{10,11... | collective-permute-start | bytes 1572872 | tf_op jit(solution)/shard_map/ppermute | solution.py:17
  463.5 21.4 %collective-permute-start.42 = (bf16[4,256,256]{2,1,0:T(8,128)(2,1)S(1)}, bf16[4,256,256]{2,1,0:T(8,128)(2,1)S(1)}, u32[]{:S(2)}, u32[]{:S(2)}) collective-permute-start(bf16[4,256,256]{2,1,0:T(8,128)(2,1)S(1)} %get-tuple-element.183.refs_0_.refs_16_), channel_id=1, source_target_pairs={{0,1},{1,0},{2,3},{3,2},{4,5},{5,4},{6,7},{7,6},{8,9},{9,8},{10,11... | collective-permute-start | bytes 1572872 | tf_op jit(solution)/shard_map/ppermute | solution.py:17
  463.9 20.9 %collective-permute-start.41 = (bf16[4,256,256]{2,1,0:T(8,128)(2,1)S(1)}, bf16[4,256,256]{2,1,0:T(8,128)(2,1)S(1)}, u32[]{:S(2)}, u32[]{:S(2)}) collective-permute-start(bf16[4,256,256]{2,1,0:T(8,128)(2,1)S(1)} %get-tuple-element.183.refs_0_.refs_16_), channel_id=1, source_target_pairs={{0,4},{4,0},{1,5},{5,1},{2,6},{6,2},{3,7},{7,3},{8,12},{12,8},{9,1... | collective-permute-start | bytes 1572872 | tf_op jit(solution)/shard_map/ppermute | solution.py:17
  484.9 10.4 %collective-permute-start.43 = (bf16[4,256,256]{2,1,0:T(8,128)(2,1)S(1)}, bf16[4,256,256]{2,1,0:T(8,128)(2,1)S(1)}, u32[]{:S(2)}, u32[]{:S(2)}) collective-permute-start(bf16[4,256,256]{2,1,0:T(8,128)(2,1)S(1)} %collective-permute-done.41.refs_1_.refs_17_), channel_id=1, source_target_pairs={{0,1},{1,0},{2,3},{3,2},{4,5},{5,4},{6,7},{7,6},{8,9},{9,8},{10,11... | collective-permute-start | bytes 1572872 | tf_op jit(solution)/shard_map/ppermute | solution.py:17
  486.4 9.3 %collective-permute-start.48 = (bf16[4,256,256]{2,1,0:T(8,128)(2,1)S(1)}, bf16[4,256,256]{2,1,0:T(8,128)(2,1)S(1)}, u32[]{:S(2)}, u32[]{:S(2)}) collective-permute-start(bf16[4,256,256]{2,1,0:T(8,128)(2,1)S(1)} %collective-permute-done.46.refs_5_.refs_21_), channel_id=1, source_target_pairs={{0,4},{4,0},{1,5},{5,1},{2,6},{6,2},{3,7},{7,3},{8,12},{12,8},{9,1... | collective-permute-start | bytes 1572872 | tf_op jit(solution)/shard_map/ppermute | solution.py:17
  509.2 15.0 %collective-permute-start.51 = (bf16[1,2,2,128,256]{4,3,2,1,0:T(8,128)(2,1)S(1)}, bf16[1,2,2,128,256]{4,3,2,1,0:T(8,128)(2,1)S(1)}, u32[]{:S(2)}, u32[]{:S(2)}) collective-permute-start(bf16[1,2,2,128,256]{4,3,2,1,0:T(8,128)(2,1)S(1)} %get-tuple-element.162), channel_id=1, source_target_pairs={{0,5},{1,4},{4,1},{5,0},{2,7},{3,6},{6,3},{7,2},{8,13},{9,12},{12,... | collective-permute-start | bytes 786440 | tf_op jit(solution)/shard_map/ppermute | solution.py:528
  511.3 12.8 %collective-permute-start.50 = (bf16[1,2,2,128,256]{4,3,2,1,0:T(8,128)(2,1)S(1)}, bf16[1,2,2,128,256]{4,3,2,1,0:T(8,128)(2,1)S(1)}, u32[]{:S(2)}, u32[]{:S(2)}) collective-permute-start(bf16[1,2,2,128,256]{4,3,2,1,0:T(8,128)(2,1)S(1)} %get-tuple-element.163), channel_id=1, source_target_pairs={{0,4},{4,0},{1,5},{5,1},{2,6},{6,2},{3,7},{7,3},{8,12},{12,8},{9,1... | collective-permute-start | bytes 786440 | tf_op jit(solution)/shard_map/ppermute | solution.py:17
  512.3 11.9 %collective-permute-start.49 = (bf16[1,2,2,128,256]{4,3,2,1,0:T(8,128)(2,1)S(1)}, bf16[1,2,2,128,256]{4,3,2,1,0:T(8,128)(2,1)S(1)}, u32[]{:S(2)}, u32[]{:S(2)}) collective-permute-start(bf16[1,2,2,128,256]{4,3,2,1,0:T(8,128)(2,1)S(1)} %get-tuple-element.164), channel_id=1, source_target_pairs={{0,1},{1,0},{2,3},{3,2},{4,5},{5,4},{6,7},{7,6},{8,9},{9,8},{10,11... | collective-permute-start | bytes 786440 | tf_op jit(solution)/shard_map/ppermute | solution.py:17
  525.5 28.4 %all-to-all-start = ((bf16[4,1,2,2,128,256]{5,4,3,2,1,0:T(8,128)(2,1)}), bf16[4,1,2,2,128,256]{5,4,3,2,1,0:T(8,128)(2,1)S(1)}, u32[]{:S(2)}, u32[]{:S(2)}) async-start(bf16[4,1,2,2,128,256]{5,4,3,2,1,0:T(8,128)(2,1)} %bitcast.54), calls=%async_computation | async-start | bytes 2097152 | tf_op jit(solution)/shard_map/all_to_all | solution.py:546
  530.3 22.3 %collective-permute-start.54 = (bf16[1,2,2,128,256]{4,3,2,1,0:T(8,128)(2,1)S(1)}, bf16[1,2,2,128,256]{4,3,2,1,0:T(8,128)(2,1)S(1)}, u32[]{:S(2)}, u32[]{:S(2)}) collective-permute-start(bf16[1,2,2,128,256]{4,3,2,1,0:T(8,128)(2,1)S(1)} %get-tuple-element.156), channel_id=1, source_target_pairs={{0,5},{1,4},{4,1},{5,0},{2,7},{3,6},{6,3},{7,2},{8,13},{9,12},{12,... | collective-permute-start | bytes 786440 | tf_op jit(solution)/shard_map/ppermute | solution.py:528
  532.4 20.2 %collective-permute-start.53 = (bf16[1,2,2,128,256]{4,3,2,1,0:T(8,128)(2,1)S(1)}, bf16[1,2,2,128,256]{4,3,2,1,0:T(8,128)(2,1)S(1)}, u32[]{:S(2)}, u32[]{:S(2)}) collective-permute-start(bf16[1,2,2,128,256]{4,3,2,1,0:T(8,128)(2,1)S(1)} %get-tuple-element.157), channel_id=1, source_target_pairs={{0,4},{4,0},{1,5},{5,1},{2,6},{6,2},{3,7},{7,3},{8,12},{12,8},{9,1... | collective-permute-start | bytes 786440 | tf_op jit(solution)/shard_map/ppermute | solution.py:17
  533.4 19.2 %collective-permute-start.52 = (bf16[1,2,2,128,256]{4,3,2,1,0:T(8,128)(2,1)S(1)}, bf16[1,2,2,128,256]{4,3,2,1,0:T(8,128)(2,1)S(1)}, u32[]{:S(2)}, u32[]{:S(2)}) collective-permute-start(bf16[1,2,2,128,256]{4,3,2,1,0:T(8,128)(2,1)S(1)} %get-tuple-element.158), channel_id=1, source_target_pairs={{0,1},{1,0},{2,3},{3,2},{4,5},{5,4},{6,7},{7,6},{8,9},{9,8},{10,11... | collective-permute-start | bytes 786440 | tf_op jit(solution)/shard_map/ppermute | solution.py:17
  554.0 24.6 %all-to-all-start.1 = ((bf16[4,1,2,2,128,256]{5,4,3,2,1,0:T(8,128)(2,1)}), bf16[4,1,2,2,128,256]{5,4,3,2,1,0:T(8,128)(2,1)S(1)}, u32[]{:S(2)}, u32[]{:S(2)}) async-start(bf16[4,1,2,2,128,256]{5,4,3,2,1,0:T(8,128)(2,1)} %bitcast.190), calls=%async_computation.1 | async-start | bytes 2097152 | tf_op jit(solution)/shard_map/all_to_all | solution.py:546
  559.1 7.4 %collective-permute-start.57 = (bf16[1,2,2,128,256]{4,3,2,1,0:T(8,128)(2,1)S(1)}, bf16[1,2,2,128,256]{4,3,2,1,0:T(8,128)(2,1)S(1)}, u32[]{:S(2)}, u32[]{:S(2)}) collective-permute-start(bf16[1,2,2,128,256]{4,3,2,1,0:T(8,128)(2,1)S(1)} %get-tuple-element.150), channel_id=1, source_target_pairs={{0,5},{1,4},{4,1},{5,0},{2,7},{3,6},{6,3},{7,2},{8,13},{9,12},{12,... | collective-permute-start | bytes 786440 | tf_op jit(solution)/shard_map/ppermute | solution.py:528
  561.3 8.0 %collective-permute-start.56 = (bf16[1,2,2,128,256]{4,3,2,1,0:T(8,128)(2,1)S(1)}, bf16[1,2,2,128,256]{4,3,2,1,0:T(8,128)(2,1)S(1)}, u32[]{:S(2)}, u32[]{:S(2)}) collective-permute-start(bf16[1,2,2,128,256]{4,3,2,1,0:T(8,128)(2,1)S(1)} %get-tuple-element.151), channel_id=1, source_target_pairs={{0,4},{4,0},{1,5},{5,1},{2,6},{6,2},{3,7},{7,3},{8,12},{12,8},{9,1... | collective-permute-start | bytes 786440 | tf_op jit(solution)/shard_map/ppermute | solution.py:17
  562.2 7.0 %collective-permute-start.55 = (bf16[1,2,2,128,256]{4,3,2,1,0:T(8,128)(2,1)S(1)}, bf16[1,2,2,128,256]{4,3,2,1,0:T(8,128)(2,1)S(1)}, u32[]{:S(2)}, u32[]{:S(2)}) collective-permute-start(bf16[1,2,2,128,256]{4,3,2,1,0:T(8,128)(2,1)S(1)} %get-tuple-element.152), channel_id=1, source_target_pairs={{0,1},{1,0},{2,3},{3,2},{4,5},{5,4},{6,7},{7,6},{8,9},{9,8},{10,11... | collective-permute-start | bytes 786440 | tf_op jit(solution)/shard_map/ppermute | solution.py:17
  (40 other events, 372.9 us)
Sparse Core Ops, SparseCore 0:
  17.4 32.5 all-gather.17
  51.6 42.9 all-gather.7
  96.2 42.3 all-gather.9
  141.4 76.7 all-gather.11
  219.6 74.9 all-gather.13
  296.0 74.9 all-gather.15

commit v4 on v3

--- a/solution.py
+++ b/solution.py
@@ -540,7 +540,7 @@
         made.append(contract(chosen, held, sib, flips, blocks, c, n_v, at, 1, n_orb, base))
         held = {o: after(array, made[-1]) for o, array in held.items()}
     for at, value in enumerate(made):
-        value = exchange(value, *made[at + 1 : at + 2])
+        value = exchange(value, *(made[at + 1 : at + 2] if at else ()))
         value = value.reshape((n_z, 2 * n_v // n_z) + value.shape[2:])
         value = after(value, *results[-1:])
         results.append(lax.all_to_all(value, "z", 0, 0, tiled=True))

time: 619 us -> 626 us (1.011)
  waiting for transfers between devices: 156 us -> 163 us
  transfers between devices with their start and end apart: 66 -> 66, of which waited for: 28 -> 29; matrix products, arithmetic and copies ran while one was open for 20% -> 20% of each run, Pallas kernels for 28% -> 28%
where the time goes in v4:
time: 626 us; the launch traced here: 624 us
  Pallas kernels  190 us (30%)
  waiting for transfers between devices  163 us (26%)
  starting transfers between devices  68.9 us (11%)
  matrix products  61.3 us (10%)
  other arithmetic  52.7 us (8%)
  local copies, waits for them, and re-layouts  33 us (5%)
  between operations  30.4 us (5%)
  blocking collectives  25.4 us (4%)
    pallas_call x16, Pallas kernels, call(): pl.pallas_call(kernel, grid_spec=pltpu.PrefetchScalarGridSpec(num_scalar_...  184 us
    ppermute x55, waiting for transfers between devices, swap(): return lax.ppermute(value, axis, [(0, 1), (1, 0)])  146 us
    dot_general x4, matrix products, transform(): own[orbital] = jnp.dot(coef, held, preferred_element_type=F32).astype(BF)  61.3 us
    ppermute x55, starting transfers between devices, swap(): return lax.ppermute(value, axis, [(0, 1), (1, 0)])  53.4 us
    all_to_all x1, blocking collectives, local(): results.append(lax.all_to_all(value, 'z', 0, 0, tiled=True))  25.4 us
  transfers between devices with their start and end apart: 66, of which 29 were waited for; matrix products, arithmetic and copies ran while one was open for 20% of the time, Pallas kernels for 28%

profile of v4, /device:TPU:0, one launch (start us, length us, event | category | flops | bytes accessed | tf_op | source)
XLA Modules:
  0.0 624.3 jit_solution(8438200124207231202)
XLA Ops:
  6.5 5.4 fusion.42
  12.1 3.0 collective-permute-start.2
  17.4 19.5 %collective-permute-done.2.refs_2_ = bf16[320,1536]{1,0:T(8,128)(2,1)S(1)} collective-permute-done((bf16[320,1536]{1,0:T(8,128)(2,1)S(1)}, bf16[320,1536]{1,0:T(8,128)(2,1)S(1)}, u32[]{:S(2)}, u32[]{:S(2)}) %collective-permute-start.2) | collective-permute-done | bytes 983072 | tf_op jit(solution)/shard_map/ppermute | solution.py:17
  36.9 2.0 copy.48
  39.0 1.8 collective-permute-start.6
  41.5 8.8 %fit.6 = bf16[320,768]{1,0:T(8,128)(2,1)} custom-call(s32[5]{0:T(128)} %concatenate.171.index, bf16[320,1536]{1,0:T(8,128)(2,1)} %bitcast.184, bf16[320,1536]{1,0:T(8,128)(2,1)} %collective-permute-done.1.refs_1_, bf16[320,1536]{1,0:T(8,128)(2,1)} %copy-done.27, bf16[320,1536]{1,0:T(8,128)(2,1)} %collective-permute-done.3.refs_3_, bf16[1536,6144]{1,0:T(8,128)(2,1)} %refs_4_.11), custom_call_target="tpu_custom_call" | custom-call | flops 3019898880 | bytes 13860864 | tf_op jit(solution)/shard_map/fit/pallas_call | solution.py:29
  50.4 12.6 %collective-permute-done.6.refs_2_ = bf16[320,1536]{1,0:T(8,128)(2,1)} collective-permute-done((bf16[320,1536]{1,0:T(8,128)(2,1)S(1)}, bf16[320,1536]{1,0:T(8,128)(2,1)}, u32[]{:S(2)}, u32[]{:S(2)}) %collective-permute-start.6) | collective-permute-done | bytes 983072 | tf_op jit(solution)/shard_map/ppermute | solution.py:17
  62.9 2.7 copy.33
  65.8 1.8 collective-permute-start.8
  68.3 8.8 %fit.7 = bf16[320,768]{1,0:T(8,128)(2,1)} custom-call(s32[5]{0:T(128)} %concatenate.172.index, bf16[320,1536]{1,0:T(8,128)(2,1)} %bitcast.185, bf16[320,1536]{1,0:T(8,128)(2,1)} %collective-permute-done.1.refs_1_, bf16[320,1536]{1,0:T(8,128)(2,1)} %copy-done.27, bf16[320,1536]{1,0:T(8,128)(2,1)} %collective-permute-done.3.refs_3_, bf16[1536,6144]{1,0:T(8,128)(2,1)} %refs_4_.11), custom_call_target="tpu_custom_call" | custom-call | flops 3019898880 | bytes 13860864 | tf_op jit(solution)/shard_map/fit/pallas_call | solution.py:29
  80.2 8.8 %fit.8 = bf16[320,768]{1,0:T(8,128)(2,1)} custom-call(s32[5]{0:T(128)} %concatenate.171.index, bf16[320,1536]{1,0:T(8,128)(2,1)} %bitcast.187, bf16[320,1536]{1,0:T(8,128)(2,1)} %collective-permute-done.5.refs_1_, bf16[320,1536]{1,0:T(8,128)(2,1)} %collective-permute-done.6.refs_2_, bf16[320,1536]{1,0:T(8,128)(2,1)} %collective-permute-done.7.refs_3_, ...), custom_call_target="tpu_custom_call" | custom-call | flops 3019898880 | bytes 13860864 | tf_op jit(solution)/shard_map/fit/pallas_call | solution.py:29
  89.1 9.1 %fit.9 = bf16[320,768]{1,0:T(8,128)(2,1)} custom-call(s32[5]{0:T(128)} %concatenate.172.index, bf16[320,1536]{1,0:T(8,128)(2,1)} %bitcast.188, bf16[320,1536]{1,0:T(8,128)(2,1)} %collective-permute-done.5.refs_1_, bf16[320,1536]{1,0:T(8,128)(2,1)} %collective-permute-done.6.refs_2_, bf16[320,1536]{1,0:T(8,128)(2,1)} %collective-permute-done.7.refs_3_, ...), custom_call_target="tpu_custom_call" | custom-call | flops 3019898880 | bytes 13860864 | tf_op jit(solution)/shard_map/fit/pallas_call | solution.py:29
  98.1 10.6 %collective-permute-done.4 = bf16[1,256,2560]{2,1,0:T(8,128)(2,1)} collective-permute-done((bf16[1,256,2560]{2,1,0:T(8,128)(2,1)}, bf16[1,256,2560]{2,1,0:T(8,128)(2,1)}, u32[]{:S(2)}, u32[]{:S(2)}) %collective-permute-start.4) | collective-permute-done | bytes 1310752 | tf_op jit(solution)/shard_map/ppermute | solution.py:17
  117.6 22.6 %collective-permute-done.13 = bf16[640,768]{1,0:T(8,128)(2,1)S(1)} collective-permute-done((bf16[640,768]{1,0:T(8,128)(2,1)}, bf16[640,768]{1,0:T(8,128)(2,1)S(1)}, u32[]{:S(2)}, u32[]{:S(2)}) %collective-permute-start.13) | collective-permute-done | bytes 983072 | tf_op jit(solution)/shard_map/ppermute | solution.py:17
  141.6 12.4 %fit.11 = bf16[640,768]{1,0:T(8,128)(2,1)} custom-call(s32[5]{0:T(128)} %concatenate.172.index, bf16[640,1536]{1,0:T(8,128)(2,1)} %copy-done.3, bf16[640,1536]{1,0:T(8,128)(2,1)} %collective-permute-done.10.refs_1_, bf16[640,1536]{1,0:T(8,128)(2,1)} %collective-permute-done.8.refs_2_, bf16[640,1536]{1,0:T(8,128)(2,1)} %collective-permute-done.11.refs_3_, ...), custom_call_target="tpu_custom_call" | custom-call | flops 6039797760 | bytes 18284544 | tf_op jit(solution)/shard_map/fit/pallas_call | solution.py:29
  154.0 12.5 %fit.10 = bf16[640,768]{1,0:T(8,128)(2,1)} custom-call(s32[5]{0:T(128)} %concatenate.171.index, bf16[640,1536]{1,0:T(8,128)(2,1)} %copy-done.3, bf16[640,1536]{1,0:T(8,128)(2,1)} %collective-permute-done.10.refs_1_, bf16[640,1536]{1,0:T(8,128)(2,1)} %collective-permute-done.8.refs_2_, bf16[640,1536]{1,0:T(8,128)(2,1)} %collective-permute-done.11.refs_3_, ...), custom_call_target="tpu_custom_call" | custom-call | flops 6039797760 | bytes 18284544 | tf_op jit(solution)/shard_map/fit/pallas_call | solution.py:29
  166.5 6.4 %collective-permute-done.9 = bf16[2,256,2560]{2,1,0:T(8,128)(2,1)} collective-permute-done((bf16[2,256,2560]{2,1,0:T(8,128)(2,1)}, bf16[2,256,2560]{2,1,0:T(8,128)(2,1)}, u32[]{:S(2)}, u32[]{:S(2)}) %collective-permute-start.9) | collective-permute-done | bytes 2621472 | tf_op jit(solution)/shard_map/ppermute | solution.py:17
  172.9 2.9 broadcast_select_fusion.7
  175.8 3.1 pad_maximum_fusion.1
  180.7 4.4 pad_maximum_fusion.2
  185.0 18.4 %collective-permute-done.14 = bf16[640,768]{1,0:T(8,128)(2,1)} collective-permute-done((bf16[640,768]{1,0:T(8,128)(2,1)}, bf16[640,768]{1,0:T(8,128)(2,1)}, u32[]{:S(2)}, u32[]{:S(2)}) %collective-permute-start.14) | collective-permute-done | bytes 983072 | tf_op jit(solution)/shard_map/ppermute | solution.py:17
  203.4 2.8 broadcast_select_fusion.10
  206.3 4.1 broadcast_select_fusion.1
  211.4 3.9 copy-done.4
  215.3 9.6 %convolution_convert_fusion.3 = bf16[2048,768]{1,0:T(8,128)(2,1)} fusion(bf16[2048,2560]{1,0:T(8,128)(2,1)S(1)} %bitcast.178, bf16[2560,768]{1,0:T(8,128)(2,1)S(1)} %bitcast.192), kind=kOutput, calls=%fused_computation.8 | convolution fusion | flops 8054636544 | bytes 17563648 | tf_op jit(solution)/shard_map/dot_general | solution.py:400
  224.9 15.4 %broadcast_select_fusion.4 = (bf16[2048,768]{1,0:T(8,128)(2,1)}, bf16[2048,768]{1,0:T(8,128)(2,1)}, bf16[2048,768]{1,0:T(8,128)(2,1)}) fusion(bf16[2048,768]{1,0:T(8,128)(2,1)} %convolution_convert_fusion.3, pred[]{:T(512)S(6)} %eq.28, bf16[2048,2560]{1,0:T(8,128)(2,1)} %bitcast.179, bf16[2560,768]{1,0:T(8,128)(2,1)} %all-gather.12.cloned.1.call-done), kind=kOutput, calls=%fused_computation.11 | convolution fusion | flops 8057782272 | bytes 27000832 | tf_op jit(solution)/shard_map/dot_general | solution.py:400
  242.5 1.9 collective-permute-done
  246.5 5.0 broadcast_select_fusion.2
  251.5 9.0 %coulomb.6 = (bf16[2,3,256,256]{3,2,1,0:T(8,128)(2,1)}, bf16[2,3,256,256]{3,2,1,0:T(8,128)(2,1)}) custom-call(s32[6]{0:T(128)} %concatenate.180.index, bf16[2048,768]{1,0:T(8,128)(2,1)} %get-tuple-element.107.refs_0_.refs_4_.refs_6_.refs_8_.refs_16_.refs_24_, bf16[2048,768]{1,0:T(8,128)(2,1)} %get-tuple-element.109.refs_1_.refs_5_.refs_2_.refs_8_.refs_10_.refs_18_.refs_26_, ...), custom_call_target="tpu_custom_call" | custom-call | flops 241591904 | bytes 786432 | tf_op jit(solution)/shard_map/coulomb/pallas_call | solution.py:29
  260.6 1.9 collective-permute-start.17
  268.9 9.1 %coulomb.7 = (bf16[2,3,256,256]{3,2,1,0:T(8,128)(2,1)}, bf16[2,3,256,256]{3,2,1,0:T(8,128)(2,1)}) custom-call(s32[6]{0:T(128)} %concatenate.179.index, bf16[2048,768]{1,0:T(8,128)(2,1)} %get-tuple-element.107.refs_0_.refs_4_.refs_6_.refs_8_.refs_16_.refs_24_, bf16[2048,768]{1,0:T(8,128)(2,1)} %get-tuple-element.109.refs_1_.refs_5_.refs_2_.refs_8_.refs_10_.refs_18_.refs_26_, ...), custom_call_target="tpu_custom_call" | custom-call | flops 241591904 | bytes 786432 | tf_op jit(solution)/shard_map/coulomb/pallas_call | solution.py:29
  283.9 1.8 collective-permute-start.18
  291.7 3.4 collective-permute-done.18
  295.1 4.8 collective-permute-done.20
  299.8 3.2 fusion.33
  304.9 24.1 %convolution_convert_fusion.1.refs_1_.refs_7_.refs_9_.refs_17_.refs_25_ = bf16[2048,768]{1,0:T(8,128)(2,1)S(1)} fusion(bf16[2048,2560]{1,0:T(8,128)(2,1)} %bitcast.180, bf16[2560,768]{1,0:T(8,128)(2,1)} %all-gather.14.cloned.1.call-done), kind=kOutput, calls=%fused_computation.6 | convolution fusion | flops 8054636544 | bytes 17563648 | tf_op jit(solution)/shard_map/dot_general | solution.py:400
  329.2 2.0 collective-permute-start.26
  331.5 1.8 collective-permute-start.25
  335.1 9.9 %coulomb.8 = (bf16[2,3,256,256]{3,2,1,0:T(8,128)(2,1)}, bf16[2,3,256,256]{3,2,1,0:T(8,128)(2,1)}) custom-call(s32[7]{0:T(128)} %concatenate.182.index, bf16[2048,768]{1,0:T(8,128)(2,1)} %get-tuple-element.107.refs_0_.refs_4_.refs_6_.refs_8_.refs_16_.refs_24_, bf16[2048,768]{1,0:T(8,128)(2,1)} %copy-done, ...), custom_call_target="tpu_custom_call" | custom-call | flops 241591904 | bytes 1101004 | tf_op jit(solution)/shard_map/coulomb/pallas_call | solution.py:29
  345.0 4.5 collective-permute-done.27.refs_7_
  352.3 10.3 %coulomb.9 = (bf16[2,3,256,256]{3,2,1,0:T(8,128)(2,1)}, bf16[2,3,256,256]{3,2,1,0:T(8,128)(2,1)}) custom-call(s32[7]{0:T(128)} %concatenate.181.index, bf16[2048,768]{1,0:T(8,128)(2,1)} %get-tuple-element.107.refs_0_.refs_4_.refs_6_.refs_8_.refs_16_.refs_24_, bf16[2048,768]{1,0:T(8,128)(2,1)} %copy-done, ...), custom_call_target="tpu_custom_call" | custom-call | flops 241591904 | bytes 1101004 | tf_op jit(solution)/shard_map/coulomb/pallas_call | solution.py:29
  365.1 4.9 collective-permute-done.28
  375.6 4.3 collective-permute-done.29
  383.8 12.1 %convolution_convert_fusion.refs_3_.refs_11_.refs_27_ = bf16[2048,768]{1,0:T(8,128)(2,1)S(1)} fusion(bf16[2048,2560]{1,0:T(8,128)(2,1)} %bitcast.181, bf16[2560,768]{1,0:T(8,128)(2,1)} %all-gather.16.cloned.1.call-done), kind=kOutput, calls=%fused_computation.5 | convolution fusion | flops 8054636544 | bytes 17563648 | tf_op jit(solution)/shard_map/dot_general | solution.py:400
  402.7 12.2 %coulomb.10 = (bf16[2,4,256,256]{3,2,1,0:T(8,128)(2,1)}, bf16[2,4,256,256]{3,2,1,0:T(8,128)(2,1)}) custom-call(s32[8]{0:T(128)} %concatenate.178.index, bf16[2048,768]{1,0:T(8,128)(2,1)} %get-tuple-element.107.refs_0_.refs_4_.refs_6_.refs_8_.refs_16_.refs_24_, bf16[2048,768]{1,0:T(8,128)(2,1)} %copy-done, ...), custom_call_target="tpu_custom_call" | custom-call | flops 322122560 | bytes 1468006 | tf_op jit(solution)/shard_map/coulomb/pallas_call | solution.py:29
  420.4 12.8 %coulomb.11 = (bf16[2,4,256,256]{3,2,1,0:T(8,128)(2,1)}, bf16[2,4,256,256]{3,2,1,0:T(8,128)(2,1)}) custom-call(s32[8]{0:T(128)} %concatenate.169.index, bf16[2048,768]{1,0:T(8,128)(2,1)} %get-tuple-element.107.refs_0_.refs_4_.refs_6_.refs_8_.refs_16_.refs_24_, bf16[2048,768]{1,0:T(8,128)(2,1)} %copy-done, ...), custom_call_target="tpu_custom_call" | custom-call | flops 322122560 | bytes 1468006 | tf_op jit(solution)/shard_map/coulomb/pallas_call | solution.py:29
  435.0 6.8 %collective-permute-done.39 = bf16[2,4,256,256]{3,2,1,0:T(8,128)(2,1)S(1)} collective-permute-done((bf16[2,4,256,256]{3,2,1,0:T(8,128)(2,1)}, bf16[2,4,256,256]{3,2,1,0:T(8,128)(2,1)S(1)}, u32[]{:S(2)}, u32[]{:S(2)}) %collective-permute-start.39) | collective-permute-done | bytes 1048608 | tf_op jit(solution)/shard_map/ppermute | solution.py:17
  454.7 3.3 collective-permute-done.45
  458.0 2.8 fusion.11
  464.9 19.2 %contract.4.refs_16_ = f32[4,4,256,256]{3,2,1,0:T(8,128)} custom-call(s32[12]{0:T(128)} %concatenate.183.index, bf16[3,256,256]{2,1,0:T(8,128)(2,1)} %get-tuple-element.183.refs_0_, bf16[3,256,256]{2,1,0:T(8,128)(2,1)} %collective-permute-done.21.refs_1_, bf16[3,256,256]{2,1,0:T(8,128)(2,1)} %collective-permute-done.24.refs_2_, ...), custom_call_target="tpu_custom_call" | custom-call | flops 6442450944 | bytes 18874368 | tf_op jit(solution)/shard_map/contract/pallas_call | solution.py:29
  488.3 7.0 %collective-permute-done.43.refs_3_.refs_19_ = bf16[4,256,256]{2,1,0:T(8,128)(2,1)S(1)} collective-permute-done((bf16[4,256,256]{2,1,0:T(8,128)(2,1)S(1)}, bf16[4,256,256]{2,1,0:T(8,128)(2,1)S(1)}, u32[]{:S(2)}, u32[]{:S(2)}) %collective-permute-start.43) | collective-permute-done | bytes 524320 | tf_op jit(solution)/shard_map/ppermute | solution.py:17
  496.9 11.2 %contract.5 = bf16[2,2,2,2,128,256]{5,4,3,2,1,0:T(8,128)(2,1)} custom-call(s32[12]{0:T(128)} %concatenate.168.index, bf16[4,256,256]{2,1,0:T(8,128)(2,1)} %copy-done.9, bf16[4,256,256]{2,1,0:T(8,128)(2,1)} %copy-done.18, bf16[4,256,256]{2,1,0:T(8,128)(2,1)} %copy-done.17, bf16[4,256,256]{2,1,0:T(8,128)(2,1)} %copy-done.19, bf16[4,256,256]{2,1,0:T(8,128)(2,1)} %copy-done.8, ...), custom_call_target="tpu_custom_call" | custom-call | flops 2147483648 | bytes 12582912 | tf_op jit(solution)/shard_map/contract/pallas_call | solution.py:29
  509.4 2.2 collective-permute-start.51
  513.6 3.5 collective-permute-done.51
  517.1 2.7 collective-permute-done.50
  521.1 4.3 all-to-all-start
  525.4 11.1 %contract.6 = bf16[2,2,2,2,128,256]{5,4,3,2,1,0:T(8,128)(2,1)} custom-call(s32[12]{0:T(128)} %concatenate.168.index, bf16[4,256,256]{2,1,0:T(8,128)(2,1)} %copy-done.9, bf16[4,256,256]{2,1,0:T(8,128)(2,1)} %copy-done.18, bf16[4,256,256]{2,1,0:T(8,128)(2,1)} %copy-done.17, bf16[4,256,256]{2,1,0:T(8,128)(2,1)} %copy-done.19, bf16[4,256,256]{2,1,0:T(8,128)(2,1)} %copy-done.8, ...), custom_call_target="tpu_custom_call" | custom-call | flops 2147483648 | bytes 12582912 | tf_op jit(solution)/shard_map/contract/pallas_call | solution.py:29
  541.3 19.0 %contract.7 = bf16[2,2,2,2,128,256]{5,4,3,2,1,0:T(8,128)(2,1)} custom-call(s32[15]{0:T(128)} %concatenate.184.index, bf16[3,256,256]{2,1,0:T(8,128)(2,1)} %get-tuple-element.183.refs_0_, bf16[3,256,256]{2,1,0:T(8,128)(2,1)} %collective-permute-done.21.refs_1_, bf16[3,256,256]{2,1,0:T(8,128)(2,1)} %collective-permute-done.24.refs_2_, ...), custom_call_target="tpu_custom_call" | custom-call | flops 5368709120 | bytes 18874368 | tf_op jit(solution)/shard_map/contract/pallas_call | solution.py:29
  561.8 5.1 all-to-all-start.1
  570.5 3.9 collective-permute-done.57
  574.4 2.7 collective-permute-done.56
  577.4 8.8 %all-to-all-done.1.refs_1_ = bf16[4,1,2,2,128,256]{5,4,3,2,1,0:T(8,128)(2,1)S(1)} async-done(((bf16[4,1,2,2,128,256]{5,4,3,2,1,0:T(8,128)(2,1)}), bf16[4,1,2,2,128,256]{5,4,3,2,1,0:T(8,128)(2,1)S(1)}, u32[]{:S(2)}, u32[]{:S(2)}) %all-to-all-start.1) | async-done | bytes 1048608 | tf_op jit(solution)/shard_map/all_to_all | solution.py:546
  586.2 25.4 %all_to_all.15.refs_2_ = bf16[4,1,2,2,128,256]{5,4,3,2,1,0:T(8,128)(2,1)} all-to-all(bf16[4,1,2,2,128,256]{5,4,3,2,1,0:T(8,128)(2,1)S(1)} %bitcast.191), channel_id=1, replica_groups=mesh['z'=4,'v'=2,'c'=2,'x'=2] {'z'}, dimensions={0} | all-to-all | bytes 2097152 | tf_op jit(solution)/shard_map/all_to_all | solution.py:546
  611.6 5.7 finish.1
  (247 shorter events, 96.8 us)
Async XLA Ops:
  6.5 71.1 %all-gather.18.cloned.1.call-start = ((), (), s32[]{:S(2)}) async-start(), calls=%async_computation.8 | async-start | bytes 1638400 | tf_op jit(solution)/shard_map/all_gather | solution.py:359
  12.1 24.8 %collective-permute-start.2 = (bf16[320,1536]{1,0:T(8,128)(2,1)S(1)}, bf16[320,1536]{1,0:T(8,128)(2,1)S(1)}, u32[]{:S(2)}, u32[]{:S(2)}) collective-permute-start(bf16[320,1536]{1,0:T(8,128)(2,1)S(1)} %bitcast.182), channel_id=1, source_target_pairs={{0,4},{4,0},{1,5},{5,1},{2,6},{6,2},{3,7},{7,3},{8,12},{12,8},{9,1... | collective-permute-start | bytes 2949128 | tf_op jit(solution)/shard_map/ppermute | solution.py:17
  17.3 163.4 %all-gather.8.cloned.1.call-start = ((), (), s32[]{:S(2)}) async-start(), calls=%async_computation.3 | async-start | bytes 2457600 | tf_op jit(solution)/shard_map/all_gather | solution.py:359
  17.4 24.1 %collective-permute-start.1 = (bf16[320,1536]{1,0:T(8,128)(2,1)S(1)}, bf16[320,1536]{1,0:T(8,128)(2,1)}, u32[]{:S(2)}, u32[]{:S(2)}) collective-permute-start(bf16[320,1536]{1,0:T(8,128)(2,1)S(1)} %bitcast.183), channel_id=1, source_target_pairs={{0,2},{2,0},{1,3},{3,1},{4,6},{6,4},{5,7},{7,5},{8,10},{10,8},{9,1... | collective-permute-start | bytes 2949128 | tf_op jit(solution)/shard_map/ppermute | solution.py:17
  36.9 4.5 collective-permute-start.3
  39.0 24.0 %collective-permute-start.6 = (bf16[320,1536]{1,0:T(8,128)(2,1)S(1)}, bf16[320,1536]{1,0:T(8,128)(2,1)}, u32[]{:S(2)}, u32[]{:S(2)}) collective-permute-start(bf16[320,1536]{1,0:T(8,128)(2,1)S(1)} %bitcast.186), channel_id=1, source_target_pairs={{0,4},{4,0},{1,5},{5,1},{2,6},{6,2},{3,7},{7,3},{8,12},{12,8},{9,1... | collective-permute-start | bytes 2949128 | tf_op jit(solution)/shard_map/ppermute | solution.py:17
  50.3 130.3 %all-gather.10.cloned.1.call-start = ((), (), s32[]{:S(2)}) async-start(), calls=%async_computation.4 | async-start | bytes 2457600 | tf_op jit(solution)/shard_map/all_gather | solution.py:359
  65.8 44.2 %collective-permute-start.8 = (bf16[640,1536]{1,0:T(8,128)(2,1)S(1)}, bf16[640,1536]{1,0:T(8,128)(2,1)}, u32[]{:S(2)}, u32[]{:S(2)}) collective-permute-start(bf16[640,1536]{1,0:T(8,128)(2,1)S(1)} %slice_bitcast_fusion.refs_0_), channel_id=1, source_target_pairs={{0,4},{4,0},{1,5},{5,1},{2,6},{6,2},{3,7},{7,3},{8,12},{12,8},{9,1... | collective-permute-start | bytes 5898248 | tf_op jit(solution)/shard_map/ppermute | solution.py:17
  68.3 10.9 %collective-permute-start.5 = (bf16[320,1536]{1,0:T(8,128)(2,1)S(1)}, bf16[320,1536]{1,0:T(8,128)(2,1)}, u32[]{:S(2)}, u32[]{:S(2)}) collective-permute-start(bf16[320,1536]{1,0:T(8,128)(2,1)S(1)} %bitcast.189), channel_id=1, source_target_pairs={{0,2},{2,0},{1,3},{3,1},{4,6},{6,4},{5,7},{7,5},{8,10},{10,8},{9,1... | collective-permute-start | bytes 2949128 | tf_op jit(solution)/shard_map/ppermute | solution.py:17
  77.6 31.1 %collective-permute-start.4 = (bf16[1,256,2560]{2,1,0:T(8,128)(2,1)}, bf16[1,256,2560]{2,1,0:T(8,128)(2,1)}, u32[]{:S(2)}, u32[]{:S(2)}) collective-permute-start(bf16[1,256,2560]{2,1,0:T(8,128)(2,1)} %bitcast.195), channel_id=1, source_target_pairs={{0,1},{1,0},{2,3},{3,2},{4,5},{5,4},{6,7},{7,6},{8,9},{9,8},{10,11... | collective-permute-start | bytes 3932168 | tf_op jit(solution)/shard_map/ppermute | solution.py:17
  79.1 62.4 %collective-permute-start.10 = (bf16[640,1536]{1,0:T(8,128)(2,1)S(1)}, bf16[640,1536]{1,0:T(8,128)(2,1)}, u32[]{:S(2)}, u32[]{:S(2)}) collective-permute-start(bf16[640,1536]{1,0:T(8,128)(2,1)S(1)} %slice_bitcast_fusion.refs_0_), channel_id=1, source_target_pairs={{0,2},{2,0},{1,3},{3,1},{4,6},{6,4},{5,7},{7,5},{8,10},{10,8},{9,1... | collective-permute-start | bytes 5898248 | tf_op jit(solution)/shard_map/ppermute | solution.py:17
  89.0 135.9 %all-gather.12.cloned.1.call-start = ((), (), s32[]{:S(2)}) async-start(), calls=%async_computation.5 | async-start | bytes 4915200 | tf_op jit(solution)/shard_map/all_gather | solution.py:359
  110.1 31.5 %collective-permute-start.11 = (bf16[640,1536]{1,0:T(8,128)(2,1)}, bf16[640,1536]{1,0:T(8,128)(2,1)}, u32[]{:S(2)}, u32[]{:S(2)}) collective-permute-start(bf16[640,1536]{1,0:T(8,128)(2,1)} %collective-permute-done.8.refs_2_), channel_id=1, source_target_pairs={{0,2},{2,0},{1,3},{3,1},{4,6},{6,4},{5,7},{7,5},{8,10},{10,8},{9,1... | collective-permute-start | bytes 5898248 | tf_op jit(solution)/shard_map/ppermute | solution.py:17
  113.3 59.6 %collective-permute-start.9 = (bf16[2,256,2560]{2,1,0:T(8,128)(2,1)}, bf16[2,256,2560]{2,1,0:T(8,128)(2,1)}, u32[]{:S(2)}, u32[]{:S(2)}) collective-permute-start(bf16[2,256,2560]{2,1,0:T(8,128)(2,1)} %pad_maximum_fusion.3), channel_id=1, source_target_pairs={{0,4},{4,0},{1,5},{5,1},{2,6},{6,2},{3,7},{7,3},{8,12},{12,8},{9,1... | collective-permute-start | bytes 7864328 | tf_op jit(solution)/shard_map/ppermute | solution.py:17
  116.1 24.1 %collective-permute-start.13 = (bf16[640,768]{1,0:T(8,128)(2,1)}, bf16[640,768]{1,0:T(8,128)(2,1)S(1)}, u32[]{:S(2)}, u32[]{:S(2)}) collective-permute-start(bf16[640,768]{1,0:T(8,128)(2,1)} %pad_maximum_fusion.7), channel_id=1, source_target_pairs={{0,1},{1,0},{2,3},{3,2},{4,5},{5,4},{6,7},{7,6},{8,9},{9,8},{10,11... | collective-permute-start | bytes 2949128 | tf_op jit(solution)/shard_map/ppermute | solution.py:17
  141.3 163.7 %all-gather.14.cloned.1.call-start = ((), (), s32[]{:S(2)}) async-start(), calls=%async_computation.6 | async-start | bytes 4915200 | tf_op jit(solution)/shard_map/all_gather | solution.py:359
  178.9 27.3 %collective-permute-start.12 = (bf16[4,256,2560]{2,1,0:T(8,128)(2,1)}, bf16[4,256,2560]{2,1,0:T(8,128)(2,1)}, u32[]{:S(2)}, u32[]{:S(2)}) collective-permute-start(bf16[4,256,2560]{2,1,0:T(8,128)(2,1)} %pad_maximum_fusion.1), channel_id=1, source_target_pairs={{0,2},{2,0},{1,3},{3,1},{4,6},{6,4},{5,7},{7,5},{8,10},{10,8},{9,1... | collective-permute-start | bytes 15728648 | tf_op jit(solution)/shard_map/ppermute | solution.py:17
  179.0 24.5 %collective-permute-start.14 = (bf16[640,768]{1,0:T(8,128)(2,1)}, bf16[640,768]{1,0:T(8,128)(2,1)}, u32[]{:S(2)}, u32[]{:S(2)}) collective-permute-start(bf16[640,768]{1,0:T(8,128)(2,1)} %fit.11), channel_id=1, source_target_pairs={{0,1},{1,0},{2,3},{3,2},{4,5},{5,4},{6,7},{7,6},{8,9},{9,8},{10,11... | collective-permute-start | bytes 2949128 | tf_op jit(solution)/shard_map/ppermute | solution.py:17
  206.2 177.6 %all-gather.16.cloned.1.call-start = ((), (), s32[]{:S(2)}) async-start(), calls=%async_computation.7 | async-start | bytes 4915200 | tf_op jit(solution)/shard_map/all_gather | solution.py:359
  224.9 21.6 %collective-permute-start.15 = (bf16[2048,768]{1,0:T(8,128)(2,1)}, bf16[2048,768]{1,0:T(8,128)(2,1)S(1)}, u32[]{:S(2)}, u32[]{:S(2)}) collective-permute-start(bf16[2048,768]{1,0:T(8,128)(2,1)} %convolution_convert_fusion.3), channel_id=1, source_target_pairs={{0,2},{2,0},{1,3},{3,1},{4,6},{6,4},{5,7},{7,5},{8,10},{10,8},{9,1... | collective-permute-start | bytes 9437192 | tf_op jit(solution)/shard_map/ppermute | solution.py:17
  240.3 6.2 collective-permute-start.16
  260.6 20.0 %collective-permute-start.17 = (bf16[2,3,256,256]{3,2,1,0:T(8,128)(2,1)}, bf16[2,3,256,256]{3,2,1,0:T(8,128)(2,1)}, u32[]{:S(2)}, u32[]{:S(2)}) collective-permute-start(bf16[2,3,256,256]{3,2,1,0:T(8,128)(2,1)} %get-tuple-element.72), channel_id=1, source_target_pairs={{0,1},{1,0},{2,3},{3,2},{4,5},{5,4},{6,7},{7,6},{8,9},{9,8},{10,11... | collective-permute-start | bytes 2359304 | tf_op jit(solution)/shard_map/ppermute | solution.py:17
  262.5 23.2 %collective-permute-start.19 = (bf16[2,3,256,256]{3,2,1,0:T(8,128)(2,1)}, bf16[2,3,256,256]{3,2,1,0:T(8,128)(2,1)}, u32[]{:S(2)}, u32[]{:S(2)}) collective-permute-start(bf16[2,3,256,256]{3,2,1,0:T(8,128)(2,1)} %get-tuple-element.73), channel_id=1, source_target_pairs={{0,4},{4,0},{1,5},{5,1},{2,6},{6,2},{3,7},{7,3},{8,12},{12,8},{9,1... | collective-permute-start | bytes 2359304 | tf_op jit(solution)/shard_map/ppermute | solution.py:17
  283.9 11.2 %collective-permute-start.18 = (bf16[3,256,256]{2,1,0:T(8,128)(2,1)}, bf16[3,256,256]{2,1,0:T(8,128)(2,1)}, u32[]{:S(2)}, u32[]{:S(2)}) collective-permute-start(bf16[3,256,256]{2,1,0:T(8,128)(2,1)} %fusion.38), channel_id=1, source_target_pairs={{0,4},{4,0},{1,5},{5,1},{2,6},{6,2},{3,7},{7,3},{8,12},{12,8},{9,1... | collective-permute-start | bytes 1179656 | tf_op jit(solution)/shard_map/ppermute | solution.py:17
  288.9 10.9 %collective-permute-start.20 = (bf16[3,256,256]{2,1,0:T(8,128)(2,1)}, bf16[3,256,256]{2,1,0:T(8,128)(2,1)}, u32[]{:S(2)}, u32[]{:S(2)}) collective-permute-start(bf16[3,256,256]{2,1,0:T(8,128)(2,1)} %fusion.39), channel_id=1, source_target_pairs={{0,1},{1,0},{2,3},{3,2},{4,5},{5,4},{6,7},{7,6},{8,9},{9,8},{10,11... | collective-permute-start | bytes 1179656 | tf_op jit(solution)/shard_map/ppermute | solution.py:17
  303.1 26.0 %collective-permute-start.22 = (bf16[3,256,256]{2,1,0:T(8,128)(2,1)}, bf16[3,256,256]{2,1,0:T(8,128)(2,1)}, u32[]{:S(2)}, u32[]{:S(2)}) collective-permute-start(bf16[3,256,256]{2,1,0:T(8,128)(2,1)} %get-tuple-element.182.refs_4_), channel_id=1, source_target_pairs={{0,1},{1,0},{2,3},{3,2},{4,5},{5,4},{6,7},{7,6},{8,9},{9,8},{10,11... | collective-permute-start | bytes 1179656 | tf_op jit(solution)/shard_map/ppermute | solution.py:17
  304.8 24.3 %collective-permute-start.21 = (bf16[3,256,256]{2,1,0:T(8,128)(2,1)}, bf16[3,256,256]{2,1,0:T(8,128)(2,1)}, u32[]{:S(2)}, u32[]{:S(2)}) collective-permute-start(bf16[3,256,256]{2,1,0:T(8,128)(2,1)} %get-tuple-element.183.refs_0_), channel_id=1, source_target_pairs={{0,4},{4,0},{1,5},{5,1},{2,6},{6,2},{3,7},{7,3},{8,12},{12,8},{9,1... | collective-permute-start | bytes 1179656 | tf_op jit(solution)/shard_map/ppermute | solution.py:17
  329.1 6.0 collective-permute-start.23
  329.2 15.9 %collective-permute-start.26 = (bf16[3,256,256]{2,1,0:T(8,128)(2,1)}, bf16[3,256,256]{2,1,0:T(8,128)(2,1)}, u32[]{:S(2)}, u32[]{:S(2)}) collective-permute-start(bf16[3,256,256]{2,1,0:T(8,128)(2,1)} %get-tuple-element.182.refs_4_), channel_id=1, source_target_pairs={{0,4},{4,0},{1,5},{5,1},{2,6},{6,2},{3,7},{7,3},{8,12},{12,8},{9,1... | collective-permute-start | bytes 1179656 | tf_op jit(solution)/shard_map/ppermute | solution.py:17
  331.1 13.9 %collective-permute-start.24 = (bf16[3,256,256]{2,1,0:T(8,128)(2,1)}, bf16[3,256,256]{2,1,0:T(8,128)(2,1)}, u32[]{:S(2)}, u32[]{:S(2)}) collective-permute-start(bf16[3,256,256]{2,1,0:T(8,128)(2,1)} %get-tuple-element.183.refs_0_), channel_id=1, source_target_pairs={{0,1},{1,0},{2,3},{3,2},{4,5},{5,4},{6,7},{7,6},{8,9},{9,8},{10,11... | collective-permute-start | bytes 1179656 | tf_op jit(solution)/shard_map/ppermute | solution.py:17
  331.4 18.2 %collective-permute-start.27 = (bf16[3,256,256]{2,1,0:T(8,128)(2,1)}, bf16[3,256,256]{2,1,0:T(8,128)(2,1)}, u32[]{:S(2)}, u32[]{:S(2)}) collective-permute-start(bf16[3,256,256]{2,1,0:T(8,128)(2,1)} %collective-permute-done.22.refs_5_), channel_id=1, source_target_pairs={{0,4},{4,0},{1,5},{5,1},{2,6},{6,2},{3,7},{7,3},{8,12},{12,8},{9,1... | collective-permute-start | bytes 1179656 | tf_op jit(solution)/shard_map/ppermute | solution.py:17
  331.5 19.5 %collective-permute-start.25 = (bf16[3,256,256]{2,1,0:T(8,128)(2,1)}, bf16[3,256,256]{2,1,0:T(8,128)(2,1)}, u32[]{:S(2)}, u32[]{:S(2)}) collective-permute-start(bf16[3,256,256]{2,1,0:T(8,128)(2,1)} %collective-permute-done.21.refs_1_), channel_id=1, source_target_pairs={{0,1},{1,0},{2,3},{3,2},{4,5},{5,4},{6,7},{7,6},{8,9},{9,8},{10,11... | collective-permute-start | bytes 1179656 | tf_op jit(solution)/shard_map/ppermute | solution.py:17
  351.0 19.0 %collective-permute-start.28 = (bf16[2,3,256,256]{3,2,1,0:T(8,128)(2,1)}, bf16[2,3,256,256]{3,2,1,0:T(8,128)(2,1)S(1)}, u32[]{:S(2)}, u32[]{:S(2)}) collective-permute-start(bf16[2,3,256,256]{3,2,1,0:T(8,128)(2,1)} %get-tuple-element.86), channel_id=1, source_target_pairs={{0,1},{1,0},{2,3},{3,2},{4,5},{5,4},{6,7},{7,6},{8,9},{9,8},{10,11... | collective-permute-start | bytes 2359304 | tf_op jit(solution)/shard_map/ppermute | solution.py:17
  351.3 19.7 %collective-permute-start.30 = (bf16[2,3,256,256]{3,2,1,0:T(8,128)(2,1)}, bf16[2,3,256,256]{3,2,1,0:T(8,128)(2,1)S(1)}, u32[]{:S(2)}, u32[]{:S(2)}) collective-permute-start(bf16[2,3,256,256]{3,2,1,0:T(8,128)(2,1)} %get-tuple-element.88), channel_id=1, source_target_pairs={{0,4},{4,0},{1,5},{5,1},{2,6},{6,2},{3,7},{7,3},{8,12},{12,8},{9,1... | collective-permute-start | bytes 2359304 | tf_op jit(solution)/shard_map/ppermute | solution.py:17
  370.3 9.6 %collective-permute-start.29 = (bf16[3,256,256]{2,1,0:T(8,128)(2,1)S(1)}, bf16[3,256,256]{2,1,0:T(8,128)(2,1)S(1)}, u32[]{:S(2)}, u32[]{:S(2)}) collective-permute-start(bf16[3,256,256]{2,1,0:T(8,128)(2,1)S(1)} %fusion.40), channel_id=1, source_target_pairs={{0,4},{4,0},{1,5},{5,1},{2,6},{6,2},{3,7},{7,3},{8,12},{12,8},{9,1... | collective-permute-start | bytes 1179656 | tf_op jit(solution)/shard_map/ppermute | solution.py:17
  371.3 9.7 %collective-permute-start.31 = (bf16[3,256,256]{2,1,0:T(8,128)(2,1)S(1)}, bf16[3,256,256]{2,1,0:T(8,128)(2,1)S(1)}, u32[]{:S(2)}, u32[]{:S(2)}) collective-permute-start(bf16[3,256,256]{2,1,0:T(8,128)(2,1)S(1)} %fusion.41), channel_id=1, source_target_pairs={{0,1},{1,0},{2,3},{3,2},{4,5},{5,4},{6,7},{7,6},{8,9},{9,8},{10,11... | collective-permute-start | bytes 1179656 | tf_op jit(solution)/shard_map/ppermute | solution.py:17
  382.4 13.5 %collective-permute-start.33 = (bf16[3,256,256]{2,1,0:T(8,128)(2,1)}, bf16[3,256,256]{2,1,0:T(8,128)(2,1)}, u32[]{:S(2)}, u32[]{:S(2)}) collective-permute-start(bf16[3,256,256]{2,1,0:T(8,128)(2,1)} %get-tuple-element.180.refs_12_), channel_id=1, source_target_pairs={{0,1},{1,0},{2,3},{3,2},{4,5},{5,4},{6,7},{7,6},{8,9},{9,8},{10,11... | collective-permute-start | bytes 1179656 | tf_op jit(solution)/shard_map/ppermute | solution.py:17
  382.9 13.1 %collective-permute-start.32 = (bf16[3,256,256]{2,1,0:T(8,128)(2,1)}, bf16[3,256,256]{2,1,0:T(8,128)(2,1)}, u32[]{:S(2)}, u32[]{:S(2)}) collective-permute-start(bf16[3,256,256]{2,1,0:T(8,128)(2,1)} %get-tuple-element.181.refs_8_), channel_id=1, source_target_pairs={{0,4},{4,0},{1,5},{5,1},{2,6},{6,2},{3,7},{7,3},{8,12},{12,8},{9,1... | collective-permute-start | bytes 1179656 | tf_op jit(solution)/shard_map/ppermute | solution.py:17
  396.0 6.7 %collective-permute-start.34 = (bf16[2048,768]{1,0:T(8,128)(2,1)S(1)}, bf16[2048,768]{1,0:T(8,128)(2,1)}, u32[]{:S(2)}, u32[]{:S(2)}) collective-permute-start(bf16[2048,768]{1,0:T(8,128)(2,1)S(1)} %convolution_convert_fusion.refs_3_.refs_11_.refs_27_), channel_id=1, source_target_pairs={{0,2},{2,0},{1,3},{3,1},{4,6},{6,4},{5,7},{7,5},{8,10},{10,8},{9,1... | collective-permute-start | bytes 9437192 | tf_op jit(solution)/shard_map/ppermute | solution.py:17
  396.1 18.9 %collective-permute-start.37 = (bf16[3,256,256]{2,1,0:T(8,128)(2,1)}, bf16[3,256,256]{2,1,0:T(8,128)(2,1)}, u32[]{:S(2)}, u32[]{:S(2)}) collective-permute-start(bf16[3,256,256]{2,1,0:T(8,128)(2,1)} %get-tuple-element.180.refs_12_), channel_id=1, source_target_pairs={{0,4},{4,0},{1,5},{5,1},{2,6},{6,2},{3,7},{7,3},{8,12},{12,8},{9,1... | collective-permute-start | bytes 1179656 | tf_op jit(solution)/shard_map/ppermute | solution.py:17
  397.2 17.8 %collective-permute-start.35 = (bf16[3,256,256]{2,1,0:T(8,128)(2,1)}, bf16[3,256,256]{2,1,0:T(8,128)(2,1)}, u32[]{:S(2)}, u32[]{:S(2)}) collective-permute-start(bf16[3,256,256]{2,1,0:T(8,128)(2,1)} %get-tuple-element.181.refs_8_), channel_id=1, source_target_pairs={{0,1},{1,0},{2,3},{3,2},{4,5},{5,4},{6,7},{7,6},{8,9},{9,8},{10,11... | collective-permute-start | bytes 1179656 | tf_op jit(solution)/shard_map/ppermute | solution.py:17
  398.8 17.5 %collective-permute-start.38 = (bf16[3,256,256]{2,1,0:T(8,128)(2,1)}, bf16[3,256,256]{2,1,0:T(8,128)(2,1)}, u32[]{:S(2)}, u32[]{:S(2)}) collective-permute-start(bf16[3,256,256]{2,1,0:T(8,128)(2,1)} %collective-permute-done.33.refs_13_), channel_id=1, source_target_pairs={{0,4},{4,0},{1,5},{5,1},{2,6},{6,2},{3,7},{7,3},{8,12},{12,8},{9,1... | collective-permute-start | bytes 1179656 | tf_op jit(solution)/shard_map/ppermute | solution.py:17
  399.9 17.3 %collective-permute-start.36 = (bf16[3,256,256]{2,1,0:T(8,128)(2,1)}, bf16[3,256,256]{2,1,0:T(8,128)(2,1)}, u32[]{:S(2)}, u32[]{:S(2)}) collective-permute-start(bf16[3,256,256]{2,1,0:T(8,128)(2,1)} %collective-permute-done.32.refs_9_), channel_id=1, source_target_pairs={{0,1},{1,0},{2,3},{3,2},{4,5},{5,4},{6,7},{7,6},{8,9},{9,8},{10,11... | collective-permute-start | bytes 1179656 | tf_op jit(solution)/shard_map/ppermute | solution.py:17
  417.2 24.6 %collective-permute-start.39 = (bf16[2,4,256,256]{3,2,1,0:T(8,128)(2,1)}, bf16[2,4,256,256]{3,2,1,0:T(8,128)(2,1)S(1)}, u32[]{:S(2)}, u32[]{:S(2)}) collective-permute-start(bf16[2,4,256,256]{3,2,1,0:T(8,128)(2,1)} %get-tuple-element.98), channel_id=1, source_target_pairs={{0,1},{1,0},{2,3},{3,2},{4,5},{5,4},{6,7},{7,6},{8,9},{9,8},{10,11... | collective-permute-start | bytes 3145736 | tf_op jit(solution)/shard_map/ppermute | solution.py:17
  418.8 24.4 %collective-permute-start.44 = (bf16[2,4,256,256]{3,2,1,0:T(8,128)(2,1)}, bf16[2,4,256,256]{3,2,1,0:T(8,128)(2,1)}, u32[]{:S(2)}, u32[]{:S(2)}) collective-permute-start(bf16[2,4,256,256]{3,2,1,0:T(8,128)(2,1)} %get-tuple-element.101), channel_id=1, source_target_pairs={{0,4},{4,0},{1,5},{5,1},{2,6},{6,2},{3,7},{7,3},{8,12},{12,8},{9,1... | collective-permute-start | bytes 3145736 | tf_op jit(solution)/shard_map/ppermute | solution.py:17
  442.2 12.5 %collective-permute-start.40 = (bf16[4,256,256]{2,1,0:T(8,128)(2,1)S(1)}, bf16[4,256,256]{2,1,0:T(8,128)(2,1)}, u32[]{:S(2)}, u32[]{:S(2)}) collective-permute-start(bf16[4,256,256]{2,1,0:T(8,128)(2,1)S(1)} %fusion.36), channel_id=1, source_target_pairs={{0,4},{4,0},{1,5},{5,1},{2,6},{6,2},{3,7},{7,3},{8,12},{12,8},{9,1... | collective-permute-start | bytes 1572872 | tf_op jit(solution)/shard_map/ppermute | solution.py:17
  445.6 12.4 %collective-permute-start.45 = (bf16[4,256,256]{2,1,0:T(8,128)(2,1)}, bf16[4,256,256]{2,1,0:T(8,128)(2,1)}, u32[]{:S(2)}, u32[]{:S(2)}) collective-permute-start(bf16[4,256,256]{2,1,0:T(8,128)(2,1)} %fusion.37), channel_id=1, source_target_pairs={{0,1},{1,0},{2,3},{3,2},{4,5},{5,4},{6,7},{7,6},{8,9},{9,8},{10,11... | collective-permute-start | bytes 1572872 | tf_op jit(solution)/shard_map/ppermute | solution.py:17
  460.8 23.4 %collective-permute-start.47 = (bf16[4,256,256]{2,1,0:T(8,128)(2,1)S(1)}, bf16[4,256,256]{2,1,0:T(8,128)(2,1)S(1)}, u32[]{:S(2)}, u32[]{:S(2)}) collective-permute-start(bf16[4,256,256]{2,1,0:T(8,128)(2,1)S(1)} %get-tuple-element.174.refs_4_.refs_20_), channel_id=1, source_target_pairs={{0,4},{4,0},{1,5},{5,1},{2,6},{6,2},{3,7},{7,3},{8,12},{12,8},{9,1... | collective-permute-start | bytes 1572872 | tf_op jit(solution)/shard_map/ppermute | solution.py:17
  462.0 22.3 %collective-permute-start.46 = (bf16[4,256,256]{2,1,0:T(8,128)(2,1)S(1)}, bf16[4,256,256]{2,1,0:T(8,128)(2,1)S(1)}, u32[]{:S(2)}, u32[]{:S(2)}) collective-permute-start(bf16[4,256,256]{2,1,0:T(8,128)(2,1)S(1)} %get-tuple-element.174.refs_4_.refs_20_), channel_id=1, source_target_pairs={{0,1},{1,0},{2,3},{3,2},{4,5},{5,4},{6,7},{7,6},{8,9},{9,8},{10,11... | collective-permute-start | bytes 1572872 | tf_op jit(solution)/shard_map/ppermute | solution.py:17
  463.6 21.4 %collective-permute-start.42 = (bf16[4,256,256]{2,1,0:T(8,128)(2,1)S(1)}, bf16[4,256,256]{2,1,0:T(8,128)(2,1)S(1)}, u32[]{:S(2)}, u32[]{:S(2)}) collective-permute-start(bf16[4,256,256]{2,1,0:T(8,128)(2,1)S(1)} %get-tuple-element.175.refs_0_.refs_16_), channel_id=1, source_target_pairs={{0,1},{1,0},{2,3},{3,2},{4,5},{5,4},{6,7},{7,6},{8,9},{9,8},{10,11... | collective-permute-start | bytes 1572872 | tf_op jit(solution)/shard_map/ppermute | solution.py:17
  464.0 20.9 %collective-permute-start.41 = (bf16[4,256,256]{2,1,0:T(8,128)(2,1)S(1)}, bf16[4,256,256]{2,1,0:T(8,128)(2,1)S(1)}, u32[]{:S(2)}, u32[]{:S(2)}) collective-permute-start(bf16[4,256,256]{2,1,0:T(8,128)(2,1)S(1)} %get-tuple-element.175.refs_0_.refs_16_), channel_id=1, source_target_pairs={{0,4},{4,0},{1,5},{5,1},{2,6},{6,2},{3,7},{7,3},{8,12},{12,8},{9,1... | collective-permute-start | bytes 1572872 | tf_op jit(solution)/shard_map/ppermute | solution.py:17
  484.9 10.4 %collective-permute-start.43 = (bf16[4,256,256]{2,1,0:T(8,128)(2,1)S(1)}, bf16[4,256,256]{2,1,0:T(8,128)(2,1)S(1)}, u32[]{:S(2)}, u32[]{:S(2)}) collective-permute-start(bf16[4,256,256]{2,1,0:T(8,128)(2,1)S(1)} %collective-permute-done.41.refs_1_.refs_17_), channel_id=1, source_target_pairs={{0,1},{1,0},{2,3},{3,2},{4,5},{5,4},{6,7},{7,6},{8,9},{9,8},{10,11... | collective-permute-start | bytes 1572872 | tf_op jit(solution)/shard_map/ppermute | solution.py:17
  486.5 9.3 %collective-permute-start.48 = (bf16[4,256,256]{2,1,0:T(8,128)(2,1)S(1)}, bf16[4,256,256]{2,1,0:T(8,128)(2,1)S(1)}, u32[]{:S(2)}, u32[]{:S(2)}) collective-permute-start(bf16[4,256,256]{2,1,0:T(8,128)(2,1)S(1)} %collective-permute-done.46.refs_5_.refs_21_), channel_id=1, source_target_pairs={{0,4},{4,0},{1,5},{5,1},{2,6},{6,2},{3,7},{7,3},{8,12},{12,8},{9,1... | collective-permute-start | bytes 1572872 | tf_op jit(solution)/shard_map/ppermute | solution.py:17
  509.4 7.7 %collective-permute-start.51 = (bf16[1,2,2,128,256]{4,3,2,1,0:T(8,128)(2,1)S(1)}, bf16[1,2,2,128,256]{4,3,2,1,0:T(8,128)(2,1)S(1)}, u32[]{:S(2)}, u32[]{:S(2)}) collective-permute-start(bf16[1,2,2,128,256]{4,3,2,1,0:T(8,128)(2,1)S(1)} %get-tuple-element.154), channel_id=1, source_target_pairs={{0,5},{1,4},{4,1},{5,0},{2,7},{3,6},{6,3},{7,2},{8,13},{9,12},{12,... | collective-permute-start | bytes 786440 | tf_op jit(solution)/shard_map/ppermute | solution.py:528
  511.5 8.2 %collective-permute-start.50 = (bf16[1,2,2,128,256]{4,3,2,1,0:T(8,128)(2,1)S(1)}, bf16[1,2,2,128,256]{4,3,2,1,0:T(8,128)(2,1)S(1)}, u32[]{:S(2)}, u32[]{:S(2)}) collective-permute-start(bf16[1,2,2,128,256]{4,3,2,1,0:T(8,128)(2,1)S(1)} %get-tuple-element.155), channel_id=1, source_target_pairs={{0,4},{4,0},{1,5},{5,1},{2,6},{6,2},{3,7},{7,3},{8,12},{12,8},{9,1... | collective-permute-start | bytes 786440 | tf_op jit(solution)/shard_map/ppermute | solution.py:17
  512.5 7.3 %collective-permute-start.49 = (bf16[1,2,2,128,256]{4,3,2,1,0:T(8,128)(2,1)S(1)}, bf16[1,2,2,128,256]{4,3,2,1,0:T(8,128)(2,1)S(1)}, u32[]{:S(2)}, u32[]{:S(2)}) collective-permute-start(bf16[1,2,2,128,256]{4,3,2,1,0:T(8,128)(2,1)S(1)} %get-tuple-element.156), channel_id=1, source_target_pairs={{0,1},{1,0},{2,3},{3,2},{4,5},{5,4},{6,7},{7,6},{8,9},{9,8},{10,11... | collective-permute-start | bytes 786440 | tf_op jit(solution)/shard_map/ppermute | solution.py:17
  521.1 40.6 %all-to-all-start = ((bf16[4,1,2,2,128,256]{5,4,3,2,1,0:T(8,128)(2,1)}), bf16[4,1,2,2,128,256]{5,4,3,2,1,0:T(8,128)(2,1)S(1)}, u32[]{:S(2)}, u32[]{:S(2)}) async-start(bf16[4,1,2,2,128,256]{5,4,3,2,1,0:T(8,128)(2,1)} %bitcast.54), calls=%async_computation | async-start | bytes 2097152 | tf_op jit(solution)/shard_map/all_to_all | solution.py:546
  537.8 22.6 %collective-permute-start.54 = (bf16[1,2,2,128,256]{4,3,2,1,0:T(8,128)(2,1)S(1)}, bf16[1,2,2,128,256]{4,3,2,1,0:T(8,128)(2,1)S(1)}, u32[]{:S(2)}, u32[]{:S(2)}) collective-permute-start(bf16[1,2,2,128,256]{4,3,2,1,0:T(8,128)(2,1)S(1)} %get-tuple-element.148), channel_id=1, source_target_pairs={{0,5},{1,4},{4,1},{5,0},{2,7},{3,6},{6,3},{7,2},{8,13},{9,12},{12,... | collective-permute-start | bytes 786440 | tf_op jit(solution)/shard_map/ppermute | solution.py:528
  539.5 20.9 %collective-permute-start.53 = (bf16[1,2,2,128,256]{4,3,2,1,0:T(8,128)(2,1)S(1)}, bf16[1,2,2,128,256]{4,3,2,1,0:T(8,128)(2,1)S(1)}, u32[]{:S(2)}, u32[]{:S(2)}) collective-permute-start(bf16[1,2,2,128,256]{4,3,2,1,0:T(8,128)(2,1)S(1)} %get-tuple-element.149), channel_id=1, source_target_pairs={{0,4},{4,0},{1,5},{5,1},{2,6},{6,2},{3,7},{7,3},{8,12},{12,8},{9,1... | collective-permute-start | bytes 786440 | tf_op jit(solution)/shard_map/ppermute | solution.py:17
  540.5 19.9 %collective-permute-start.52 = (bf16[1,2,2,128,256]{4,3,2,1,0:T(8,128)(2,1)S(1)}, bf16[1,2,2,128,256]{4,3,2,1,0:T(8,128)(2,1)S(1)}, u32[]{:S(2)}, u32[]{:S(2)}) collective-permute-start(bf16[1,2,2,128,256]{4,3,2,1,0:T(8,128)(2,1)S(1)} %get-tuple-element.150), channel_id=1, source_target_pairs={{0,1},{1,0},{2,3},{3,2},{4,5},{5,4},{6,7},{7,6},{8,9},{9,8},{10,11... | collective-permute-start | bytes 786440 | tf_op jit(solution)/shard_map/ppermute | solution.py:17
  561.8 24.4 %all-to-all-start.1 = ((bf16[4,1,2,2,128,256]{5,4,3,2,1,0:T(8,128)(2,1)}), bf16[4,1,2,2,128,256]{5,4,3,2,1,0:T(8,128)(2,1)S(1)}, u32[]{:S(2)}, u32[]{:S(2)}) async-start(bf16[4,1,2,2,128,256]{5,4,3,2,1,0:T(8,128)(2,1)} %bitcast.190), calls=%async_computation.1 | async-start | bytes 2097152 | tf_op jit(solution)/shard_map/all_to_all | solution.py:546
  567.0 7.4 %collective-permute-start.57 = (bf16[1,2,2,128,256]{4,3,2,1,0:T(8,128)(2,1)S(1)}, bf16[1,2,2,128,256]{4,3,2,1,0:T(8,128)(2,1)S(1)}, u32[]{:S(2)}, u32[]{:S(2)}) collective-permute-start(bf16[1,2,2,128,256]{4,3,2,1,0:T(8,128)(2,1)S(1)} %get-tuple-element.142), channel_id=1, source_target_pairs={{0,5},{1,4},{4,1},{5,0},{2,7},{3,6},{6,3},{7,2},{8,13},{9,12},{12,... | collective-permute-start | bytes 786440 | tf_op jit(solution)/shard_map/ppermute | solution.py:528
  568.7 8.4 %collective-permute-start.56 = (bf16[1,2,2,128,256]{4,3,2,1,0:T(8,128)(2,1)S(1)}, bf16[1,2,2,128,256]{4,3,2,1,0:T(8,128)(2,1)S(1)}, u32[]{:S(2)}, u32[]{:S(2)}) collective-permute-start(bf16[1,2,2,128,256]{4,3,2,1,0:T(8,128)(2,1)S(1)} %get-tuple-element.143), channel_id=1, source_target_pairs={{0,4},{4,0},{1,5},{5,1},{2,6},{6,2},{3,7},{7,3},{8,12},{12,8},{9,1... | collective-permute-start | bytes 786440 | tf_op jit(solution)/shard_map/ppermute | solution.py:17
  569.7 7.4 %collective-permute-start.55 = (bf16[1,2,2,128,256]{4,3,2,1,0:T(8,128)(2,1)S(1)}, bf16[1,2,2,128,256]{4,3,2,1,0:T(8,128)(2,1)S(1)}, u32[]{:S(2)}, u32[]{:S(2)}) collective-permute-start(bf16[1,2,2,128,256]{4,3,2,1,0:T(8,128)(2,1)S(1)} %get-tuple-element.144), channel_id=1, source_target_pairs={{0,1},{1,0},{2,3},{3,2},{4,5},{5,4},{6,7},{7,6},{8,9},{9,8},{10,11... | collective-permute-start | bytes 786440 | tf_op jit(solution)/shard_map/ppermute | solution.py:17
  (39 other events, 367.3 us)
Sparse Core Ops, SparseCore 0:
  17.4 32.5 all-gather.17
  51.6 42.9 all-gather.7
  96.2 42.3 all-gather.9
  141.4 76.7 all-gather.11
  219.6 74.9 all-gather.13
  296.0 74.9 all-gather.15
